TPU v7x, 32 devices: a whole 2x2x4 slice. The times are simulated.
32 devices in a mesh: dp: 8 (over y, x, core), grid: 4 (over z).
Axes of the slice: x: 2, y: 2, z: 4, core: 2. Of those that a mesh axis runs over, the one named last changes fastest.
Arguments:
- tokens: bfloat16 [32, 1024, 768], P(('dp', 'grid')), may hold values from -6 to 6
- boxes: int32 [32, 2, 1024], P(('dp', 'grid')), may hold values from 0 to 999
- segments: int32 [32, 448], P(('dp', 'grid')), may hold values from 0 to 63, never falling along the last dimension, each value on 1 to 14 neighbouring positions
- patches: int32 [32], P(('dp', 'grid')), may hold values from 256 to 576, as said below
- cot_out: bfloat16 [32, 1024, 768], P(('dp', 'grid')), may hold values from -6 to 6
- cot_pair: float32 [32, 64, 64], P(('dp', 'grid')), may hold values from -6 to 6
- weights: float32 [10752, 768], P(('dp', 'grid')), may hold values from -4 to 4
- weight_momentum: float32 [10752, 768], P(('dp', 'grid')), may hold values from -320 to 320
- weight_average: float32 [10752, 768], P(('dp', 'grid')), may hold values from -4 to 4
- vectors: float32 [12, 768], replicated, may hold values from -4 to 4
- vector_momentum: float32 [12, 768], replicated, may hold values from -512 to 512
- vector_average: float32 [12, 768], replicated, may hold values from -4 to 4
- box_coef: float32 [2, 12], replicated, may hold values from -0.1 to 0.1
- coef_momentum: float32 [2, 12], replicated, may hold values from -5120 to 5120
- coef_average: float32 [2, 12], replicated, may hold values from -0.1 to 0.1
Outputs:
- mixed: bfloat16 [32, 1024, 768], P(('dp', 'grid'))
- pair_scores: float32 [32, 64, 64], P(('dp', 'grid'))
- token_grad: bfloat16 [32, 1024, 768], P(('dp', 'grid'))
- weight_grad: float32 [10752, 768], P(('dp', 'grid'))
- new_weights: float32 [10752, 768], P(('dp', 'grid'))
- new_weight_momentum: float32 [10752, 768], P(('dp', 'grid'))
- new_weight_average: float32 [10752, 768], P(('dp', 'grid'))
- new_weights_low: bfloat16 [10752, 768], P(('dp', 'grid'))
- vector_grad: float32 [12, 768], replicated
- new_vectors: float32 [12, 768], replicated
- new_vector_momentum: float32 [12, 768], replicated
- new_vector_average: float32 [12, 768], replicated
- coef_grad: float32 [2, 12], replicated
- new_coef: float32 [2, 12], replicated
- new_coef_momentum: float32 [2, 12], replicated
- new_coef_average: float32 [2, 12], replicated
Inputs may be any that keep to these rules, and one draw needn't show every extreme that they name: Each page has 256 or 576 patches; both occur in every draw. `segments`: segment numbers never fall along a page; every segment holds 1 to 14 text tokens, some exactly 14.
All inputs are finite; a program needn't handle non-finite values.
Results may differ from a plain program's by a relative error of at most 0.022.
Values may be sent and summed in bfloat16 or wider, within the bound.
No kernel may reach another device: no remote copies, remote signals or barrier semaphores. Data moves between devices by JAX's collectives and lax.ppermute only.
A program may use at most 256 MiB of HBM per device.

v0:
```python
import jax
import jax.numpy as jnp
from jax import lax
from jax.sharding import PartitionSpec as P

D = 768
HEADS = 12
HDIM = 64
FF = 3072
TEXT = 448
SEGS = 64
BLOCK = 512
HGROUP = 4


highest = lax.Precision.HIGHEST


def fetch_weights(shard):
    gathered = lax.all_gather(shard, ("dp", "grid"), axis=0, tiled=True)
    return gathered


def reduce_grads(full_grad, small_flat):
    summed, small_part = (
        lax.psum_scatter(full_grad, ("dp", "grid"), scatter_dimension=0, tiled=True),
        lax.psum_scatter(small_flat, ("dp", "grid"), scatter_dimension=0, tiled=True),
    )
    return (summed, small_part)


def split_weights(gathered):
    return (
        gathered[: 3 * D],
        gathered[3 * D : 4 * D],
        gathered[4 * D : 4 * D + FF],
        gathered[4 * D + FF : 4 * D + 2 * FF],
        gathered[4 * D + 2 * FF : 5 * D + 2 * FF],
        gathered[5 * D + 2 * FF :],
    )


def normalize(values):
    row_mean = jnp.mean(values, axis=-1, keepdims=True)
    centered = values - row_mean
    variance = jnp.mean(centered * centered, axis=-1, keepdims=True)
    inv_std = lax.rsqrt(variance + 1e-05)
    return (centered * inv_std, inv_std)


def normalize_back(grad_normed, normed, inv_std):
    first_mean = jnp.mean(grad_normed, axis=-1, keepdims=True)
    second_mean = jnp.mean(grad_normed * normed, axis=-1, keepdims=True)
    return inv_std * (grad_normed - first_mean - normed * second_mean)


def buckets(row_boxes, col_boxes):
    spread = jnp.abs(row_boxes[:, :, None] - col_boxes[:, None, :])
    return jnp.minimum(spread // 32, 31).astype(jnp.float32)


def gelu_exact(values):
    return jax.nn.gelu(values, approximate=False)


def block_scores(packed_pages, boxes, patches, box_coef, item_index):
    slot_count = packed_pages.shape[1]
    blocks = slot_count // BLOCK
    groups = HEADS // HGROUP
    group_width = HGROUP * HDIM
    page_index = item_index // (blocks * groups)
    block_index = item_index // groups % blocks
    group_index = item_index % groups
    page_rows = lax.dynamic_index_in_dim(packed_pages, page_index, 0, keepdims=False)
    query_part = lax.dynamic_slice(
        page_rows, (block_index * BLOCK, group_index * group_width), (BLOCK, group_width)
    ).reshape(BLOCK, HGROUP, HDIM)
    key_part = lax.dynamic_slice(
        page_rows, (0, D + group_index * group_width), (slot_count, group_width)
    ).reshape(slot_count, HGROUP, HDIM)
    value_part = lax.dynamic_slice(
        page_rows, (0, 2 * D + group_index * group_width), (slot_count, group_width)
    ).reshape(slot_count, HGROUP, HDIM)
    page_boxes = lax.dynamic_index_in_dim(boxes, page_index, 0, keepdims=False)
    row_boxes = lax.dynamic_slice_in_dim(page_boxes, block_index * BLOCK, BLOCK, 1)
    bucket = buckets(row_boxes, page_boxes)
    coef_part = lax.dynamic_slice_in_dim(box_coef, group_index * HGROUP, HGROUP, 1)
    scores = jnp.einsum(
        "qgd,kgd->gqk", query_part, key_part, preferred_element_type=jnp.float32
    ) * HDIM ** (-0.5)
    scores = (
        scores + coef_part[0][:, None, None] * bucket[0] + coef_part[1][:, None, None] * bucket[1]
    )
    page_patches = lax.dynamic_index_in_dim(patches, page_index, 0, keepdims=False)
    key_live = jnp.arange(slot_count, dtype=jnp.int32) < TEXT + page_patches
    scores = jnp.where(key_live, scores, -1e30)
    return (scores, query_part, key_part, value_part, bucket, page_index, block_index, group_index)


def momentum_step(grad, param, moment, average, rate):
    new_moment = 0.5 * moment + grad
    new_param = param - rate * (grad + 0.5 * new_moment)
    new_average = 0.5 * average + 0.5 * new_param
    return (new_moment, new_param, new_average)


def on_device(
    tokens,
    boxes,
    segments,
    patches,
    cot_out,
    cot_pair,
    weights,
    weight_momentum,
    weight_average,
    vectors,
    vector_momentum,
    vector_average,
    box_coef,
    coef_momentum,
    coef_average,
):
    page_count = tokens.shape[0]
    slot_count = tokens.shape[1]
    row_count = page_count * slot_count
    blocks = slot_count // BLOCK
    groups = HEADS // HGROUP
    group_width = HGROUP * HDIM
    items = jnp.arange(page_count * blocks * groups, dtype=jnp.int32)
    shard_low = weights.astype(jnp.bfloat16)
    gathered = fetch_weights(shard_low)
    weight_qkv, weight_out, weight_up, weight_down, weight_left, weight_right = split_weights(
        gathered
    )
    gain_one = vectors[0]
    shift_one = vectors[1]
    bias_query = vectors[2]
    bias_value = vectors[3]
    bias_out = vectors[4]
    gain_two = vectors[5]
    shift_two = vectors[6]
    bias_down = vectors[7]
    bias_up = vectors[8:].reshape(FF)
    flat_tokens = tokens.reshape(row_count, D)
    bias_qkv = jnp.concatenate([bias_query, jnp.zeros((D,), jnp.float32), bias_value])
    packed = (
        jnp.einsum("rd,cd->rc", flat_tokens, weight_qkv, preferred_element_type=jnp.float32)
        + bias_qkv
    ).astype(jnp.bfloat16)
    packed_pages = packed.reshape(page_count, slot_count, 3 * D)

    def forward_item(item_index):
        found = block_scores(packed_pages, boxes, patches, box_coef, item_index)
        scores = found[0]
        top = jnp.max(scores, axis=-1, keepdims=True)
        exponent = jnp.exp(scores - top)
        total = jnp.sum(exponent, axis=-1, keepdims=True)
        softmax_out = (exponent / total).astype(jnp.bfloat16)
        blended = jnp.einsum(
            "gqk,kgd->qgd", softmax_out, found[3], preferred_element_type=jnp.float32
        )
        return (
            blended.astype(jnp.bfloat16).reshape(BLOCK, group_width),
            (top + jnp.log(total))[:, :, 0],
        )

    def assemble(per_item):
        return (
            per_item.reshape(page_count, blocks, groups, BLOCK, group_width)
            .transpose(0, 1, 3, 2, 4)
            .reshape(row_count, D)
        )

    attended_items, log_totals = lax.map(forward_item, items)
    attended = assemble(attended_items)
    branch = (
        jnp.einsum("rd,od->ro", attended, weight_out, preferred_element_type=jnp.float32) + bias_out
    )
    normed_one, inv_one = normalize(flat_tokens.astype(jnp.float32) + branch)
    hidden_one = normed_one * gain_one + shift_one
    hidden_low = hidden_one.astype(jnp.bfloat16)
    pre_act = (
        jnp.einsum("rd,fd->rf", hidden_low, weight_up, preferred_element_type=jnp.float32) + bias_up
    )
    activated = gelu_exact(pre_act).astype(jnp.bfloat16)
    feed = (
        jnp.einsum("rf,fd->rd", activated, weight_down, preferred_element_type=jnp.float32)
        + bias_down
    )
    normed_two, inv_two = normalize(hidden_one + feed)
    output = normed_two * gain_two + shift_two
    mixed = output.astype(jnp.bfloat16).reshape(page_count, slot_count, D)
    text_rows = output.reshape(page_count, slot_count, D)[:, :TEXT]
    member = (segments[:, None, :] == jnp.arange(SEGS, dtype=jnp.int32)[None, :, None]).astype(
        jnp.float32
    )
    counted = jnp.sum(member, axis=2, keepdims=True)
    pooled = (jnp.einsum("pst,ptd->psd", member, text_rows, precision=highest) / counted).astype(
        jnp.bfloat16
    )
    left_side = jnp.einsum(
        "psd,od->pso", pooled, weight_left, preferred_element_type=jnp.float32
    ).astype(jnp.bfloat16)
    right_side = jnp.einsum(
        "psd,od->pso", pooled, weight_right, preferred_element_type=jnp.float32
    ).astype(jnp.bfloat16)
    pair_scale = D ** (-0.5)
    pair_scores = (
        jnp.einsum("pso,pto->pst", left_side, right_side, preferred_element_type=jnp.float32)
        * pair_scale
    )
    back_weights = fetch_weights(shard_low)
    back_qkv, back_out, back_up, back_down, back_left, back_right = split_weights(back_weights)
    grad_left = (
        jnp.einsum("pst,pto->pso", cot_pair, right_side.astype(jnp.float32), precision=highest)
        * pair_scale
    ).astype(jnp.bfloat16)
    grad_right = (
        jnp.einsum("pst,pso->pto", cot_pair, left_side.astype(jnp.float32), precision=highest)
        * pair_scale
    ).astype(jnp.bfloat16)
    grad_pooled = jnp.einsum(
        "pso,od->psd", grad_left, back_left, preferred_element_type=jnp.float32
    ) + jnp.einsum("pso,od->psd", grad_right, back_right, preferred_element_type=jnp.float32)
    grad_text = jnp.einsum("pst,psd->ptd", member, grad_pooled / counted, precision=highest)
    grad_wleft = jnp.einsum("pso,psd->od", grad_left, pooled, preferred_element_type=jnp.float32)
    grad_wright = jnp.einsum("pso,psd->od", grad_right, pooled, preferred_element_type=jnp.float32)
    live = (jnp.arange(slot_count, dtype=jnp.int32)[None, :] < (TEXT + patches)[:, None]).astype(
        jnp.float32
    )
    grad_output = cot_out.astype(jnp.float32) * live[:, :, None]
    grad_output = jnp.concatenate(
        [grad_output[:, :TEXT] + grad_text, grad_output[:, TEXT:]], axis=1
    ).reshape(row_count, D)
    grad_gain_two = jnp.sum(grad_output * normed_two, axis=0)
    grad_shift_two = jnp.sum(grad_output, axis=0)
    grad_res_two = normalize_back(grad_output * gain_two, normed_two, inv_two)
    grad_feed = grad_res_two.astype(jnp.bfloat16)
    grad_bias_down = jnp.sum(grad_feed.astype(jnp.float32), axis=0)
    grad_wdown = jnp.einsum("rf,rd->fd", activated, grad_feed, preferred_element_type=jnp.float32)
    grad_act = jnp.einsum("rd,fd->rf", grad_feed, back_down, preferred_element_type=jnp.float32)
    grad_pre = jax.vjp(gelu_exact, pre_act)[1](grad_act)[0].astype(jnp.bfloat16)
    grad_bias_up = jnp.sum(grad_pre.astype(jnp.float32), axis=0)
    grad_wup = jnp.einsum("rf,rd->fd", grad_pre, hidden_low, preferred_element_type=jnp.float32)
    grad_hidden = grad_res_two + jnp.einsum(
        "rf,fd->rd", grad_pre, back_up, preferred_element_type=jnp.float32
    )
    grad_gain_one = jnp.sum(grad_hidden * normed_one, axis=0)
    grad_shift_one = jnp.sum(grad_hidden, axis=0)
    grad_res_one = normalize_back(grad_hidden * gain_one, normed_one, inv_one)
    grad_branch = grad_res_one.astype(jnp.bfloat16)
    grad_bias_out = jnp.sum(grad_branch.astype(jnp.float32), axis=0)
    grad_wout = jnp.einsum("ro,rd->od", grad_branch, attended, preferred_element_type=jnp.float32)
    grad_attended = jnp.einsum(
        "ro,od->rd", grad_branch, back_out, preferred_element_type=jnp.float32
    ).astype(jnp.bfloat16)
    grad_attn_pages = grad_attended.reshape(page_count, slot_count, D)

    def backward_item(item_index):
        found = block_scores(packed_pages, boxes, patches, box_coef, item_index)
        scores, query_part, key_part, value_part, bucket, page_index, block_index, group_index = (
            found
        )
        log_total = lax.dynamic_index_in_dim(log_totals, item_index, 0, keepdims=False)
        softmax_out = jnp.exp(scores - log_total[:, :, None])
        grad_page = lax.dynamic_index_in_dim(grad_attn_pages, page_index, 0, keepdims=False)
        grad_block = lax.dynamic_slice(
            grad_page, (block_index * BLOCK, group_index * group_width), (BLOCK, group_width)
        ).reshape(BLOCK, HGROUP, HDIM)
        grad_prob = jnp.einsum(
            "qgd,kgd->gqk", grad_block, value_part, preferred_element_type=jnp.float32
        )
        delta_sum = jnp.sum(softmax_out * grad_prob, axis=-1, keepdims=True)
        grad_scores = (softmax_out * (grad_prob - delta_sum)).astype(jnp.bfloat16)
        score_float = grad_scores.astype(jnp.float32)
        grad_coef = jnp.stack(
            [
                jnp.sum(score_float * bucket[0], axis=(1, 2)),
                jnp.sum(score_float * bucket[1], axis=(1, 2)),
            ]
        )
        grad_query = jnp.einsum(
            "gqk,kgd->qgd", grad_scores, key_part, preferred_element_type=jnp.float32
        ) * HDIM ** (-0.5)
        grad_key = jnp.einsum(
            "gqk,qgd->kgd", grad_scores, query_part, preferred_element_type=jnp.float32
        ) * HDIM ** (-0.5)
        grad_value = jnp.einsum(
            "gqk,qgd->kgd",
            softmax_out.astype(jnp.bfloat16),
            grad_block,
            preferred_element_type=jnp.float32,
        )
        return (
            grad_query.reshape(BLOCK, group_width),
            grad_key.reshape(slot_count, group_width),
            grad_value.reshape(slot_count, group_width),
            grad_coef,
        )

    def fold_keys(per_item):
        return (
            per_item.reshape(page_count, blocks, groups, slot_count, group_width)
            .sum(axis=1)
            .transpose(0, 2, 1, 3)
            .reshape(row_count, D)
        )

    query_items, key_items, value_items, coef_items = lax.map(backward_item, items)
    grad_packed = jnp.concatenate(
        [assemble(query_items), fold_keys(key_items), fold_keys(value_items)], axis=1
    ).astype(jnp.bfloat16)
    coef_total = (
        coef_items.reshape(page_count * blocks, groups, 2, HGROUP)
        .sum(axis=0)
        .transpose(1, 0, 2)
        .reshape(2, HEADS)
    )
    grad_bias_query = jnp.sum(grad_packed[:, :D].astype(jnp.float32), axis=0)
    grad_bias_value = jnp.sum(grad_packed[:, 2 * D :].astype(jnp.float32), axis=0)
    grad_wqkv = jnp.einsum(
        "rc,rd->cd", grad_packed, flat_tokens, preferred_element_type=jnp.float32
    )
    grad_tokens = grad_res_one + jnp.einsum(
        "rc,cd->rd", grad_packed, back_qkv, preferred_element_type=jnp.float32
    )
    token_grad = grad_tokens.astype(jnp.bfloat16).reshape(page_count, slot_count, D)
    full_grad = jnp.concatenate(
        [grad_wqkv, grad_wout, grad_wup, grad_wdown, grad_wleft, grad_wright], axis=0
    )
    head_rows = jnp.stack(
        [
            grad_gain_one,
            grad_shift_one,
            grad_bias_query,
            grad_bias_value,
            grad_bias_out,
            grad_gain_two,
            grad_shift_two,
            grad_bias_down,
        ]
    )
    local_vectors = jnp.concatenate([head_rows, grad_bias_up.reshape(FF // D, D)], axis=0)
    vector_len = local_vectors.shape[0] * D
    small_len = vector_len + 2 * HEADS
    device_count = lax.axis_size(("dp", "grid"))
    padded_len = (small_len + device_count - 1) // device_count * device_count
    small_flat = jnp.pad(
        jnp.concatenate([local_vectors.reshape(vector_len), coef_total.reshape(2 * HEADS)]),
        (0, padded_len - small_len),
    )
    weight_grad, small_part = reduce_grads(full_grad, small_flat)
    small_whole = lax.all_gather(small_part, ("dp", "grid"), axis=0, tiled=True)
    vector_grad = small_whole[:vector_len].reshape(local_vectors.shape[0], D)
    coef_grad = small_whole[vector_len:small_len].reshape(2, HEADS)
    rate_scale = (device_count * page_count * slot_count) ** (-0.5)
    new_weight_momentum, new_weights, new_weight_average = momentum_step(
        weight_grad, weights, weight_momentum, weight_average, 0.1 * rate_scale
    )
    new_vector_momentum, new_vectors, new_vector_average = momentum_step(
        vector_grad, vectors, vector_momentum, vector_average, 0.1 * rate_scale
    )
    new_coef_momentum, new_coef, new_coef_average = momentum_step(
        coef_grad, box_coef, coef_momentum, coef_average, 0.01 * rate_scale
    )
    return (
        mixed,
        pair_scores,
        token_grad,
        weight_grad,
        new_weights,
        new_weight_momentum,
        new_weight_average,
        new_weights.astype(jnp.bfloat16),
        vector_grad,
        new_vectors,
        new_vector_momentum,
        new_vector_average,
        coef_grad,
        new_coef,
        new_coef_momentum,
        new_coef_average,
    )


def solution(mesh):
    placed = (
        P(("dp", "grid"), None, None),
        P(("dp", "grid"), None, None),
        P(("dp", "grid"), None),
        P(("dp", "grid")),
        P(("dp", "grid"), None, None),
        P(("dp", "grid"), None, None),
        P(("dp", "grid"), None),
        P(("dp", "grid"), None),
        P(("dp", "grid"), None),
        P(),
        P(),
        P(),
        P(),
        P(),
        P(),
    )
    return jax.shard_map(
        on_device,
        mesh=mesh,
        in_specs=placed,
        out_specs=(
            P(("dp", "grid"), None, None),
            P(("dp", "grid"), None, None),
            P(("dp", "grid"), None, None),
            P(("dp", "grid"), None),
            P(("dp", "grid"), None),
            P(("dp", "grid"), None),
            P(("dp", "grid"), None),
            P(("dp", "grid"), None),
            P(),
            P(),
            P(),
            P(),
            P(),
            P(),
            P(),
            P(),
        ),
        check_vma=False,
    )
```

profile of v0, /device:TPU:0, one launch (start us, length us, event | category | flops | bytes accessed | tf_op | source)
XLA Modules:
  0.0 889.8 jit_solution(108155777906304353)
XLA Ops:
  19.3 108.5 %all-gather.2.cloned.1.call-done = bf16[10752,768]{1,0:T(8,128)(2,1)} async-done(((bf16[336,768]{1,0:T(8,128)(2,1)}), bf16[10752,768]{1,0:T(8,128)(2,1)}) %all-gather.2.cloned.1.call-update) | async-done | bytes 16515088 | tf_op jit(solution)/shard_map/all_gather | solution.py:20
  127.8 7.5 fusion.23
  135.3 6.7 copy.45
  142.0 97.5 %while.34 = (s32[]{:T(128)}, bf16[6,512,256]{1,2,0:T(8,128)(2,1)S(1)}, f32[6,4,512]{2,1,0:T(4,128)}, s32[6]{0:T(128)S(1)}, bf16[1,1024,2304]{1,2,0:T(8,128)(2,1)...) while((s32[]{:T(128)}, ...), condition=%wide.region_3.4_spmd, body=%wide.region_0.3_spmd.sunk | while | flops 582089728 | bytes 46750584 | solution.py:175
  147.0 3.4 fusion.141
  241.6 3.5 fusion.82
  245.7 37.1 %multiply_convert_fusion.1 = (bf16[1024,3072]{1,0:T(8,128)(2,1)}, f32[1024,3072]{1,0:T(8,128)}, f32[1024,3072]{1,0:T(8,128)}) fusion(f32[3072]{0:T(1024)S(1)} %add.402, bf16[10752,768]{1,0:T(8,128)(2,1)} %all-gather.2.cloned.1.call-done, f32[1024,768]{1,0:T(8,128)S(1)} %get-tuple-element.560, f32[768]{0:T(1024)S(1)} %get-tuple-element.475, ...), kind=kOutput, calls=%fused_computation.72 | convolution fusion | flops 5043388416 | bytes 39348224 | tf_op jit(solution)/shard_map/rd,fd->rf/dot_general | solution.py:184
  282.9 17.3 %fusion.83 = (f32[1024]{0:T(1024)S(1)}, f32[1024,768]{1,0:T(8,128)S(1)}) fusion(f32[768]{0:T(1024)S(1)} %copy-done.50, bf16[1024,3072]{1,0:T(8,128)(2,1)} %get-tuple-element.535, bf16[10752,768]{1,0:T(8,128)(2,1)S(1)} %bitcast.272, f32[768]{0:T(1024)S(1)} %get-tuple-element.475, f32[768]{0:T(1024)S(1)} %get-tuple-element.476, ...), kind=kOutput, calls=%fused_computation.209 | convolution fusion | flops 4837342208 | bytes 17326080 | tf_op jit(solution)/shard_map/rf,fd->rd/dot_general | solution.py:188
  314.2 19.3 %convert_reduce_fusion = (f32[3072]{0:T(1024)}, bf16[1024,3072]{1,0:T(8,128)(2,1)}) fusion(f32[1024,3072]{1,0:T(8,128)} %get-tuple-element.536, bf16[10752,768]{1,0:T(8,128)(2,1)} %all-gather.2.cloned.1.call-done, f32[1024,768]{1,0:T(8,128)} %get-tuple-element.529, f32[1024,3072]{1,0:T(8,128)} %get-tuple-element.561, f32[3072]{0:T(1024)S(1)} %add.402), kind=kOutput, calls=%fused_computation.70 | convolution fusion | flops 4886098944 | bytes 39346176 | tf_op jit(solution)/shard_map/rd,fd->rf/dot_general | solution.py:242
  333.6 10.5 %multiply_reduce_fusion.2 = (f32[768]{0:T(1024)}, f32[1024]{0:T(1024)S(1)}, f32[1024]{0:T(1024)S(1)}, f32[768]{0:T(1024)}, f32[1024,768]{1,0:T(8,128)S(1)}) fusion(f32[1024,768]{1,0:T(8,128)S(1)} %get-tuple-element.560, f32[1024]{0:T(1024)S(1)} %add_rsqrt_fusion.1, f32[1024]{0:T(1024)S(1)} %broadcast_multiply_fusion.5, f32[768]{0:T(1024)S(1)} %get-tuple-element.476, ...), kind=kOutput, calls=%fused_computation.105 | convolution fusion | flops 4839698432 | bytes 20472832 | tf_op jit(solution)/shard_map/rf,fd->rd/dot_general | solution.py:246
  350.2 164.0 %while.35 = (s32[]{:T(128)}, bf16[6,512,256]{1,2,0:T(8,128)(2,1)}, f32[6,1024,256]{1,2,0:T(8,128)}, f32[6,1024,256]{1,2,0:T(8,128)}, f32[6,2,4]{2,1,0:T(2,128)S(...) while((s32[]{:T(128)}, bf16[6,512,256]{1,2,0:T(8,128)(2,1)}, ...), condition=%wide.region_17.18_spmd, body=%wide.region_13.17_spmd.sunk | while | flops 1400372224 | bytes 118293552 | solution.py:310
  363.5 3.9 multiply_reduce_fusion.10
  367.4 5.0 fusion.157
  390.9 3.9 multiply_reduce_fusion.10
  394.8 5.0 fusion.157
  418.1 3.9 multiply_reduce_fusion.10
  422.0 5.0 fusion.157
  445.3 3.9 multiply_reduce_fusion.10
  449.2 5.0 fusion.157
  472.5 3.9 multiply_reduce_fusion.10
  476.4 5.0 fusion.157
  499.8 3.9 multiply_reduce_fusion.10
  503.7 5.0 fusion.157
  517.7 3.9 reduce_sum.272
  521.6 5.1 reduce_sum.270
  526.7 8.8 convolution_dynamic-update-slice_fusion.2
  538.5 11.3 %convolution_dynamic-update-slice_fusion.1 = f32[10752,768]{1,0:T(8,128)} fusion(f32[10752,768]{1,0:T(8,128)} %convolution_dynamic-update-slice_fusion.5, bf16[1024,3072]{1,0:T(8,128)(2,1)} %get-tuple-element.568, f32[1024,768]{1,0:T(8,128)S(1)} %copy-done.5, f32[768]{0:T(1024)S(1)} %copy-done.49, f32[768]{0:T(1024)S(1)} %copy-done.37, ...), kind=kOutput, calls=%fused_computation.88 | convolution fusion | flops 4835770368 | bytes 18888704 | tf_op jit(solution)/shard_map/rf,rd->fd/dot_general | solution.py:245
  549.9 8.0 convolution_dynamic-update-slice_fusion
  563.4 38.8 %all-reduce.2 = f32[9248]{0:T(1024)S(1)} all-reduce(f32[9248]{0:T(1024)S(1)} %select_maximum_fusion), channel_id=3, replica_groups=mesh['dp'=8,'grid'=4] {'dp','grid'}, use_global_device_ids=true, to_apply=%region_32.33.clone | all-reduce | flops 9248 | bytes 73984
  602.4 41.9 %all-reduce.1 = f32[9248]{0:T(1024)S(1)} all-reduce(f32[9248]{0:T(1024)S(1)} %dynamic-slice_dynamic-update-slice_fusion), channel_id=1, replica_groups=mesh['dp'=8,'grid'=4] {'dp','grid'}, use_global_device_ids=true, to_apply=%add.1 | all-reduce | flops 9248 | bytes 73984
  648.0 8.7 fusion.47
  656.7 221.5 %reduce-scatter.2.cloned.1.call-done = f32[336,768]{1,0:T(8,128)} async-done(((f32[10752,768]{1,0:T(8,128)}), f32[336,768]{1,0:T(8,128)}) %reduce-scatter.2.cloned.1.call-update) | async-done | bytes 1032208 | tf_op jit(solution)/shard_map/reduce_scatter | solution.py:26
  (435 shorter events, 221.2 us)
Async XLA Ops:
  7.2 296.4 %copy-start = (f32[1,64,64]{2,1,0:T(8,128)S(1)}, f32[1,64,64]{2,1,0:T(8,128)}, u32[]{:S(2)}) copy-start(f32[1,64,64]{2,1,0:T(8,128)} %param.24) | copy-start | bytes 49156
  7.2 120.6 %all-gather.2.cloned.1.call-start = ((), (), s32[]{:S(2)}) async-start(), calls=%async_computation.1 | async-start | bytes 17031168 | tf_op jit(solution)/shard_map/all_gather | solution.py:20
  9.3 868.9 %reduce-scatter.2.cloned.1.call-start = ((), (), s32[]{:S(2)}) async-start(), calls=%async_computation.2 | async-start | bytes 34062336 | tf_op jit(solution)/shard_map/reduce_scatter | solution.py:26
  10.8 117.0 %copy-start.56 = (bf16[1,1024,768]{2,1,0:T(8,128)(2,1)S(1)}, bf16[1,1024,768]{2,1,0:T(8,128)(2,1)}, u32[]{:S(2)}) copy-start(bf16[1,1024,768]{2,1,0:T(8,128)(2,1)} %param.19) | copy-start | bytes 4718596
  12.5 270.3 %copy-start.48 = (f32[768]{0:T(1024)}, f32[768]{0:T(1024)S(1)}, u32[]{:S(2)}) copy-start(f32[768]{0:T(1024)S(1)} %get-tuple-element.475) | copy-start | bytes 9220
  12.6 331.5 %copy-start.36 = (f32[768]{0:T(1024)}, f32[768]{0:T(1024)S(1)}, u32[]{:S(2)}) copy-start(f32[768]{0:T(1024)S(1)} %get-tuple-element.476) | copy-start | bytes 9220
  241.6 41.2 %slice-start = ((s8[16515072]{0:T(1024)(128)(4,1)}), s8[4194304]{0:T(1024)(128)(4,1)S(1)}, s32[]{:S(2)}) async-start(s8[16515072]{0:T(1024)(128)(4,1)} %bitcast.271), calls=%async_computation.3 | async-start | bytes 8388608
  245.1 98.9 %copy-start.4 = (f32[1024,768]{1,0:T(8,128)}, f32[1024,768]{1,0:T(8,128)S(1)}, u32[]{:S(2)}) copy-start(f32[1024,768]{1,0:T(8,128)S(1)} %get-tuple-element.560) | copy-start | bytes 9437188
  245.1 98.9 %copy-start.33 = (f32[1024]{0:T(1024)}, f32[1024]{0:T(1024)S(1)}, u32[]{:S(2)}) copy-start(f32[1024]{0:T(1024)S(1)} %broadcast_multiply_fusion.5) | copy-start | bytes 12292
  245.7 98.4 %copy-start.43 = (f32[1024]{0:T(1024)}, f32[1024]{0:T(1024)S(1)}, u32[]{:S(2)}) copy-start(f32[1024]{0:T(1024)S(1)} %add_rsqrt_fusion.1) | copy-start | bytes 12292
  245.7 37.1 %slice-start.1 = ((s8[16515072]{0:T(1024)(128)(4,1)}), s8[4194304]{0:T(1024)(128)(4,1)S(1)}, s32[]{:S(2)}) async-start(s8[16515072]{0:T(1024)(128)(4,1)} %bitcast.271), calls=%async_computation.4 | async-start | bytes 8388608
  245.7 37.1 %slice-start.2 = ((s8[16515072]{0:T(1024)(128)(4,1)}), s8[4194304]{0:T(1024)(128)(4,1)S(1)}, s32[]{:S(2)}) async-start(s8[16515072]{0:T(1024)(128)(4,1)} %bitcast.271), calls=%async_computation.5 | async-start | bytes 8388608
  245.7 37.1 %slice-start.3 = ((s8[16515072]{0:T(1024)(128)(4,1)}), s8[3932160]{0:T(1024)(128)(4,1)S(1)}, s32[]{:S(2)}) async-start(s8[16515072]{0:T(1024)(128)(4,1)} %bitcast.271), calls=%async_computation.6 | async-start | bytes 7864320
  245.7 37.1 %copy-start.50 = (f32[768]{0:T(1024)S(1)}, f32[768]{0:T(1024)}, u32[]{:S(2)}) copy-start(f32[768]{0:T(1024)} %get-tuple-element.474) | copy-start | bytes 9220
  282.9 17.9 %copy-start.32 = (f32[768]{0:T(1024)S(1)}, f32[768]{0:T(1024)}, u32[]{:S(2)}) copy-start(f32[768]{0:T(1024)} %get-tuple-element.473) | copy-start | bytes 9220
  282.9 17.9 %copy-start.38 = (f32[768]{0:T(1024)S(1)}, f32[768]{0:T(1024)}, u32[]{:S(2)}) copy-start(f32[768]{0:T(1024)} %get-tuple-element.480) | copy-start | bytes 9220
  350.6 11.6 %copy-start.15 = (bf16[1,1024,768]{2,1,0:T(8,128)(2,1)}, bf16[1,1024,768]{2,1,0:T(8,128)(2,1)S(1)}, u32[]{:S(2)}) copy-start(bf16[1,1024,768]{2,1,0:T(8,128)(2,1)S(1)} %get-tuple-element.877) | copy-start | bytes 4718596 | tf_op jit(solution)/shard_map/while
  377.9 11.6 %copy-start.15 = (bf16[1,1024,768]{2,1,0:T(8,128)(2,1)}, bf16[1,1024,768]{2,1,0:T(8,128)(2,1)S(1)}, u32[]{:S(2)}) copy-start(bf16[1,1024,768]{2,1,0:T(8,128)(2,1)S(1)} %get-tuple-element.877) | copy-start | bytes 4718596 | tf_op jit(solution)/shard_map/while
  405.1 11.6 %copy-start.15 = (bf16[1,1024,768]{2,1,0:T(8,128)(2,1)}, bf16[1,1024,768]{2,1,0:T(8,128)(2,1)S(1)}, u32[]{:S(2)}) copy-start(bf16[1,1024,768]{2,1,0:T(8,128)(2,1)S(1)} %get-tuple-element.877) | copy-start | bytes 4718596 | tf_op jit(solution)/shard_map/while
  432.4 11.6 %copy-start.15 = (bf16[1,1024,768]{2,1,0:T(8,128)(2,1)}, bf16[1,1024,768]{2,1,0:T(8,128)(2,1)S(1)}, u32[]{:S(2)}) copy-start(bf16[1,1024,768]{2,1,0:T(8,128)(2,1)S(1)} %get-tuple-element.877) | copy-start | bytes 4718596 | tf_op jit(solution)/shard_map/while
  459.6 11.6 %copy-start.15 = (bf16[1,1024,768]{2,1,0:T(8,128)(2,1)}, bf16[1,1024,768]{2,1,0:T(8,128)(2,1)S(1)}, u32[]{:S(2)}) copy-start(bf16[1,1024,768]{2,1,0:T(8,128)(2,1)S(1)} %get-tuple-element.877) | copy-start | bytes 4718596 | tf_op jit(solution)/shard_map/while
  486.9 11.6 %copy-start.15 = (bf16[1,1024,768]{2,1,0:T(8,128)(2,1)}, bf16[1,1024,768]{2,1,0:T(8,128)(2,1)S(1)}, u32[]{:S(2)}) copy-start(bf16[1,1024,768]{2,1,0:T(8,128)(2,1)S(1)} %get-tuple-element.877) | copy-start | bytes 4718596 | tf_op jit(solution)/shard_map/while
  535.5 14.3 %slice-start.4 = ((s8[6291456]{0:T(1024)(128)(4,1)}), s8[2097152]{0:T(1024)(128)(4,1)S(1)}, s32[]{:S(2)}) async-start(s8[6291456]{0:T(1024)(128)(4,1)} %bitcast.280), calls=%async_computation.7 | async-start | bytes 4194304
  538.4 11.4 %copy-start.10 = (f32[1024,768]{1,0:T(8,128)S(1)}, f32[1024,768]{1,0:T(8,128)}, u32[]{:S(2)}) copy-start(f32[1024,768]{1,0:T(8,128)} %get-tuple-element.529) | copy-start | bytes 9437188
  561.8 82.6 %copy-start.25 = (bf16[64,768]{1,0:T(8,128)(2,1)S(1)}, bf16[64,768]{1,0:T(8,128)(2,1)}, u32[]{:S(2)}) copy-start(bf16[64,768]{1,0:T(8,128)(2,1)} %copy-done.24) | copy-start | bytes 294916
  561.8 82.6 %copy-start.27 = (bf16[64,768]{1,0:T(8,128)(2,1)S(1)}, bf16[64,768]{1,0:T(8,128)(2,1)}, u32[]{:S(2)}) copy-start(bf16[64,768]{1,0:T(8,128)(2,1)} %copy-done.26) | copy-start | bytes 294916
  561.9 83.4 %copy-start.54 = (f32[2,12]{1,0:T(2,128)S(1)}, f32[2,12]{1,0:T(2,128)}, u32[]{:S(2)}) copy-start(f32[2,12]{1,0:T(2,128)} %param.33) | copy-start | bytes 292
  561.9 84.6 %copy-start.29 = (f32[12,768]{1,0:T(8,128)S(1)}, f32[12,768]{1,0:T(8,128)}, u32[]{:S(2)}) copy-start(f32[12,768]{1,0:T(8,128)} %param.28) | copy-start | bytes 110596
  644.4 12.3 %copy-start.55 = (f32[2,12]{1,0:T(2,128)}, f32[2,12]{1,0:T(2,128)S(1)}, u32[]{:S(2)}) copy-start(f32[2,12]{1,0:T(2,128)S(1)} %reshape.438) | copy-start | bytes 292
  644.4 12.3 %copy-start.28 = (f32[12,768]{1,0:T(8,128)}, f32[12,768]{1,0:T(8,128)S(1)}, u32[]{:S(2)}) copy-start(f32[12,768]{1,0:T(8,128)S(1)} %reshape.437) | copy-start | bytes 110596
  648.0 234.8 %copy-start.1 = (f32[1,64,64]{2,1,0:T(8,128)S(1)}, f32[1,64,64]{2,1,0:T(8,128)}, u32[]{:S(2)}) copy-start(f32[1,64,64]{2,1,0:T(8,128)} %param.24) | copy-start | bytes 49156
  656.7 224.8 %copy-start.17 = (f32[336,768]{1,0:T(8,128)S(1)}, f32[336,768]{1,0:T(8,128)}, u32[]{:S(2)}) copy-start(f32[336,768]{1,0:T(8,128)} %param.27) | copy-start | bytes 3096580
  (48 other events, 158.0 us)
Sparse Core Ops, SparseCore 0:
  11.4 116.3 all-gather.1
  562.0 316.1 reduce-scatter.1
where the time goes:
time: 896 us; the launch traced here: 890 us
  waiting for transfers between devices  330 us (37%)
  matrix products  228 us (25%)
  other arithmetic  120 us (13%)
  blocking collectives  80.7 us (9%)
  local copies, waits for them, and re-layouts  78.1 us (9%)
  loops' own time  37.5 us (4%)
  between operations  15.8 us (2%)
    reduce_scatter x1, waiting for transfers between devices, reduce_grads(): lax.psum_scatter(full_grad, ('dp', 'grid'), scatter_dimension=0, tiled=True)  222 us
    all_gather x1, waiting for transfers between devices, fetch_weights(): gathered = lax.all_gather(shard, ('dp', 'grid'), axis=0, tiled=True)  109 us
    unnamed x2, blocking collectives  80.7 us
    dot_general x12, matrix products, block_scores(): jnp.einsum('qgd,kgd->gqk', query_part, key_part, preferred_element_type=j...  40.9 us
    convert_element_type x12, other arithmetic, buckets(): return jnp.minimum(spread // 32, 31).astype(jnp.float32)  40.6 us
    dot_general x1, matrix products, on_device(): jnp.einsum('rd,fd->rf', hidden_low, weight_up, preferred_element_type=jnp...  37.1 us
    reduce_sum x6, other arithmetic, backward_item(): jnp.sum(score_float * bucket[0], axis=(1, 2))  30.2 us
    another operation x1, loops' own time, on_device(): lax.map(backward_item, items)  24.8 us
  transfers between devices with their start and end apart: 2, of which 2 were waited for; matrix products, arithmetic and copies ran while one was open for 2% of the time, Pallas kernels for 0%

commit v1 on v0

v1 whole, which is shorter than its diff:
```python
import math

import jax
import jax.numpy as jnp
from jax import lax
from jax.experimental import pallas as pl
from jax.experimental.pallas import tpu as pltpu
from jax.sharding import PartitionSpec as P

D = 768
HEADS = 12
HDIM = 64
FF = 3072
TEXT = 448
SEGS = 64
GROUP = 4
GW = GROUP * HDIM
TILE = 256
VMEM_LIMIT = 60 * 1024 * 1024
NT = (((1,), (1,)), ((), ()))
NN = (((1,), (0,)), ((), ()))
TN = (((0,), (0,)), ((), ()))

def dot(a, b, dims):
    return lax.dot_general(a, b, dims, preferred_element_type=jnp.float32)


def split_dot(exact, b, dims):
    high = b.astype(jnp.bfloat16)
    rest = b - high.astype(jnp.float32)
    middle = rest.astype(jnp.bfloat16)
    last = (rest - middle.astype(jnp.float32)).astype(jnp.bfloat16)
    return dot(exact, high, dims) + dot(exact, middle, dims) + dot(exact, last, dims)


def params():
    return pltpu.CompilerParams(vmem_limit_bytes=VMEM_LIMIT)


def cost(flops, nbytes):
    return pl.CostEstimate(flops=int(flops), bytes_accessed=int(nbytes), transcendentals=0)


def tile_rows(step):
    return pl.ds(pl.multiple_of(step * TILE, TILE), TILE)


def fixed(shape):
    return pl.BlockSpec(shape, lambda *_: (0,) * len(shape))


def write_buckets(box_row_ref, box_col_ref, bucket_refs):
    def fill(step):
        rows = tile_rows(step)
        for c in range(2):
            spread = jnp.abs(box_col_ref[rows, c : c + 1] - box_row_ref[c : c + 1, :])
            bucket_refs[c][rows, :] = jnp.minimum(spread >> 5, 31).astype(jnp.float32)

    pl.loop(0, box_row_ref.shape[1] // TILE)(fill)


def attention_forward_kernel(
    coef_ref,
    patches_ref,
    tokens_ref,
    wq_ref,
    wk_ref,
    wv_ref,
    bq_ref,
    bv_ref,
    box_row_ref,
    box_col_ref,
    q_ref,
    k_ref,
    v_ref,
    grown_ref,
    att_ref,
    inv_ref,
    bucket0_ref,
    bucket1_ref,
    key_ref,
    value_ref,
):
    head = pl.program_id(0)
    slots = tokens_ref.shape[0]
    own = head % GROUP

    @pl.when(head == 0)
    def _():
        write_buckets(box_row_ref, box_col_ref, (bucket0_ref, bucket1_ref))

    @pl.when(own == 0)
    def _():
        q_ref[...] = (dot(tokens_ref[...], wq_ref[...], NT) + bq_ref[...]).astype(jnp.bfloat16)
        k_ref[...] = dot(tokens_ref[...], wk_ref[...], NT).astype(jnp.bfloat16)
        v_ref[...] = (dot(tokens_ref[...], wv_ref[...], NT) + bv_ref[...]).astype(jnp.bfloat16)

    lanes = lax.broadcasted_iota(jnp.int32, (1, GW), 1)
    mine = lanes // HDIM == own
    mask_lane = lanes == (own * HDIM + HDIM) % GW
    empty = lax.broadcasted_iota(jnp.int32, (slots, 1), 0) >= TEXT + patches_ref[0]
    empty_term = jnp.where(empty, -1e30, 0.0)
    key_ref[...] = jnp.where(
        mine, k_ref[...].astype(jnp.float32), jnp.where(mask_lane, empty_term, 0.0)
    ).astype(jnp.bfloat16)
    value_ref[...] = jnp.where(mine, v_ref[...].astype(jnp.float32), 1.0).astype(jnp.bfloat16)
    coef0 = coef_ref[0, head]
    coef1 = coef_ref[1, head]
    lead = jnp.where(mask_lane, 1.0, 0.0)
    later = own > 0

    def rows_step(step):
        rows = tile_rows(step)
        query = jnp.where(
            mine, q_ref[rows, :].astype(jnp.float32) * HDIM ** (-0.5), lead
        ).astype(jnp.bfloat16)
        score = dot(query, key_ref[...], NT)
        score = score + coef0 * bucket0_ref[rows, :] + coef1 * bucket1_ref[rows, :]
        top = jnp.max(score, axis=1, keepdims=True)
        grown = jnp.exp(score - top).astype(jnp.bfloat16)
        grown_ref[0, rows, :] = grown
        both = dot(grown, value_ref[...], NN)
        inv = 1.0 / pltpu.roll(both, HDIM, 1)
        kept = jnp.where(later, att_ref[rows, :].astype(jnp.float32), 0.0)
        att_ref[rows, :] = jnp.where(mine, both * inv, kept).astype(jnp.bfloat16)
        inv_ref[rows, :] = jnp.where(mine, inv, jnp.where(later, inv_ref[rows, :], 0.0))

    pl.loop(0, slots // TILE, unroll=4)(rows_step)


def attention_forward(tokens, weight_qkv, vectors, boxes, patches, box_coef):
    slots = tokens.shape[0]
    blocks = D // GW
    smem = pl.BlockSpec(memory_space=pltpu.SMEM)
    lane_block = pl.BlockSpec((slots, GW), lambda h: (0, h // GROUP))
    bias = pl.BlockSpec((1, GW), lambda h: (0, h // GROUP))
    wide = jax.ShapeDtypeStruct((slots, D), jnp.bfloat16)

    def weight(at):
        return pl.BlockSpec((GW, D), lambda h: (at * blocks + h // GROUP, 0))

    return pl.pallas_call(
        attention_forward_kernel,
        grid=(HEADS,),
        in_specs=[
            smem,
            smem,
            fixed((slots, D)),
            weight(0),
            weight(1),
            weight(2),
            bias,
            bias,
            fixed((2, slots)),
            fixed((slots, 2)),
        ],
        out_specs=[lane_block] * 3
        + [pl.BlockSpec((1, slots, slots), lambda h: (h, 0, 0)), lane_block, lane_block],
        out_shape=[wide] * 3
        + [
            jax.ShapeDtypeStruct((HEADS, slots, slots), jnp.bfloat16),
            wide,
            jax.ShapeDtypeStruct((slots, D), jnp.float32),
        ],
        scratch_shapes=[pltpu.VMEM((slots, slots), jnp.float32)] * 2
        + [pltpu.VMEM((slots, GW), jnp.bfloat16)] * 2,
        compiler_params=params(),
        cost_estimate=cost(10e9, 40e6),
        name="attention_forward",
    )(
        box_coef,
        patches,
        tokens,
        weight_qkv,
        weight_qkv,
        weight_qkv,
        vectors[2:3],
        vectors[3:4],
        boxes,
        boxes.T,
    )


def normalize(values):
    centered = values - jnp.mean(values, axis=-1, keepdims=True)
    inv_std = lax.rsqrt(jnp.mean(centered * centered, axis=-1, keepdims=True) + 1e-05)
    return (centered * inv_std, inv_std)


def normalize_back(grad_normed, normed, inv_std):
    first_mean = jnp.mean(grad_normed, axis=-1, keepdims=True)
    second_mean = jnp.mean(grad_normed * normed, axis=-1, keepdims=True)
    return inv_std * (grad_normed - first_mean - normed * second_mean)


def gelu_pair(values):
    half = values * (0.5**0.5)
    size = jnp.abs(half)
    fraction = 1.0 / (1.0 + 0.3275911 * size)
    series = fraction * (
        0.254829592
        + fraction
        * (
            -0.284496736
            + fraction * (1.421413741 + fraction * (-1.453152027 + fraction * 1.061405429))
        )
    )
    bell = jnp.exp(-half * half)
    tail = 0.5 * series * bell
    below = jnp.where(values >= 0, 1.0 - tail, tail)
    return (values * below, below + values * bell * (0.5 / math.pi) ** 0.5)


def feed_forward_kernel(
    att_ref,
    tokens_ref,
    wo_ref,
    wu_ref,
    wd_ref,
    wl_ref,
    wr_ref,
    vectors_ref,
    segments_ref,
    cot_pair_ref,
    mixed_ref,
    normed1_ref,
    inv1_ref,
    hidden_ref,
    act_ref,
    slope_ref,
    normed2_ref,
    inv2_ref,
    pair_ref,
    spread_ref,
    dleft_ref,
    dright_ref,
    total_ref,
):
    step = pl.program_id(0)
    tile = att_ref.shape[0]
    branch = dot(att_ref[...], wo_ref[...], NT) + vectors_ref[4:5, :]
    normed1, inv1 = normalize(tokens_ref[...].astype(jnp.float32) + branch)
    hidden = normed1 * vectors_ref[0:1, :] + vectors_ref[1:2, :]
    low = hidden.astype(jnp.bfloat16)
    normed1_ref[...] = normed1
    inv1_ref[...] = inv1
    hidden_ref[...] = low
    feed = hidden + vectors_ref[7:8, :]
    for part in range(FF // D):
        cols = slice(part * D, (part + 1) * D)
        pre = dot(low, wu_ref[cols, :], NT) + vectors_ref[8 + part : 9 + part, :]
        act, slope = gelu_pair(pre)
        act = act.astype(jnp.bfloat16)
        act_ref[:, cols] = act
        slope_ref[:, cols] = slope.astype(jnp.bfloat16)
        feed = feed + dot(act, wd_ref[cols, :], NN)
    normed2, inv2 = normalize(feed)
    output = normed2 * vectors_ref[5:6, :] + vectors_ref[6:7, :]
    normed2_ref[...] = normed2
    inv2_ref[...] = inv2
    mixed_ref[...] = output.astype(jnp.bfloat16)

    @pl.when(step == 0)
    def _():
        total_ref[...] = jnp.zeros_like(total_ref)

    slot = step * tile + lax.broadcasted_iota(jnp.int32, (1, tile), 1)
    numbers = lax.broadcasted_iota(jnp.int32, (SEGS, 1), 0)

    @pl.when(step * tile < TEXT)
    def _():
        member = (segments_ref[:, pl.ds(pl.multiple_of(step * tile, tile), tile)] == numbers) & (slot < TEXT)
        total_ref[...] += split_dot(member.astype(jnp.bfloat16), output, NN)

    @pl.when(step == pl.num_programs(0) - 1)
    def _():
        member = (segments_ref[...] == numbers) & (
            lax.broadcasted_iota(jnp.int32, (1, segments_ref.shape[1]), 1) < TEXT
        )
        counted = jnp.sum(member.astype(jnp.float32), axis=1, keepdims=True)
        pooled = (total_ref[...] / counted).astype(jnp.bfloat16)
        scale = D ** (-0.5)
        left = dot(pooled, wl_ref[...], NT).astype(jnp.bfloat16)
        right = dot(pooled, wr_ref[...], NT).astype(jnp.bfloat16)
        pair_ref[...] = dot(left, right, NT) * scale
        cot = cot_pair_ref[...]
        grad_left = (split_dot_left(cot, right, NN) * scale).astype(jnp.bfloat16)
        grad_right = (split_dot_left(cot, left, TN) * scale).astype(jnp.bfloat16)
        grad_pooled = dot(grad_left, wl_ref[...], NN) + dot(grad_right, wr_ref[...], NN)
        spread_ref[...] = grad_pooled / counted
        dleft_ref[...] = dot(grad_left, pooled, TN).astype(jnp.bfloat16)
        dright_ref[...] = dot(grad_right, pooled, TN).astype(jnp.bfloat16)


def split_dot_left(a, exact, dims):
    high = a.astype(jnp.bfloat16)
    rest = a - high.astype(jnp.float32)
    middle = rest.astype(jnp.bfloat16)
    last = (rest - middle.astype(jnp.float32)).astype(jnp.bfloat16)
    return dot(high, exact, dims) + dot(middle, exact, dims) + dot(last, exact, dims)


def feed_forward(att, tokens, weights, vectors, segments, cot_pair):
    slots = att.shape[0]
    tile = pl.BlockSpec((TILE, D), lambda i: (i, 0))
    wide = pl.BlockSpec((TILE, FF), lambda i: (i, 0))
    column = pl.BlockSpec((TILE, 1), lambda i: (i, 0))

    def weight(rows, at):
        return pl.BlockSpec((rows, D), lambda i: (at // rows, 0), pipeline_mode=pl.Buffered(1))

    def shape(dims, dtype=jnp.float32):
        return jax.ShapeDtypeStruct(dims, dtype)

    return pl.pallas_call(
        feed_forward_kernel,
        grid=(slots // TILE,),
        in_specs=[
            tile,
            tile,
            weight(D, 3 * D),
            pl.BlockSpec((pl.Element(FF), pl.Element(D)), lambda i: (4 * D, 0), pipeline_mode=pl.Buffered(1)),
            pl.BlockSpec((pl.Element(FF), pl.Element(D)), lambda i: (4 * D + FF, 0), pipeline_mode=pl.Buffered(1)),
            weight(D, 4 * D + 2 * FF),
            weight(D, 5 * D + 2 * FF),
            fixed(vectors.shape),
            fixed((1, 512)),
            fixed((SEGS, SEGS)),
        ],
        out_specs=[tile, tile, column, tile, wide, wide, tile, column, fixed((SEGS, SEGS)), fixed((SEGS, D)), fixed((D, D)), fixed((D, D))],
        out_shape=[
            shape((slots, D), jnp.bfloat16),
            shape((slots, D)),
            shape((slots, 1)),
            shape((slots, D), jnp.bfloat16),
            shape((slots, FF), jnp.bfloat16),
            shape((slots, FF), jnp.bfloat16),
            shape((slots, D)),
            shape((slots, 1)),
            shape((SEGS, SEGS)),
            shape((SEGS, D)),
            shape((D, D), jnp.bfloat16),
            shape((D, D), jnp.bfloat16),
        ],
        scratch_shapes=[pltpu.VMEM((SEGS, D), jnp.float32)],
        compiler_params=params(),
        cost_estimate=cost(11e9, 50e6),
        name="feed_forward",
    )(
        att,
        tokens,
        weights,
        weights,
        weights,
        weights,
        weights,
        vectors,
        jnp.pad(segments, ((0, 0), (0, 512 - segments.shape[1])), constant_values=SEGS),
        cot_pair,
    )


def feed_backward_kernel(
    patches_ref,
    cot_ref,
    segments_ref,
    spread_ref,
    normed2_ref,
    inv2_ref,
    normed1_ref,
    inv1_ref,
    hidden_ref,
    att_ref,
    inv_sum_ref,
    vectors_ref,
    act_ref,
    slope_ref,
    wd_ref,
    wu_ref,
    wo_ref,
    dwd_ref,
    dwu_ref,
    dbu_ref,
    sums_ref,
    dwo_ref,
    dres_ref,
    datt_ref,
    grad_ref,
    total_ref,
):
    step = pl.program_id(0)
    slots = cot_ref.shape[0]

    @pl.when(step == 0)
    def _():
        sums_ref[...] = jnp.zeros_like(sums_ref)
        numbers = lax.broadcasted_iota(jnp.int32, (1, SEGS), 1)

        def rows_step(at):
            rows = tile_rows(at)
            slot = at * TILE + lax.broadcasted_iota(jnp.int32, (TILE, 1), 0)
            live = (slot < TEXT + patches_ref[0]).astype(jnp.float32)
            member = (segments_ref[rows, :] == numbers) & (slot < TEXT)
            grad = cot_ref[rows, :].astype(jnp.float32) * live
            grad = grad + split_dot(member.astype(jnp.bfloat16), spread_ref[...], NN)
            normed = normed2_ref[rows, :]
            sums_ref[5:6, :] += jnp.sum(grad * normed, axis=0, keepdims=True)
            sums_ref[6:7, :] += jnp.sum(grad, axis=0, keepdims=True)
            dres = normalize_back(grad * vectors_ref[5:6, :], normed, inv2_ref[rows, :])
            low = dres.astype(jnp.bfloat16)
            sums_ref[7:8, :] += jnp.sum(low.astype(jnp.float32), axis=0, keepdims=True)
            total_ref[rows, :] = dres
            grad_ref[rows, :] = low

        pl.loop(0, slots // TILE)(rows_step)

    dwd_ref[...] = dot(act_ref[...], grad_ref[...], TN).astype(jnp.bfloat16)
    dact = dot(grad_ref[...], wd_ref[...], NT)
    dpre = (dact * slope_ref[...].astype(jnp.float32)).astype(jnp.bfloat16)
    dbu_ref[...] = jnp.sum(dpre.astype(jnp.float32), axis=0, keepdims=True)
    dwu_ref[...] = dot(dpre, hidden_ref[...], TN).astype(jnp.bfloat16)
    total_ref[...] += dot(dpre, wu_ref[...], NN)

    @pl.when(step == pl.num_programs(0) - 1)
    def _():
        def rows_step(at):
            rows = tile_rows(at)
            grad = total_ref[rows, :]
            normed = normed1_ref[rows, :]
            sums_ref[0:1, :] += jnp.sum(grad * normed, axis=0, keepdims=True)
            sums_ref[1:2, :] += jnp.sum(grad, axis=0, keepdims=True)
            dres = normalize_back(grad * vectors_ref[0:1, :], normed, inv1_ref[rows, :])
            low = dres.astype(jnp.bfloat16)
            sums_ref[4:5, :] += jnp.sum(low.astype(jnp.float32), axis=0, keepdims=True)
            dres_ref[rows, :] = dres
            grad_ref[rows, :] = low
            datt = dot(low, wo_ref[...], NN).astype(jnp.bfloat16).astype(jnp.float32)
            datt_ref[rows, :] = (datt * inv_sum_ref[rows, :]).astype(jnp.bfloat16)

        pl.loop(0, slots // TILE)(rows_step)
        dwo_ref[...] = dot(grad_ref[...], att_ref[...], TN).astype(jnp.bfloat16)


def feed_backward(patches, cot_out, segments, spread, forward, att, inv_sum, vectors, weights):
    _, normed1, inv1, hidden, act, slope, normed2, inv2 = forward
    slots = cot_out.shape[0]
    chunk = 512

    def once(shape):
        return pl.BlockSpec(shape, lambda *_: (0,) * len(shape), pipeline_mode=pl.Buffered(1))

    def weight(at):
        return pl.BlockSpec((chunk, D), lambda i: (at // chunk + i, 0))

    def shape(dims, dtype=jnp.float32):
        return jax.ShapeDtypeStruct(dims, dtype)

    lane_block = pl.BlockSpec((slots, chunk), lambda i: (0, i))
    row_block = pl.BlockSpec((chunk, D), lambda i: (i, 0))
    full = once((slots, D))
    column = once((slots, 1))
    return pl.pallas_call(
        feed_backward_kernel,
        grid=(FF // chunk,),
        in_specs=[
            pl.BlockSpec(memory_space=pltpu.SMEM),
            full,
            column,
            once((SEGS, D)),
            full,
            column,
            full,
            column,
            full,
            full,
            full,
            once(vectors.shape),
            lane_block,
            lane_block,
            weight(4 * D + FF),
            weight(4 * D),
            pl.BlockSpec((D, D), lambda i: (3, 0), pipeline_mode=pl.Buffered(1)),
        ],
        out_specs=[row_block, row_block, pl.BlockSpec((1, chunk), lambda i: (0, i)), fixed((8, D)), fixed((D, D)), full, full],
        out_shape=[
            shape((FF, D), jnp.bfloat16),
            shape((FF, D), jnp.bfloat16),
            shape((1, FF)),
            shape((8, D)),
            shape((D, D), jnp.bfloat16),
            shape((slots, D)),
            shape((slots, D), jnp.bfloat16),
        ],
        scratch_shapes=[pltpu.VMEM((slots, D), jnp.bfloat16), pltpu.VMEM((slots, D), jnp.float32)],
        compiler_params=params(),
        cost_estimate=cost(22e9, 60e6),
        name="feed_backward",
    )(
        patches,
        cot_out,
        jnp.pad(segments, ((0, 0), (0, slots - segments.shape[1])), constant_values=SEGS).reshape(slots, 1),
        spread,
        normed2,
        inv2,
        normed1,
        inv1,
        hidden,
        att,
        inv_sum,
        vectors,
        act,
        slope,
        weights,
        weights,
        weights,
    )


def attention_backward_kernel(
    grown_ref,
    datt_ref,
    att_ref,
    v_ref,
    k_ref,
    q_ref,
    box_row_ref,
    box_col_ref,
    dqkv_ref,
    dcoef_ref,
    bucket0_ref,
    bucket1_ref,
    value_ref,
    lead_ref,
    qt_ref,
    dt_ref,
    kt_ref,
    dscore_ref,
):
    head = pl.program_id(0)
    slots = datt_ref.shape[0]
    own = head % GROUP

    @pl.when(head == 0)
    def _():
        write_buckets(box_row_ref, box_col_ref, (bucket0_ref, bucket1_ref))

    @pl.when(own == 0)
    def _():
        scale = HDIM ** (-0.5)
        qt_ref[...] = (q_ref[...].astype(jnp.float32) * scale).T.astype(jnp.bfloat16)
        kt_ref[...] = (k_ref[...].astype(jnp.float32) * scale).T.astype(jnp.bfloat16)
        dt_ref[...] = datt_ref[...].astype(jnp.float32).T.astype(jnp.bfloat16)

    lanes = lax.broadcasted_iota(jnp.int32, (1, GW), 1)
    mine = lanes // HDIM == own
    at = (own * HDIM + HDIM) % GW
    value_ref[...] = jnp.where(
        mine,
        v_ref[...].astype(jnp.float32),
        jnp.where((lanes >= at) & (lanes < at + 3), -1.0, 0.0),
    ).astype(jnp.bfloat16)
    grad = datt_ref[...].astype(jnp.float32)
    delta = jnp.sum(
        jnp.where(mine, grad * att_ref[...].astype(jnp.float32), 0.0), axis=1, keepdims=True
    )
    high = delta.astype(jnp.bfloat16).astype(jnp.float32)
    middle = (delta - high).astype(jnp.bfloat16).astype(jnp.float32)
    last = delta - high - middle
    terms = jnp.where(lanes == at, high, jnp.where(lanes == at + 1, middle, last))
    terms = jnp.where((lanes >= at) & (lanes < at + 3), terms, 0.0)
    lead_ref[...] = jnp.where(mine, grad, terms).astype(jnp.bfloat16)
    dcoef_ref[...] = jnp.zeros_like(dcoef_ref)

    def rows_step(step):
        rows = tile_rows(step)
        diff = dot(lead_ref[rows, :], value_ref[...], NT)
        dscore = grown_ref[0, rows, :].astype(jnp.float32) * diff
        dscore_ref[rows, :] = dscore.astype(jnp.bfloat16)
        dcoef_ref[0, 0:1, :] += jnp.sum(dscore * bucket0_ref[rows, :], axis=0, keepdims=True)
        dcoef_ref[0, 1:2, :] += jnp.sum(dscore * bucket1_ref[rows, :], axis=0, keepdims=True)

    pl.loop(0, slots // TILE, unroll=4)(rows_step)
    head_rows = pl.ds(pl.multiple_of(own * HDIM, HDIM), HDIM)
    dqkv_ref[0] = dot(kt_ref[head_rows, :], dscore_ref[...], NT).astype(jnp.bfloat16)
    dqkv_ref[1] = dot(qt_ref[head_rows, :], dscore_ref[...], NN).astype(jnp.bfloat16)
    dqkv_ref[2] = dot(dt_ref[head_rows, :], grown_ref[0], NN).astype(jnp.bfloat16)


def attention_backward(grown, datt, att, q, k, v, boxes):
    slots = datt.shape[0]
    lane_block = pl.BlockSpec((slots, GW), lambda h: (0, h // GROUP))
    return pl.pallas_call(
        attention_backward_kernel,
        grid=(HEADS,),
        in_specs=[pl.BlockSpec((1, slots, slots), lambda h: (h, 0, 0))]
        + [lane_block] * 5
        + [fixed((2, slots)), fixed((slots, 2))],
        out_specs=[
            pl.BlockSpec((3, HDIM, slots), lambda h: (0, h, 0)),
            pl.BlockSpec((1, 2, slots), lambda h: (h, 0, 0)),
        ],
        out_shape=[
            jax.ShapeDtypeStruct((3, D, slots), jnp.bfloat16),
            jax.ShapeDtypeStruct((HEADS, 2, slots), jnp.float32),
        ],
        scratch_shapes=[pltpu.VMEM((slots, slots), jnp.float32)] * 2
        + [pltpu.VMEM((slots, GW), jnp.bfloat16)] * 2
        + [pltpu.VMEM((GW, slots), jnp.bfloat16)] * 3
        + [pltpu.VMEM((slots, slots), jnp.bfloat16)],
        compiler_params=params(),
        cost_estimate=cost(15e9, 40e6),
        name="attention_backward",
    )(grown, datt, att, v, k, q, boxes, boxes.T)


def token_backward_kernel(dqkv_ref, weight_ref, tokens_ref, dres_ref, dweight_ref, sums_ref, grad_ref, total_ref):
    step = pl.program_id(0)
    part = dqkv_ref[0]
    dweight_ref[...] = dot(part, tokens_ref[...], NN).astype(jnp.bfloat16)
    sums_ref[0] = dot(jnp.ones((8, part.shape[1]), jnp.bfloat16), part, NT)
    term = dot(part, weight_ref[...], TN)

    @pl.when(step == 0)
    def _():
        total_ref[...] = dres_ref[...] + term

    @pl.when(step > 0)
    def _():
        total_ref[...] += term

    @pl.when(step == pl.num_programs(0) - 1)
    def _():
        grad_ref[...] = total_ref[...].astype(jnp.bfloat16)


def token_backward(dqkv, weights, tokens, dres):
    slots = tokens.shape[0]
    block = pl.BlockSpec((D, D), lambda i: (i, 0))
    return pl.pallas_call(
        token_backward_kernel,
        grid=(3,),
        in_specs=[pl.BlockSpec((1, D, slots), lambda i: (i, 0, 0)), block, fixed((slots, D)), fixed((slots, D))],
        out_specs=[block, pl.BlockSpec((1, 8, D), lambda i: (i, 0, 0)), fixed((slots, D))],
        out_shape=[
            jax.ShapeDtypeStruct((3 * D, D), jnp.bfloat16),
            jax.ShapeDtypeStruct((3, 8, D), jnp.float32),
            jax.ShapeDtypeStruct((slots, D), jnp.bfloat16),
        ],
        scratch_shapes=[pltpu.VMEM((slots, D), jnp.float32)],
        compiler_params=params(),
        cost_estimate=cost(7.3e9, 20e6),
        name="token_backward",
    )(dqkv, weights, tokens, dres)


def page_step(tokens, boxes, segments, patches, cot_out, cot_pair, gathered, vectors, box_coef):
    q, k, v, grown, att, inv_sum = attention_forward(
        tokens, gathered, vectors, boxes, patches, box_coef
    )
    found = feed_forward(att, tokens, gathered, vectors, segments, cot_pair)
    mixed, pair_scores, spread, dwl, dwr = found[0], found[8], found[9], found[10], found[11]
    dwd, dwu, dbu, sums, dwo, dres, datt = feed_backward(
        patches, cot_out, segments, spread, found[:8], att, inv_sum, vectors, gathered
    )
    dqkv, dcoef = attention_backward(grown, datt, att, q, k, v, boxes)
    dwqkv, bias_sums, token_grad = token_backward(dqkv, gathered, tokens, dres)
    vector_part = jnp.concatenate(
        [sums[:2], bias_sums[0, :1], bias_sums[2, :1], sums[4:8], dbu.reshape(FF // D, D)], axis=0
    )
    coef_part = jnp.sum(dcoef, axis=2).T
    return (mixed, pair_scores, token_grad, (dwqkv, dwo, dwu, dwd, dwl, dwr), vector_part, coef_part)


def exchange_sum(values):
    for axis in ("dp", "grid"):
        size = lax.axis_size(axis)
        reach = 1
        while reach < size:
            values = values + lax.ppermute(values, axis, [(i, i ^ reach) for i in range(size)])
            reach *= 2
    return values


def momentum_step(grad, param, moment, average, rate):
    new_moment = 0.5 * moment + grad
    new_param = param - rate * (grad + 0.5 * new_moment)
    new_average = 0.5 * average + 0.5 * new_param
    return (new_moment, new_param, new_average)


def on_device(
    tokens,
    boxes,
    segments,
    patches,
    cot_out,
    cot_pair,
    weights,
    weight_momentum,
    weight_average,
    vectors,
    vector_momentum,
    vector_average,
    box_coef,
    coef_momentum,
    coef_average,
):
    axes = ("dp", "grid")
    page_count, slot_count = tokens.shape[:2]
    device_count = lax.axis_size(axes)
    gathered = lax.all_gather(weights.astype(jnp.bfloat16), axes, axis=0, tiled=True)
    pages = [
        page_step(
            tokens[p], boxes[p], segments[p : p + 1], patches[p : p + 1], cot_out[p], cot_pair[p], gathered, vectors, box_coef
        )
        for p in range(page_count)
    ]
    mixed, pair_scores, token_grad = (jnp.stack([page[i] for page in pages]) for i in range(3))
    full_grad = sum(jnp.concatenate(page[3], axis=0) for page in pages)
    small = sum(
        jnp.concatenate([page[4], jnp.pad(page[5].reshape(1, 2 * HEADS), ((0, 3), (0, D - 2 * HEADS)))], axis=0)
        for page in pages
    )
    small = exchange_sum(small)
    weight_grad = lax.psum_scatter(full_grad, axes, scatter_dimension=0, tiled=True).astype(jnp.float32)
    vector_rows = vectors.shape[0]
    vector_grad = small[:vector_rows]
    coef_grad = small[vector_rows, : 2 * HEADS].reshape(2, HEADS)
    rate_scale = (device_count * page_count * slot_count) ** (-0.5)
    new_weight_momentum, new_weights, new_weight_average = momentum_step(
        weight_grad, weights, weight_momentum, weight_average, 0.1 * rate_scale
    )
    new_vector_momentum, new_vectors, new_vector_average = momentum_step(
        vector_grad, vectors, vector_momentum, vector_average, 0.1 * rate_scale
    )
    new_coef_momentum, new_coef, new_coef_average = momentum_step(
        coef_grad, box_coef, coef_momentum, coef_average, 0.01 * rate_scale
    )
    return (
        mixed,
        pair_scores,
        token_grad,
        weight_grad,
        new_weights,
        new_weight_momentum,
        new_weight_average,
        new_weights.astype(jnp.bfloat16),
        vector_grad,
        new_vectors,
        new_vector_momentum,
        new_vector_average,
        coef_grad,
        new_coef,
        new_coef_momentum,
        new_coef_average,
    )


def solution(mesh):
    rows = P(("dp", "grid"))
    return jax.shard_map(
        on_device,
        mesh=mesh,
        in_specs=(rows,) * 9 + (P(),) * 6,
        out_specs=(rows,) * 8 + (P(),) * 8,
        check_vma=False,
    )
```

time: 896 us -> 510 us (0.57)
  matrix products: 228 us -> 0 us
  Pallas kernels: 0 us -> 169 us
  other arithmetic: 120 us -> 8.17 us
  blocking collectives: 80.7 us -> 0 us
  local copies, waits for them, and re-layouts: 78.1 us -> 21.1 us
  waiting for transfers between devices: 330 us -> 291 us
  loops' own time: 37.5 us -> 0 us
    dot_general x65 -> x0, matrix products: 228 us -> none  [the longest x12 40.9 us: block_scores(): jnp.einsum('qgd,kgd->gqk', query_part, key_part, preferred_element_type=j...]
    pallas_call x0 -> x5, Pallas kernels: none -> 169 us  [the longest x1 41.4 us: attention_backward(): pl.pallas_call(attention_backward_kernel, grid=(HEADS,), in_specs=[pl.Blo...]
    unnamed x2 -> x0, blocking collectives: 80.7 us -> none
    reduce_sum x25 -> x1, other arithmetic: 62.6 us -> 0.11 us  [page_step(): coef_part = jnp.sum(dcoef, axis=2).T]
    reduce_scatter x1, waiting for transfers between devices: 222 us -> 165 us  [on_device(): lax.psum_scatter(full_grad, axes, scatter_dimension=0, tiled=True)]
    convert_element_type x14 -> x1, other arithmetic: 42.6 us -> 2.06 us  [on_device(): weights.astype(jnp.bfloat16)]
    another operation x2 -> x0, loops' own time: 37.5 us -> none  [the longest x1 24.8 us: on_device(): lax.map(backward_item, items)]
    dynamic_slice x60 -> x0, local copies, waits for them, and re-layouts: 36.4 us -> none  [the longest x12 11.7 us: block_scores(): lax.dynamic_slice(page_rows, (block_index * BLOCK, group_index * group_wi...]
  transfers between devices with their start and end apart: 2 -> 7, of which waited for: 2 -> 7; matrix products, arithmetic and copies ran while one was open for 2% -> 2% of each run, Pallas kernels for 0% -> 0%
where the time goes in v1:
time: 510 us
  waiting for transfers between devices  291 us (57%)
  Pallas kernels  169 us (33%)
  local copies, waits for them, and re-layouts  21.1 us (4%)
  between operations  14.9 us (3%)
  other arithmetic  8.17 us (2%)
  starting transfers between devices  5.64 us (1%)
    reduce_scatter x1, waiting for transfers between devices, on_device(): lax.psum_scatter(full_grad, axes, scatter_dimension=0, tiled=True)  165 us
    all_gather x1, waiting for transfers between devices, on_device(): lax.all_gather(weights.astype(jnp.bfloat16), axes, axis=0, tiled=True)  112 us
    pallas_call x1, Pallas kernels, attention_backward(): pl.pallas_call(attention_backward_kernel, grid=(HEADS,), in_specs=[pl.Blo...  41.4 us
    pallas_call x1, Pallas kernels, feed_backward(): pl.pallas_call(feed_backward_kernel, grid=(FF // chunk,), in_specs=[pl.Bl...  40.1 us
    pallas_call x1, Pallas kernels, attention_forward(): pl.pallas_call(attention_forward_kernel, grid=(HEADS,), in_specs=[smem, s...  38.4 us
    pallas_call x1, Pallas kernels, feed_forward(): pl.pallas_call(feed_forward_kernel, grid=(slots // TILE,), in_specs=[tile...  34.5 us
    pallas_call x1, Pallas kernels, token_backward(): pl.pallas_call(token_backward_kernel, grid=(3,), in_specs=[pl.BlockSpec((...  14.9 us
    ppermute x5, waiting for transfers between devices, exchange_sum(): lax.ppermute(values, axis, [(i, i ^ reach) for i in range(size)])  13.6 us
  transfers between devices with their start and end apart: 7, of which 7 were waited for; matrix products, arithmetic and copies ran while one was open for 2% of the time, Pallas kernels for 0%

profile of v1, /device:TPU:0, one launch (start us, length us, event | category | flops | bytes accessed | tf_op | source)
XLA Modules:
  0.0 509.8 jit_solution(15086926703968214367)
XLA Ops:
  7.2 2.1 convert_element_type.11
  9.4 0.9 copy.38
  10.3 0.8 copy.39.box_row_ref
  11.7 1.3 pad.12.segments_ref
  13.0 0.7 pad_bitcast_fusion
  13.7 1.0 copy.40.segments_ref
  14.7 1.4 fusion.1
  16.1 111.7 %all-gather.2.cloned.1.call-done.wq_ref.wk_ref.wv_ref.wo_ref.wu_ref.wd_ref.wl_ref.wr_ref.weight_ref = bf16[10752,768]{1,0:T(8,128)(2,1)} async-done(((bf16[336,768]{1,0:T(8,128)(2,1)}), bf16[10752,768]{1,0:T(8,128)(2,1)}) %all-gather.2.cloned.1.call-update) | async-done | bytes 16515088 | tf_op jit(solution)/shard_map/all_gather | solution.py:711
  127.8 38.4 %attention_forward.1 = (bf16[1024,768]{1,0:T(8,128)(2,1)}, bf16[1024,768]{1,0:T(8,128)(2,1)}, bf16[1024,768]{1,0:T(8,128)(2,1)}, bf16[12,1024,1024]{2,1,0:T(8,12...) custom-call(f32[2,12]{1,0:T(2,128)} %coef_ref.1, s32[1]{0:T(128)S(6)} %copy.48.patches_ref, ...), custom_call_target="tpu_custom_call" | custom-call | flops 10000000000 | bytes 40000000 | tf_op jit(solution)/shard_map/attention_forward/pallas_call | solution.py:142
  166.2 34.5 %feed_forward.1 = (bf16[1024,768]{1,0:T(8,128)(2,1)}, f32[1024,768]{1,0:T(8,128)}, f32[1024,1]{1,0:T(8,128)}, bf16[1024,768]{1,0:T(8,128)(2,1)}, bf16[1024,3072]...) custom-call(bf16[1024,768]{1,0:T(8,128)(2,1)} %get-tuple-element.46., ...), custom_call_target="tpu_custom_call" | custom-call | flops 11000000512 | bytes 50000000 | tf_op jit(solution)/shard_map/feed_forward/pallas_call | solution.py:315
  200.6 40.1 %feed_backward.1 = (bf16[3072,768]{1,0:T(8,128)(2,1)}, bf16[3072,768]{1,0:T(8,128)(2,1)}, f32[1,3072]{1,0:T(1,128)}, f32[8,768]{1,0:T(8,128)}, bf16[768,768]{1,0...) custom-call(s32[1]{0:T(128)S(6)} %copy.48.patches_ref, bf16[1024,768]{1,0:T(8,128)(2,1)} %bitcast.28, ...), custom_call_target="tpu_custom_call" | custom-call | flops 22000001024 | bytes 60000000 | tf_op jit(solution)/shard_map/feed_backward/pallas_call | solution.py:462
  240.7 41.4 %attention_backward.1 = (bf16[3,768,1024]{2,1,0:T(8,128)(2,1)}, f32[12,2,1024]{2,1,0:T(2,128)}) custom-call(bf16[12,1024,1024]{2,1,0:T(8,128)(2,1)} %get-tuple-element.49.grown_ref, bf16[1024,768]{1,0:T(8,128)(2,1)} %get-tuple-element.59.datt_ref, bf16[1024,768]{1,0:T(8,128)(2,1)} %get-tuple-element.46.att_ref, bf16[1024,768]{1,0:T(8,128)(2,1)} %get-tuple-element.60.v_ref, ...), custom_call_target="tpu_custom_call" | custom-call | flops 15000000512 | bytes 40000000 | tf_op jit(solution)/shard_map/attention_backward/pallas_call | solution.py:592
  282.1 14.9 %token_backward.1 = (bf16[2304,768]{1,0:T(8,128)(2,1)}, f32[3,8,768]{2,1,0:T(8,128)}, bf16[1024,768]{1,0:T(8,128)(2,1)}) custom-call(bf16[3,768,1024]{2,1,0:T(8,128)(2,1)} %get-tuple-element.63.dqkv_ref, bf16[10752,768]{1,0:T(8,128)(2,1)} %all-gather.2.cloned.1.call-done.wq_ref.wk_ref.wv_ref.wo_ref.wu_ref.wd_ref.wl_ref.wr_ref.weight_ref, ...), custom_call_target="tpu_custom_call" | custom-call | flops 7299999744 | bytes 20000000 | tf_op jit(solution)/shard_map/token_backward/pallas_call | solution.py:639
  297.1 4.1 constant_dynamic-update-slice_fusion.5
  301.2 1.1 constant_dynamic-update-slice_fusion.4
  302.3 2.5 constant_dynamic-update-slice_fusion.3
  304.9 2.5 constant_dynamic-update-slice_fusion.2
  307.4 1.1 constant_dynamic-update-slice_fusion.1
  308.5 1.1 constant_dynamic-update-slice_fusion
  312.0 0.8 slice_bitcast_fusion
  313.2 1.0 collective-permute-done
  314.2 1.5 collective-permute-start.1
  315.7 2.7 collective-permute-done.1
  318.4 1.5 collective-permute-start.2
  319.9 2.6 collective-permute-done.2
  322.9 3.8 collective-permute-done.3
  326.7 1.8 collective-permute-start.4
  328.5 3.5 collective-permute-done.4
  332.7 0.7 add_multiply_fusion.1
  333.4 165.5 %reduce-scatter.2.cloned.1.call-done = bf16[336,768]{1,0:T(8,128)(2,1)} async-done(((bf16[10752,768]{1,0:T(8,128)(2,1)}), bf16[336,768]{1,0:T(8,128)(2,1)}) %reduce-scatter.2.cloned.1.call-update) | async-done | bytes 516112 | tf_op jit(solution)/shard_map/reduce_scatter | solution.py:725
  498.9 2.7 fusion
  501.7 1.3 add_multiply_fusion
  (70 shorter events, 4.0 us)
Async XLA Ops:
  7.2 120.6 %all-gather.2.cloned.1.call-start = ((), (), s32[]{:S(2)}) async-start(), calls=%async_computation.1 | async-start | bytes 17031168 | tf_op jit(solution)/shard_map/all_gather | solution.py:711
  9.3 489.6 %reduce-scatter.2.cloned.1.call-start = ((), (), s32[]{:S(2)}) async-start(), calls=%async_computation.2 | async-start | bytes 17031168 | tf_op jit(solution)/shard_map/reduce_scatter | solution.py:725
  10.3 117.5 %copy-start = (s32[1,2,1024]{1,2,0:T(8,128)}, s32[1,2,1024]{1,2,0:T(8,128)S(1)}, u32[]{:S(2)}) copy-start(s32[1,2,1024]{1,2,0:T(8,128)S(1)} %copy.38) | copy-start | bytes 24580
  297.1 4.2 copy-start.5
  297.1 5.2 %slice-start.2 = ((s8[4718592]{0:T(1024)(128)(4,1)}), s8[4194304]{0:T(1024)(128)(4,1)S(1)}, s32[]{:S(2)}) async-start(s8[4718592]{0:T(1024)(128)(4,1)} %bitcast.24), calls=%async_computation.5 | async-start | bytes 8388608
  297.1 5.2 %slice-start.3 = ((s8[4718592]{0:T(1024)(128)(4,1)}), s8[524288]{0:T(1024)(128)(4,1)S(1)}, s32[]{:S(2)}) async-start(s8[4718592]{0:T(1024)(128)(4,1)} %bitcast.24), calls=%async_computation.6 | async-start | bytes 1048576
  301.2 3.6 slice-start
  302.3 2.6 slice-start.1
  304.9 2.5 copy-start.4
  304.9 3.6 copy-start.3
  309.6 0.7 copy-start.12
  309.6 0.9 copy-start.9
  309.6 1.7 copy-start.13
  309.6 22.5 %copy-start.14 = (f32[2,12]{1,0:T(2,128)S(1)}, f32[2,12]{1,0:T(2,128)}, u32[]{:S(2)}) copy-start(f32[2,12]{1,0:T(2,128)} %coef_ref.1) | copy-start | bytes 292
  309.6 22.5 %copy-start.15 = (f32[2,12]{1,0:T(2,128)S(1)}, f32[2,12]{1,0:T(2,128)}, u32[]{:S(2)}) copy-start(f32[2,12]{1,0:T(2,128)} %param.29) | copy-start | bytes 292
  309.6 22.5 %copy-start.16 = (f32[2,12]{1,0:T(2,128)S(1)}, f32[2,12]{1,0:T(2,128)}, u32[]{:S(2)}) copy-start(f32[2,12]{1,0:T(2,128)} %param.28) | copy-start | bytes 292
  309.6 23.1 %copy-start.8 = (f32[12,768]{1,0:T(8,128)S(1)}, f32[12,768]{1,0:T(8,128)}, u32[]{:S(2)}) copy-start(f32[12,768]{1,0:T(8,128)} %vectors_ref.3) | copy-start | bytes 110596
  309.7 23.1 %copy-start.10 = (f32[12,768]{1,0:T(8,128)S(1)}, f32[12,768]{1,0:T(8,128)}, u32[]{:S(2)}) copy-start(f32[12,768]{1,0:T(8,128)} %param.26) | copy-start | bytes 110596
  309.7 23.1 %copy-start.11 = (f32[12,768]{1,0:T(8,128)S(1)}, f32[12,768]{1,0:T(8,128)}, u32[]{:S(2)}) copy-start(f32[12,768]{1,0:T(8,128)} %param.25) | copy-start | bytes 110596
  309.7 189.2 %copy-start.2 = (f32[336,768]{1,0:T(8,128)S(1)}, f32[336,768]{1,0:T(8,128)}, u32[]{:S(2)}) copy-start(f32[336,768]{1,0:T(8,128)} %param.21) | copy-start | bytes 3096580
  309.7 189.2 %copy-start.7 = (f32[336,768]{1,0:T(8,128)S(1)}, f32[336,768]{1,0:T(8,128)}, u32[]{:S(2)}) copy-start(f32[336,768]{1,0:T(8,128)} %param.22) | copy-start | bytes 3096580
  309.7 191.9 %copy-start.6 = (f32[336,768]{1,0:T(8,128)S(1)}, f32[336,768]{1,0:T(8,128)}, u32[]{:S(2)}) copy-start(f32[336,768]{1,0:T(8,128)} %param.23) | copy-start | bytes 3096580
  312.8 1.4 collective-permute-start
  314.2 4.2 collective-permute-start.1
  318.4 4.1 collective-permute-start.2
  322.5 4.1 collective-permute-start.3
  326.7 5.3 %collective-permute-start.4 = (f32[16,768]{1,0:T(8,128)S(1)}, f32[16,768]{1,0:T(8,128)S(1)}, u32[]{:S(2)}, u32[]{:S(2)}) collective-permute-start(f32[16,768]{1,0:T(8,128)S(1)} %add.59), channel_id=1, source_target_pairs={{0,2},{1,3},{2,0},{3,1},{4,6},{5,7},{6,4},{7,5},{8,10},{9,11},{10,... | collective-permute-start | bytes 147464 | tf_op jit(solution)/shard_map/ppermute | solution.py:679
  332.1 170.8 %copy-start.17 = (f32[2,12]{1,0:T(2,128)}, f32[2,12]{1,0:T(2,128)S(1)}, u32[]{:S(2)}) copy-start(f32[2,12]{1,0:T(2,128)S(1)} %reshape_squeeze.3) | copy-start | bytes 292
  501.6 1.3 copy-start.1
Sparse Core Ops, SparseCore 0:
  11.4 116.3 all-gather.1
  309.8 189.0 reduce-scatter.1

commit v2 on v1

--- a/solution.py
+++ b/solution.py
@@ -76,6 +76,7 @@
     grown_ref,
     att_ref,
     inv_ref,
+    exact_ref,
     bucket0_ref,
     bucket1_ref,
     key_ref,
@@ -122,7 +123,9 @@
         both = dot(grown, value_ref[...], NN)
         inv = 1.0 / pltpu.roll(both, HDIM, 1)
         kept = jnp.where(later, att_ref[rows, :].astype(jnp.float32), 0.0)
-        att_ref[rows, :] = jnp.where(mine, both * inv, kept).astype(jnp.bfloat16)
+        exact = both * inv
+        att_ref[rows, :] = jnp.where(mine, exact, kept).astype(jnp.bfloat16)
+        exact_ref[rows, :] = jnp.where(mine, exact, jnp.where(later, exact_ref[rows, :], 0.0))
         inv_ref[rows, :] = jnp.where(mine, inv, jnp.where(later, inv_ref[rows, :], 0.0))
 
     pl.loop(0, slots // TILE, unroll=4)(rows_step)
@@ -155,11 +158,12 @@
             fixed((slots, 2)),
         ],
         out_specs=[lane_block] * 3
-        + [pl.BlockSpec((1, slots, slots), lambda h: (h, 0, 0)), lane_block, lane_block],
+        + [pl.BlockSpec((1, slots, slots), lambda h: (h, 0, 0)), lane_block, lane_block, lane_block],
         out_shape=[wide] * 3
         + [
             jax.ShapeDtypeStruct((HEADS, slots, slots), jnp.bfloat16),
             wide,
+            jax.ShapeDtypeStruct((slots, D), jnp.float32),
             jax.ShapeDtypeStruct((slots, D), jnp.float32),
         ],
         scratch_shapes=[pltpu.VMEM((slots, slots), jnp.float32)] * 2
@@ -234,6 +238,7 @@
     spread_ref,
     dleft_ref,
     dright_ref,
+    pooled_ref,
     total_ref,
 ):
     step = pl.program_id(0)
@@ -288,8 +293,9 @@
         grad_right = (split_dot_left(cot, left, TN) * scale).astype(jnp.bfloat16)
         grad_pooled = dot(grad_left, wl_ref[...], NN) + dot(grad_right, wr_ref[...], NN)
         spread_ref[...] = grad_pooled / counted
-        dleft_ref[...] = dot(grad_left, pooled, TN).astype(jnp.bfloat16)
-        dright_ref[...] = dot(grad_right, pooled, TN).astype(jnp.bfloat16)
+        dleft_ref[...] = grad_left
+        dright_ref[...] = grad_right
+        pooled_ref[...] = pooled
 
 
 def split_dot_left(a, exact, dims):
@@ -327,7 +333,7 @@
             fixed((1, 512)),
             fixed((SEGS, SEGS)),
         ],
-        out_specs=[tile, tile, column, tile, wide, wide, tile, column, fixed((SEGS, SEGS)), fixed((SEGS, D)), fixed((D, D)), fixed((D, D))],
+        out_specs=[tile, tile, column, tile, wide, wide, tile, column, fixed((SEGS, SEGS))] + [fixed((SEGS, D))] * 4,
         out_shape=[
             shape((slots, D), jnp.bfloat16),
             shape((slots, D)),
@@ -339,8 +345,9 @@
             shape((slots, 1)),
             shape((SEGS, SEGS)),
             shape((SEGS, D)),
-            shape((D, D), jnp.bfloat16),
-            shape((D, D), jnp.bfloat16),
+            shape((SEGS, D), jnp.bfloat16),
+            shape((SEGS, D), jnp.bfloat16),
+            shape((SEGS, D), jnp.bfloat16),
         ],
         scratch_shapes=[pltpu.VMEM((SEGS, D), jnp.float32)],
         compiler_params=params(),
@@ -360,32 +367,31 @@
     )
 
 
-def feed_backward_kernel(
+def store_halves(ref, values):
+    ref[0] = values[:, : D // 2].astype(jnp.bfloat16)
+    ref[1] = values[:, D // 2 :].astype(jnp.bfloat16)
+
+
+def second_norm_kernel(
     patches_ref,
     cot_ref,
     segments_ref,
     spread_ref,
     normed2_ref,
     inv2_ref,
-    normed1_ref,
-    inv1_ref,
-    hidden_ref,
-    att_ref,
-    inv_sum_ref,
     vectors_ref,
     act_ref,
     slope_ref,
     wd_ref,
     wu_ref,
-    wo_ref,
-    dwd_ref,
-    dwu_ref,
+    hidden_ref,
+    dleft_ref,
+    dright_ref,
+    pooled_ref,
+    late_ref,
+    sums_ref,
     dbu_ref,
-    sums_ref,
-    dwo_ref,
-    dres_ref,
-    datt_ref,
-    grad_ref,
+    low_ref,
     total_ref,
 ):
     step = pl.program_id(0)
@@ -410,22 +416,71 @@
             low = dres.astype(jnp.bfloat16)
             sums_ref[7:8, :] += jnp.sum(low.astype(jnp.float32), axis=0, keepdims=True)
             total_ref[rows, :] = dres
-            grad_ref[rows, :] = low
+            low_ref[rows, :] = low
 
         pl.loop(0, slots // TILE)(rows_step)
-
-    dwd_ref[...] = dot(act_ref[...], grad_ref[...], TN).astype(jnp.bfloat16)
-    dact = dot(grad_ref[...], wd_ref[...], NT)
-    dpre = (dact * slope_ref[...].astype(jnp.float32)).astype(jnp.bfloat16)
-    dbu_ref[...] = jnp.sum(dpre.astype(jnp.float32), axis=0, keepdims=True)
-    dwu_ref[...] = dot(dpre, hidden_ref[...], TN).astype(jnp.bfloat16)
-    total_ref[...] += dot(dpre, wu_ref[...], NN)
-
-    @pl.when(step == pl.num_programs(0) - 1)
-    def _():
+        dact = dot(low_ref[...], wd_ref[...], NT)
+        dpre = (dact * slope_ref[...].astype(jnp.float32)).astype(jnp.bfloat16)
+        dbu_ref[...] = jnp.sum(dpre.astype(jnp.float32), axis=0, keepdims=True)
+        store_halves(late_ref, dot(dpre, hidden_ref[...], TN))
+        total_ref[...] += dot(dpre, wu_ref[...], NN)
+
+    @pl.when((step > 0) & (step <= FF // D))
+    def _():
+        store_halves(late_ref, dot(act_ref[...], low_ref[...], TN))
+
+    @pl.when(step == FF // D + 1)
+    def _():
+        store_halves(late_ref, dot(dleft_ref[...], pooled_ref[...], TN))
+
+    @pl.when(step == FF // D + 2)
+    def _():
+        store_halves(late_ref, dot(dright_ref[...], pooled_ref[...], TN))
+
+
+def feed_backward_kernel(
+    low_ref,
+    start_ref,
+    normed1_ref,
+    inv1_ref,
+    hidden_ref,
+    att_ref,
+    inv_sum_ref,
+    vectors_ref,
+    slope_ref,
+    wd_ref,
+    wu_ref,
+    wo_ref,
+    early_ref,
+    dbu_ref,
+    sums_ref,
+    dres_ref,
+    datt_ref,
+    grad_ref,
+):
+    step = pl.program_id(0)
+    slots = low_ref.shape[0]
+    last = pl.num_programs(0) - 1
+
+    @pl.when(step == 0)
+    def _():
+        dres_ref[...] = start_ref[...]
+
+    @pl.when(step < last)
+    def _():
+        dact = dot(low_ref[...], wd_ref[...], NT)
+        dpre = (dact * slope_ref[...].astype(jnp.float32)).astype(jnp.bfloat16)
+        dbu_ref[...] = jnp.sum(dpre.astype(jnp.float32), axis=0, keepdims=True)
+        store_halves(early_ref, dot(dpre, hidden_ref[...], TN))
+        dres_ref[...] += dot(dpre, wu_ref[...], NN)
+
+    @pl.when(step == last)
+    def _():
+        sums_ref[...] = jnp.zeros_like(sums_ref)
+
         def rows_step(at):
             rows = tile_rows(at)
-            grad = total_ref[rows, :]
+            grad = dres_ref[rows, :]
             normed = normed1_ref[rows, :]
             sums_ref[0:1, :] += jnp.sum(grad * normed, axis=0, keepdims=True)
             sums_ref[1:2, :] += jnp.sum(grad, axis=0, keepdims=True)
@@ -438,30 +493,31 @@
             datt_ref[rows, :] = (datt * inv_sum_ref[rows, :]).astype(jnp.bfloat16)
 
         pl.loop(0, slots // TILE)(rows_step)
-        dwo_ref[...] = dot(grad_ref[...], att_ref[...], TN).astype(jnp.bfloat16)
-
-
-def feed_backward(patches, cot_out, segments, spread, forward, att, inv_sum, vectors, weights):
-    _, normed1, inv1, hidden, act, slope, normed2, inv2 = forward
+        store_halves(early_ref, dot(grad_ref[...], att_ref[...], TN))
+
+
+def once(shape):
+    return pl.BlockSpec(shape, lambda *_: (0,) * len(shape), pipeline_mode=pl.Buffered(1))
+
+
+def shape_of(dims, dtype=jnp.float32):
+    return jax.ShapeDtypeStruct(dims, dtype)
+
+
+HALF_BLOCK = (2, D, D // 2)
+HALF_ROWS = (3 * D + D + FF + FF + 2 * D) // 2
+
+
+def second_norm(patches, cot_out, segments, spread, forward, pair_factors, vectors, weights):
+    _, _, _, hidden, act, slope, normed2, inv2 = forward
     slots = cot_out.shape[0]
-    chunk = 512
-
-    def once(shape):
-        return pl.BlockSpec(shape, lambda *_: (0,) * len(shape), pipeline_mode=pl.Buffered(1))
-
-    def weight(at):
-        return pl.BlockSpec((chunk, D), lambda i: (at // chunk + i, 0))
-
-    def shape(dims, dtype=jnp.float32):
-        return jax.ShapeDtypeStruct(dims, dtype)
-
-    lane_block = pl.BlockSpec((slots, chunk), lambda i: (0, i))
-    row_block = pl.BlockSpec((chunk, D), lambda i: (i, 0))
+    parts = FF // D
     full = once((slots, D))
     column = once((slots, 1))
+    tail = parts - 1
     return pl.pallas_call(
-        feed_backward_kernel,
-        grid=(FF // chunk,),
+        second_norm_kernel,
+        grid=(parts + 3,),
         in_specs=[
             pl.BlockSpec(memory_space=pltpu.SMEM),
             full,
@@ -469,32 +525,33 @@
             once((SEGS, D)),
             full,
             column,
-            full,
-            column,
-            full,
-            full,
-            full,
             once(vectors.shape),
-            lane_block,
-            lane_block,
-            weight(4 * D + FF),
-            weight(4 * D),
-            pl.BlockSpec((D, D), lambda i: (3, 0), pipeline_mode=pl.Buffered(1)),
-        ],
-        out_specs=[row_block, row_block, pl.BlockSpec((1, chunk), lambda i: (0, i)), fixed((8, D)), fixed((D, D)), full, full],
+            pl.BlockSpec((slots, D), lambda i: (0, jnp.clip(i - 1, 0, parts - 1))),
+            pl.BlockSpec((slots, D), lambda i: (0, tail), pipeline_mode=pl.Buffered(1)),
+            pl.BlockSpec((D, D), lambda i: (4 + parts + tail, 0), pipeline_mode=pl.Buffered(1)),
+            pl.BlockSpec((D, D), lambda i: (4 + tail, 0), pipeline_mode=pl.Buffered(1)),
+            full,
+            once((SEGS, D)),
+            once((SEGS, D)),
+            once((SEGS, D)),
+        ],
+        out_specs=[
+            pl.BlockSpec(HALF_BLOCK, lambda i: (0, i, 0)),
+            fixed((8, D)),
+            fixed((1, D)),
+            full,
+            full,
+        ],
         out_shape=[
-            shape((FF, D), jnp.bfloat16),
-            shape((FF, D), jnp.bfloat16),
-            shape((1, FF)),
-            shape((8, D)),
-            shape((D, D), jnp.bfloat16),
-            shape((slots, D)),
-            shape((slots, D), jnp.bfloat16),
-        ],
-        scratch_shapes=[pltpu.VMEM((slots, D), jnp.bfloat16), pltpu.VMEM((slots, D), jnp.float32)],
+            shape_of((2, HALF_ROWS, D // 2), jnp.bfloat16),
+            shape_of((8, D)),
+            shape_of((1, D)),
+            shape_of((slots, D), jnp.bfloat16),
+            shape_of((slots, D)),
+        ],
         compiler_params=params(),
-        cost_estimate=cost(22e9, 60e6),
-        name="feed_backward",
+        cost_estimate=cost(10e9, 30e6),
+        name="second_norm_backward",
     )(
         patches,
         cot_out,
@@ -502,24 +559,68 @@
         spread,
         normed2,
         inv2,
-        normed1,
-        inv1,
-        hidden,
-        att,
-        inv_sum,
         vectors,
         act,
         slope,
         weights,
         weights,
-        weights,
-    )
+        hidden,
+        *pair_factors,
+    )
+
+
+def feed_backward(low, start, forward, att, inv_sum, vectors, weights):
+    _, normed1, inv1, hidden, _, slope, _, _ = forward
+    slots = low.shape[0]
+    parts = FF // D
+    last = parts - 1
+    full = once((slots, D))
+
+    def at(i):
+        return jnp.minimum(i, last - 1)
+
+    return pl.pallas_call(
+        feed_backward_kernel,
+        grid=(parts,),
+        in_specs=[
+            full,
+            full,
+            full,
+            once((slots, 1)),
+            full,
+            full,
+            full,
+            once(vectors.shape),
+            pl.BlockSpec((slots, D), lambda i: (0, at(i))),
+            pl.BlockSpec((D, D), lambda i: (4 + parts + at(i), 0)),
+            pl.BlockSpec((D, D), lambda i: (4 + at(i), 0)),
+            pl.BlockSpec((D, D), lambda i: (3, 0), pipeline_mode=pl.Buffered(1)),
+        ],
+        out_specs=[
+            pl.BlockSpec(HALF_BLOCK, lambda i: (0, jnp.where(i == last, 3, 4 + i), 0)),
+            pl.BlockSpec((1, D), lambda i: (0, at(i))),
+            fixed((8, D)),
+            full,
+            full,
+        ],
+        out_shape=[
+            shape_of((2, HALF_ROWS, D // 2), jnp.bfloat16),
+            shape_of((1, FF - D)),
+            shape_of((8, D)),
+            shape_of((slots, D)),
+            shape_of((slots, D), jnp.bfloat16),
+        ],
+        scratch_shapes=[pltpu.VMEM((slots, D), jnp.bfloat16)],
+        compiler_params=params(),
+        cost_estimate=cost(17e9, 40e6),
+        name="feed_backward",
+    )(low, start, normed1, inv1, hidden, att, inv_sum, vectors, slope, weights, weights, weights)
 
 
 def attention_backward_kernel(
     grown_ref,
     datt_ref,
-    att_ref,
+    exact_ref,
     v_ref,
     k_ref,
     q_ref,
@@ -561,7 +662,7 @@
     ).astype(jnp.bfloat16)
     grad = datt_ref[...].astype(jnp.float32)
     delta = jnp.sum(
-        jnp.where(mine, grad * att_ref[...].astype(jnp.float32), 0.0), axis=1, keepdims=True
+        jnp.where(mine, grad * exact_ref[...], 0.0), axis=1, keepdims=True
     )
     high = delta.astype(jnp.bfloat16).astype(jnp.float32)
     middle = (delta - high).astype(jnp.bfloat16).astype(jnp.float32)
@@ -586,7 +687,7 @@
     dqkv_ref[2] = dot(dt_ref[head_rows, :], grown_ref[0], NN).astype(jnp.bfloat16)
 
 
-def attention_backward(grown, datt, att, q, k, v, boxes):
+def attention_backward(grown, datt, exact, q, k, v, boxes):
     slots = datt.shape[0]
     lane_block = pl.BlockSpec((slots, GW), lambda h: (0, h // GROUP))
     return pl.pallas_call(
@@ -610,13 +711,15 @@
         compiler_params=params(),
         cost_estimate=cost(15e9, 40e6),
         name="attention_backward",
-    )(grown, datt, att, v, k, q, boxes, boxes.T)
-
-
-def token_backward_kernel(dqkv_ref, weight_ref, tokens_ref, dres_ref, dweight_ref, sums_ref, grad_ref, total_ref):
+    )(grown, datt, exact, v, k, q, boxes, boxes.T)
+
+
+def token_backward_kernel(
+    dqkv_ref, weight_ref, tokens_ref, dres_ref, _, early_ref, sums_ref, grad_ref, total_ref
+):
     step = pl.program_id(0)
     part = dqkv_ref[0]
-    dweight_ref[...] = dot(part, tokens_ref[...], NN).astype(jnp.bfloat16)
+    store_halves(early_ref, dot(part, tokens_ref[...], NN))
     sums_ref[0] = dot(jnp.ones((8, part.shape[1]), jnp.bfloat16), part, NT)
     term = dot(part, weight_ref[...], TN)
 
@@ -633,42 +736,65 @@
         grad_ref[...] = total_ref[...].astype(jnp.bfloat16)
 
 
-def token_backward(dqkv, weights, tokens, dres):
+def token_backward(dqkv, weights, tokens, dres, early):
     slots = tokens.shape[0]
-    block = pl.BlockSpec((D, D), lambda i: (i, 0))
     return pl.pallas_call(
         token_backward_kernel,
         grid=(3,),
-        in_specs=[pl.BlockSpec((1, D, slots), lambda i: (i, 0, 0)), block, fixed((slots, D)), fixed((slots, D))],
-        out_specs=[block, pl.BlockSpec((1, 8, D), lambda i: (i, 0, 0)), fixed((slots, D))],
+        in_specs=[
+            pl.BlockSpec((1, D, slots), lambda i: (i, 0, 0)),
+            pl.BlockSpec((D, D), lambda i: (i, 0)),
+            fixed((slots, D)),
+            fixed((slots, D)),
+            pl.BlockSpec(memory_space=pl.ANY),
+        ],
+        out_specs=[
+            pl.BlockSpec(HALF_BLOCK, lambda i: (0, i, 0)),
+            pl.BlockSpec((1, 8, D), lambda i: (i, 0, 0)),
+            fixed((slots, D)),
+        ],
         out_shape=[
-            jax.ShapeDtypeStruct((3 * D, D), jnp.bfloat16),
-            jax.ShapeDtypeStruct((3, 8, D), jnp.float32),
-            jax.ShapeDtypeStruct((slots, D), jnp.bfloat16),
+            shape_of(early.shape, jnp.bfloat16),
+            shape_of((3, 8, D)),
+            shape_of((slots, D), jnp.bfloat16),
         ],
         scratch_shapes=[pltpu.VMEM((slots, D), jnp.float32)],
+        input_output_aliases={4: 0},
         compiler_params=params(),
         cost_estimate=cost(7.3e9, 20e6),
         name="token_backward",
-    )(dqkv, weights, tokens, dres)
+    )(dqkv, weights, tokens, dres, early)
 
 
 def page_step(tokens, boxes, segments, patches, cot_out, cot_pair, gathered, vectors, box_coef):
-    q, k, v, grown, att, inv_sum = attention_forward(
+    q, k, v, grown, att, inv_sum, exact = attention_forward(
         tokens, gathered, vectors, boxes, patches, box_coef
     )
     found = feed_forward(att, tokens, gathered, vectors, segments, cot_pair)
-    mixed, pair_scores, spread, dwl, dwr = found[0], found[8], found[9], found[10], found[11]
-    dwd, dwu, dbu, sums, dwo, dres, datt = feed_backward(
-        patches, cot_out, segments, spread, found[:8], att, inv_sum, vectors, gathered
-    )
-    dqkv, dcoef = attention_backward(grown, datt, att, q, k, v, boxes)
-    dwqkv, bias_sums, token_grad = token_backward(dqkv, gathered, tokens, dres)
+    mixed, pair_scores, spread = found[0], found[8], found[9]
+    late, sums2, dbu_tail, low, start = second_norm(
+        patches, cot_out, segments, spread, found[:8], found[10:], vectors, gathered
+    )
+    early, dbu_head, sums1, dres, datt = feed_backward(
+        low, start, found[:8], att, inv_sum, vectors, gathered
+    )
+    dqkv, dcoef = attention_backward(grown, datt, exact, q, k, v, boxes)
+    dqkv, late = lax.optimization_barrier((dqkv, scatter_dp(late)))
+    early, bias_sums, token_grad = token_backward(dqkv, gathered, tokens, dres, early)
     vector_part = jnp.concatenate(
-        [sums[:2], bias_sums[0, :1], bias_sums[2, :1], sums[4:8], dbu.reshape(FF // D, D)], axis=0
+        [
+            sums1[:2],
+            bias_sums[0, :1],
+            bias_sums[2, :1],
+            sums1[4:5],
+            sums2[5:8],
+            dbu_head.reshape(FF // D - 1, D),
+            dbu_tail,
+        ],
+        axis=0,
     )
     coef_part = jnp.sum(dcoef, axis=2).T
-    return (mixed, pair_scores, token_grad, (dwqkv, dwo, dwu, dwd, dwl, dwr), vector_part, coef_part)
+    return (mixed, pair_scores, token_grad, early, late, vector_part, coef_part)
 
 
 def exchange_sum(values):
@@ -679,6 +805,37 @@
             values = values + lax.ppermute(values, axis, [(i, i ^ reach) for i in range(size)])
             reach *= 2
     return values
+
+
+def scatter_dp(halves):
+    return lax.psum_scatter(
+        halves.reshape(-1, D // 2), "dp", scatter_dimension=0, tiled=True
+    )
+
+
+def scatter_grid(rows):
+    size = lax.axis_size("grid")
+    place = lax.axis_index("grid")
+    blocks = rows.reshape(size, -1, D // 2)
+
+    def block(at):
+        return lax.dynamic_index_in_dim(blocks, at % size, 0, keepdims=False)
+
+    got = [
+        lax.ppermute(block(place + s), "grid", [(i, (i + s) % size) for i in range(size)])
+        for s in range(1, size)
+    ]
+    return sum((g.astype(jnp.float32) for g in got), block(place).astype(jnp.float32))
+
+
+def swap_halves(first, second):
+    size = lax.axis_size("dp")
+    low = lax.axis_index("dp") < size // 2
+    other = lax.ppermute(
+        jnp.where(low, second, first).astype(jnp.bfloat16), "dp", [(i, (i + size // 2) % size) for i in range(size)]
+    ).astype(jnp.float32)
+    kept = jnp.where(low, first, second)
+    return jnp.concatenate([jnp.where(low, kept, other), jnp.where(low, other, kept)], axis=1)
 
 
 def momentum_step(grad, param, moment, average, rate):
@@ -716,13 +873,15 @@
         for p in range(page_count)
     ]
     mixed, pair_scores, token_grad = (jnp.stack([page[i] for page in pages]) for i in range(3))
-    full_grad = sum(jnp.concatenate(page[3], axis=0) for page in pages)
+    early, late = (sum(page[i] for page in pages) for i in (3, 4))
     small = sum(
-        jnp.concatenate([page[4], jnp.pad(page[5].reshape(1, 2 * HEADS), ((0, 3), (0, D - 2 * HEADS)))], axis=0)
+        jnp.concatenate([page[5], jnp.pad(page[6].reshape(1, 2 * HEADS), ((0, 3), (0, D - 2 * HEADS)))], axis=0)
         for page in pages
     )
+    late_rows = scatter_grid(late)
+    early_rows = scatter_grid(scatter_dp(early))
     small = exchange_sum(small)
-    weight_grad = lax.psum_scatter(full_grad, axes, scatter_dimension=0, tiled=True).astype(jnp.float32)
+    weight_grad = swap_halves(early_rows, late_rows)
     vector_rows = vectors.shape[0]
     vector_grad = small[:vector_rows]
     coef_grad = small[vector_rows, : 2 * HEADS].reshape(2, HEADS)

time: 510 us -> 425 us (0.83)
  waiting for transfers between devices: 291 us -> 192 us
  Pallas kernels: 169 us -> 180 us
  starting transfers between devices: 5.64 us -> 15.1 us
  local copies, waits for them, and re-layouts: 21.1 us -> 11.9 us
    reduce_scatter x1 -> x2, waiting for transfers between devices: 165 us -> 51.2 us  [scatter_dp(): lax.psum_scatter(halves.reshape(-1, D // 2), 'dp', scatter_dimension=0, t...]
    ppermute x0 -> x7, waiting for transfers between devices: none -> 23.4 us  [the longest x6 20.4 us: scatter_grid(): lax.ppermute(block(place + s), 'grid', [(i, (i + s) % size) for i in rang...]
    unnamed x50 -> x31, local copies, waits for them, and re-layouts: 13.2 us -> 1.08 us
    pallas_call x1 -> x2, Pallas kernels: 40.1 us -> 51.7 us  [the longest x1 28.6 us: feed_backward(): pl.pallas_call(feed_backward_kernel, grid=(parts,), in_specs=[full, full,...]
    ppermute x0 -> x7, starting transfers between devices: none -> 11.1 us  [the longest x6 9.69 us: scatter_grid(): lax.ppermute(block(place + s), 'grid', [(i, (i + s) % size) for i in rang...]
    ppermute x5, waiting for transfers between devices: 13.6 us -> 5.67 us  [exchange_sum(): lax.ppermute(values, axis, [(i, i ^ reach) for i in range(size)])]
  transfers between devices with their start and end apart: 7 -> 15, of which waited for: 7 -> 8; matrix products, arithmetic and copies ran while one was open for 2% -> 4% of each run, Pallas kernels for 0% -> 16%
where the time goes in v2:
time: 425 us
  waiting for transfers between devices  192 us (45%)
  Pallas kernels  180 us (42%)
  starting transfers between devices  15.1 us (4%)
  between operations  14.6 us (3%)
  local copies, waits for them, and re-layouts  11.9 us (3%)
  other arithmetic  10.5 us (2%)
    all_gather x1, waiting for transfers between devices, on_device(): lax.all_gather(weights.astype(jnp.bfloat16), axes, axis=0, tiled=True)  112 us
    reduce_scatter x2, waiting for transfers between devices, scatter_dp(): lax.psum_scatter(halves.reshape(-1, D // 2), 'dp', scatter_dimension=0, t...  51.2 us
    pallas_call x1, Pallas kernels, attention_backward(): pl.pallas_call(attention_backward_kernel, grid=(HEADS,), in_specs=[pl.Blo...  41.3 us
    pallas_call x1, Pallas kernels, attention_forward(): pl.pallas_call(attention_forward_kernel, grid=(HEADS,), in_specs=[smem, s...  39.2 us
    pallas_call x1, Pallas kernels, feed_forward(): pl.pallas_call(feed_forward_kernel, grid=(slots // TILE,), in_specs=[tile...  33.3 us
    pallas_call x1, Pallas kernels, feed_backward(): pl.pallas_call(feed_backward_kernel, grid=(parts,), in_specs=[full, full,...  28.6 us
    pallas_call x1, Pallas kernels, second_norm(): pl.pallas_call(second_norm_kernel, grid=(parts + 3,), in_specs=[pl.BlockS...  23.1 us
    ppermute x6, waiting for transfers between devices, scatter_grid(): lax.ppermute(block(place + s), 'grid', [(i, (i + s) % size) for i in rang...  20.4 us
  transfers between devices with their start and end apart: 15, of which 8 were waited for; matrix products, arithmetic and copies ran while one was open for 4% of the time, Pallas kernels for 16%

profile of v2, /device:TPU:0, one launch (start us, length us, event | category | flops | bytes accessed | tf_op | source)
XLA Modules:
  0.0 424.7 jit_solution(17400565936506543015)
XLA Ops:
  7.2 2.1 convert_element_type.44
  11.7 1.3 pad.12.segments_ref
  13.7 1.0 copy.41.segments_ref
  14.7 1.4 fusion.7
  16.1 111.7 %all-gather.2.cloned.1.call-done.wq_ref.wk_ref.wv_ref.wo_ref.wu_ref.wd_ref.wl_ref.wr_ref.weight_ref = bf16[10752,768]{1,0:T(8,128)(2,1)} async-done(((bf16[336,768]{1,0:T(8,128)(2,1)}), bf16[10752,768]{1,0:T(8,128)(2,1)}) %all-gather.2.cloned.1.call-update) | async-done | bytes 16515088 | tf_op jit(solution)/shard_map/all_gather | solution.py:868
  127.8 39.2 %attention_forward.1 = (bf16[1024,768]{1,0:T(8,128)(2,1)}, bf16[1024,768]{1,0:T(8,128)(2,1)}, bf16[1024,768]{1,0:T(8,128)(2,1)}, bf16[12,1024,1024]{2,1,0:T(8,12...) custom-call(f32[2,12]{1,0:T(2,128)} %coef_ref.1, s32[1]{0:T(128)S(6)} %copy.45.patches_ref, ...), custom_call_target="tpu_custom_call" | custom-call | flops 10000000000 | bytes 40000000 | tf_op jit(solution)/shard_map/attention_forward/pallas_call | solution.py:145
  167.0 33.3 %feed_forward.1 = (bf16[1024,768]{1,0:T(8,128)(2,1)}, f32[1024,768]{1,0:T(8,128)}, f32[1024,1]{1,0:T(8,128)}, bf16[1024,768]{1,0:T(8,128)(2,1)}, bf16[1024,3072]...) custom-call(bf16[1024,768]{1,0:T(8,128)(2,1)} %get-tuple-element.53., ...), custom_call_target="tpu_custom_call" | custom-call | flops 11000000512 | bytes 50000000 | tf_op jit(solution)/shard_map/feed_forward/pallas_call | solution.py:321
  200.3 23.1 %second_norm_backward.1 = (bf16[2,5376,384]{2,1,0:T(8,128)(2,1)}, f32[8,768]{1,0:T(8,128)}, f32[1,768]{1,0:T(1,128)}, bf16[1024,768]{1,0:T(8,128)(2,1)}, f32[1024,768]{1,0:T(8,128)}) custom-call(s32[1]{0:T(128)S(6)} %copy.45.patches_ref, bf16[1024,768]{1,0:T(8,128)(2,1)} %bitcast.48, s32[1024,1]{1,0:T(8,128)} %copy.41.segments_ref, ...), custom_call_target="tpu_custom_call" | custom-call | flops 10000000000 | bytes 30000000 | tf_op jit(solution)/shard_map/second_norm_backward/pallas_call | solution.py:518
  223.5 28.6 %feed_backward.1 = (bf16[2,5376,384]{2,1,0:T(8,128)(2,1)}, f32[1,2304]{1,0:T(1,128)}, f32[8,768]{1,0:T(8,128)}, f32[1024,768]{1,0:T(8,128)}, bf16[1024,768]{1,0:T(8,128)(2,1)}) custom-call(bf16[1024,768]{1,0:T(8,128)(2,1)} %get-tuple-element.66.low_ref, f32[1024,768]{1,0:T(8,128)} %get-tuple-element.67.start_ref, f32[1024,768]{1,0:T(8,128)} %get-tuple-element.68.normed1_ref, ...), custom_call_target="tpu_custom_call" | custom-call | flops 16999999488 | bytes 40000000 | tf_op jit(solution)/shard_map/feed_backward/pallas_call | solution.py:582
  252.1 41.3 %attention_backward.1 = (bf16[3,768,1024]{2,1,0:T(8,128)(2,1)}, f32[12,2,1024]{2,1,0:T(2,128)}) custom-call(bf16[12,1024,1024]{2,1,0:T(8,128)(2,1)} %get-tuple-element.56.grown_ref, bf16[1024,768]{1,0:T(8,128)(2,1)} %get-tuple-element.71.datt_ref, f32[1024,768]{1,0:T(8,128)} %get-tuple-element.72.exact_ref, bf16[1024,768]{1,0:T(8,128)(2,1)} %get-tuple-element.73.v_ref, ...), custom_call_target="tpu_custom_call" | custom-call | flops 15000000512 | bytes 40000000 | tf_op jit(solution)/shard_map/attention_backward/pallas_call | solution.py:693
  293.4 15.0 %token_backward.1 = (bf16[2,5376,384]{2,1,0:T(8,128)(2,1)}, f32[3,8,768]{2,1,0:T(8,128)}, bf16[1024,768]{1,0:T(8,128)(2,1)}) custom-call(bf16[3,768,1024]{2,1,0:T(8,128)(2,1)} %get-tuple-element.78.dqkv_ref, ...), custom_call_target="tpu_custom_call", output_to_operand_aliasing={{0}: (4, {})} | custom-call | flops 7299999744 | bytes 20000000 | tf_op jit(solution)/shard_map/token_backward/pallas_call | solution.py:741
  311.5 1.0 collective-permute-done.7
  312.5 1.4 collective-permute-start.8
  314.8 2.4 collective-permute-start.5
  317.2 0.9 collective-permute-start.9
  318.1 3.2 collective-permute-done.9
  321.4 2.4 collective-permute-start.4
  324.3 1.4 collective-permute-done.10
  325.7 1.3 collective-permute-start.11
  327.0 51.2 %reduce-scatter.5.cloned.1.call-done = bf16[1344,384]{1,0:T(8,128)(2,1)} async-done(((bf16[10752,384]{1,0:T(8,128)(2,1)}), bf16[1344,384]{1,0:T(8,128)(2,1)}) %reduce-scatter.5.cloned.1.call-update) | async-done | bytes 1032208 | tf_op jit(solution)/shard_map/reduce_scatter | solution.py:811
  378.2 2.1 dynamic-slice_bitcast_fusion.5
  380.3 3.3 collective-permute-start.2
  383.6 1.1 collective-permute-start
  385.6 5.0 %collective-permute-done.2 = bf16[336,384]{1,0:T(8,128)(2,1)} collective-permute-done((bf16[336,384]{1,0:T(8,128)(2,1)}, bf16[336,384]{1,0:T(8,128)(2,1)}, u32[]{:S(2)}, u32[]{:S(2)}) %collective-permute-start.2) | collective-permute-done | bytes 258080 | tf_op jit(solution)/shard_map/ppermute | solution.py:825
  390.6 15.5 %collective-permute-done.1 = bf16[336,384]{1,0:T(8,128)(2,1)} collective-permute-done((bf16[336,384]{1,0:T(8,128)(2,1)}, bf16[336,384]{1,0:T(8,128)(2,1)}, u32[]{:S(2)}, u32[]{:S(2)}) %collective-permute-start.1) | collective-permute-done | bytes 258080 | tf_op jit(solution)/shard_map/ppermute | solution.py:825
  406.1 1.8 select_convert_fusion
  407.8 1.4 collective-permute-start.6
  409.3 1.3 add_multiply_fusion.2
  410.6 1.5 add_multiply_fusion.1
  412.0 3.0 collective-permute-done.6
  415.1 1.7 fusion.4
  416.8 1.2 add_multiply_fusion
  (70 shorter events, 8.3 us)
Async XLA Ops:
  7.2 120.6 %all-gather.2.cloned.1.call-start = ((), (), s32[]{:S(2)}) async-start(), calls=%async_computation.2 | async-start | bytes 17031168 | tf_op jit(solution)/shard_map/all_gather | solution.py:868
  9.3 284.1 %reduce-scatter.3.cloned.1.call-start = ((), (), s32[]{:S(2)}) async-start(), calls=%async_computation.3 | async-start | bytes 9289728 | tf_op jit(solution)/shard_map/reduce_scatter | solution.py:811
  10.9 116.9 %copy-start = (s32[1,2,1024]{1,2,0:T(8,128)}, s32[1,2,1024]{1,2,0:T(8,128)S(1)}, u32[]{:S(2)}) copy-start(s32[1,2,1024]{1,2,0:T(8,128)S(1)} %copy.39) | copy-start | bytes 24580
  223.4 154.8 %reduce-scatter.5.cloned.1.call-start = ((), (), s32[]{:S(2)}) async-start(), calls=%async_computation.4 | async-start | bytes 9289728 | tf_op jit(solution)/shard_map/reduce_scatter | solution.py:811
  308.4 1.7 copy-start.11
  308.4 1.7 copy-start.10
  308.4 1.7 copy-start.7
  308.4 2.8 copy-start.13
  308.4 5.5 %copy-start.5 = (bf16[1344,384]{1,0:T(8,128)(2,1)S(1)}, bf16[1344,384]{1,0:T(8,128)(2,1)}, u32[]{:S(2)}) copy-start(bf16[1344,384]{1,0:T(8,128)(2,1)} %reduce-scatter.3.cloned.1.call-done) | copy-start | bytes 3096580
  311.2 1.3 collective-permute-start.7
  312.5 4.6 %collective-permute-start.8 = (f32[16,768]{1,0:T(8,128)S(1)}, f32[16,768]{1,0:T(8,128)S(1)}, u32[]{:S(2)}, u32[]{:S(2)}) collective-permute-start(f32[16,768]{1,0:T(8,128)S(1)} %add.139), channel_id=1, source_target_pairs={{0,8},{4,12},{8,0},{12,4},{16,24},{20,28},{24,16},{28,20},{1,9},{5... | collective-permute-start | bytes 147464 | tf_op jit(solution)/shard_map/ppermute | solution.py:805
  314.8 94.5 %copy-start.12 = (f32[2,12]{1,0:T(2,128)S(1)}, f32[2,12]{1,0:T(2,128)}, u32[]{:S(2)}) copy-start(f32[2,12]{1,0:T(2,128)} %coef_ref.1) | copy-start | bytes 292
  314.8 95.8 %copy-start.6 = (f32[12,768]{1,0:T(8,128)S(1)}, f32[12,768]{1,0:T(8,128)}, u32[]{:S(2)}) copy-start(f32[12,768]{1,0:T(8,128)} %vectors_ref.5) | copy-start | bytes 110596
  314.8 95.8 %copy-start.8 = (f32[12,768]{1,0:T(8,128)S(1)}, f32[12,768]{1,0:T(8,128)}, u32[]{:S(2)}) copy-start(f32[12,768]{1,0:T(8,128)} %param.26) | copy-start | bytes 110596
  314.8 68.8 %collective-permute-start.5 = (bf16[336,384]{1,0:T(8,128)(2,1)}, bf16[336,384]{1,0:T(8,128)(2,1)S(1)}, u32[]{:S(2)}, u32[]{:S(2)}) collective-permute-start(bf16[336,384]{1,0:T(8,128)(2,1)} %get-tuple-element.107), channel_id=1, source_target_pairs={{0,3},{1,0},{2,1},{3,2},{4,7},{5,4},{6,5},{7,6},{8,11},{9,8},{10,9... | collective-permute-start | bytes 774152 | tf_op jit(solution)/shard_map/ppermute | solution.py:825
  317.2 4.2 collective-permute-start.9
  321.3 4.4 %collective-permute-start.10 = (f32[16,768]{1,0:T(8,128)S(1)}, f32[16,768]{1,0:T(8,128)S(1)}, u32[]{:S(2)}, u32[]{:S(2)}) collective-permute-start(f32[16,768]{1,0:T(8,128)S(1)} %add.141), channel_id=1, source_target_pairs={{0,1},{1,0},{2,3},{3,2},{4,5},{5,4},{6,7},{7,6},{8,9},{9,8},{10,11... | collective-permute-start | bytes 147464 | tf_op jit(solution)/shard_map/ppermute | solution.py:805
  321.4 64.2 %collective-permute-start.4 = (bf16[336,384]{1,0:T(8,128)(2,1)}, bf16[336,384]{1,0:T(8,128)(2,1)}, u32[]{:S(2)}, u32[]{:S(2)}) collective-permute-start(bf16[336,384]{1,0:T(8,128)(2,1)} %get-tuple-element.108), channel_id=1, source_target_pairs={{0,2},{1,3},{2,0},{3,1},{4,6},{5,7},{6,4},{7,5},{8,10},{9,11},{10,... | collective-permute-start | bytes 774152 | tf_op jit(solution)/shard_map/ppermute | solution.py:825
  323.8 61.9 %collective-permute-start.3 = (bf16[336,384]{1,0:T(8,128)(2,1)}, bf16[336,384]{1,0:T(8,128)(2,1)}, u32[]{:S(2)}, u32[]{:S(2)}) collective-permute-start(bf16[336,384]{1,0:T(8,128)(2,1)} %get-tuple-element.106), channel_id=1, source_target_pairs={{0,1},{1,2},{2,3},{3,0},{4,5},{5,6},{6,7},{7,4},{8,9},{9,10},{10,1... | collective-permute-start | bytes 774152 | tf_op jit(solution)/shard_map/ppermute | solution.py:825
  325.7 57.9 %collective-permute-start.11 = (f32[16,768]{1,0:T(8,128)S(1)}, f32[16,768]{1,0:T(8,128)S(1)}, u32[]{:S(2)}, u32[]{:S(2)}) collective-permute-start(f32[16,768]{1,0:T(8,128)S(1)} %add.142), channel_id=1, source_target_pairs={{0,2},{1,3},{2,0},{3,1},{4,6},{5,7},{6,4},{7,5},{8,10},{9,11},{10,... | collective-permute-start | bytes 147464 | tf_op jit(solution)/shard_map/ppermute | solution.py:805
  380.3 34.8 %copy-start.2 = (f32[336,768]{1,0:T(8,128)S(1)}, f32[336,768]{1,0:T(8,128)}, u32[]{:S(2)}) copy-start(f32[336,768]{1,0:T(8,128)} %param.21) | copy-start | bytes 3096580
  380.3 34.8 %copy-start.3 = (f32[336,768]{1,0:T(8,128)S(1)}, f32[336,768]{1,0:T(8,128)}, u32[]{:S(2)}) copy-start(f32[336,768]{1,0:T(8,128)} %param.22) | copy-start | bytes 3096580
  380.3 10.3 %collective-permute-start.2 = (bf16[336,384]{1,0:T(8,128)(2,1)}, bf16[336,384]{1,0:T(8,128)(2,1)}, u32[]{:S(2)}, u32[]{:S(2)}) collective-permute-start(bf16[336,384]{1,0:T(8,128)(2,1)} %get-tuple-element.110), channel_id=1, source_target_pairs={{0,3},{1,0},{2,1},{3,2},{4,7},{5,4},{6,5},{7,6},{8,11},{9,8},{10,9... | collective-permute-start | bytes 774152 | tf_op jit(solution)/shard_map/ppermute | solution.py:825
  383.6 1.1 copy-start.9
  383.6 22.4 %collective-permute-start.1 = (bf16[336,384]{1,0:T(8,128)(2,1)}, bf16[336,384]{1,0:T(8,128)(2,1)}, u32[]{:S(2)}, u32[]{:S(2)}) collective-permute-start(bf16[336,384]{1,0:T(8,128)(2,1)} %get-tuple-element.111), channel_id=1, source_target_pairs={{0,2},{1,3},{2,0},{3,1},{4,6},{5,7},{6,4},{7,5},{8,10},{9,11},{10,... | collective-permute-start | bytes 774152 | tf_op jit(solution)/shard_map/ppermute | solution.py:825
  383.6 22.4 %collective-permute-start = (bf16[336,384]{1,0:T(8,128)(2,1)}, bf16[336,384]{1,0:T(8,128)(2,1)}, u32[]{:S(2)}, u32[]{:S(2)}) collective-permute-start(bf16[336,384]{1,0:T(8,128)(2,1)} %get-tuple-element.109), channel_id=1, source_target_pairs={{0,1},{1,2},{2,3},{3,0},{4,5},{5,6},{6,7},{7,4},{8,9},{9,10},{10,1... | collective-permute-start | bytes 774152 | tf_op jit(solution)/shard_map/ppermute | solution.py:825
  385.6 31.2 %copy-start.14 = (f32[2,12]{1,0:T(2,128)}, f32[2,12]{1,0:T(2,128)S(1)}, u32[]{:S(2)}) copy-start(f32[2,12]{1,0:T(2,128)S(1)} %reshape_squeeze.3) | copy-start | bytes 292
  407.8 7.1 %collective-permute-start.6 = (bf16[336,384]{1,0:T(8,128)(2,1)S(1)}, bf16[336,384]{1,0:T(8,128)(2,1)S(1)}, u32[]{:S(2)}, u32[]{:S(2)}) collective-permute-start(bf16[336,384]{1,0:T(8,128)(2,1)S(1)} %get-tuple-element.101), channel_id=1, source_target_pairs={{0,16},{4,20},{8,24},{12,28},{16,0},{20,4},{24,8},{28,12},{1,17},{... | collective-permute-start | bytes 774152 | tf_op jit(solution)/shard_map/ppermute | solution.py:834
  415.1 1.7 copy-start.4
  416.8 1.3 copy-start.1
Sparse Core Ops, SparseCore 0:
  11.4 116.3 all-gather.1
  223.5 68.8 reduce-scatter.2
  308.6 69.5 reduce-scatter.4

commit v3 on v2

v3 whole, which is shorter than its diff:
```python
import math

import jax
import jax.numpy as jnp
from jax import lax
from jax.experimental import pallas as pl
from jax.experimental.pallas import tpu as pltpu
from jax.sharding import PartitionSpec as P

D = 768
HEADS = 12
HDIM = 64
FF = 3072
TEXT = 448
SEGS = 64
PAIR = 2 * HDIM
GW = 2 * PAIR
LOG2E = math.log2(math.e)
TILE = 256
WIDE = 512
VMEM_LIMIT = 60 * 1024 * 1024
NT = (((1,), (1,)), ((), ()))
NN = (((1,), (0,)), ((), ()))
TN = (((0,), (0,)), ((), ()))

def dot(a, b, dims):
    return lax.dot_general(a, b, dims, preferred_element_type=jnp.float32)


def split_dot(exact, b, dims):
    high = b.astype(jnp.bfloat16)
    rest = b - high.astype(jnp.float32)
    middle = rest.astype(jnp.bfloat16)
    last = (rest - middle.astype(jnp.float32)).astype(jnp.bfloat16)
    return dot(exact, high, dims) + dot(exact, middle, dims) + dot(exact, last, dims)


def params():
    return pltpu.CompilerParams(vmem_limit_bytes=VMEM_LIMIT)


def cost(flops, nbytes):
    return pl.CostEstimate(flops=int(flops), bytes_accessed=int(nbytes), transcendentals=0)


def tile_rows(step):
    return pl.ds(pl.multiple_of(step * TILE, TILE), TILE)


def wide_rows(step):
    return pl.ds(pl.multiple_of(step * WIDE, WIDE), WIDE)


def fixed(shape):
    return pl.BlockSpec(shape, lambda *_: (0,) * len(shape))


def once(shape):
    return pl.BlockSpec(shape, lambda *_: (0,) * len(shape), pipeline_mode=pl.Buffered(1))


def shape_of(dims, dtype=jnp.float32):
    return jax.ShapeDtypeStruct(dims, dtype)


HALF_BLOCK = (2, D, D // 2)
HALF_ROWS = (3 * D + D + FF + FF + 2 * D) // 2


def square(at):
    return pl.BlockSpec((D, D), lambda i: (at, 0), pipeline_mode=pl.Buffered(1))


def write_buckets(box_row_ref, box_col_ref, bucket_refs, live_row=None):
    def fill(step):
        rows = tile_rows(step)
        for c in range(2):
            spread = jnp.abs(box_col_ref[rows, c : c + 1] - box_row_ref[c : c + 1, :])
            bucket = jnp.minimum(spread >> 5, 31).astype(jnp.float32)
            bucket_refs[c][rows, :] = bucket if live_row is None else jnp.where(live_row, bucket, 0.0)

    pl.loop(0, box_row_ref.shape[1] // TILE)(fill)


def attention_forward_kernel(
    coef_ref,
    patches_ref,
    tokens_ref,
    wq_ref,
    wk_ref,
    wv_ref,
    vectors_ref,
    box_row_ref,
    box_col_ref,
    q_ref,
    k_ref,
    v_ref,
    grown_ref,
    att_ref,
    inv_ref,
    exact_ref,
    bucket0_ref,
    bucket1_ref,
    live_ref,
    value_ref,
    size_ref,
):
    pair = pl.program_id(0)
    slots = tokens_ref.shape[0]
    side = pl.ds(pl.multiple_of(pair % 2 * PAIR, PAIR), PAIR)
    low = jnp.bfloat16

    @pl.when(pair == 0)
    def _():
        write_buckets(box_row_ref, box_col_ref, (bucket0_ref, bucket1_ref))
        slot = lax.broadcasted_iota(jnp.int32, (slots, PAIR), 0)
        live_ref[...] = (slot < TEXT + patches_ref[0]).astype(jnp.float32).astype(low)

    @pl.when(pair % 2 == 0)
    def _():
        query = (dot(tokens_ref[...], wq_ref[...], NT) + vectors_ref[2:3, :]) * (
            LOG2E * HDIM ** (-0.5)
        )
        key = dot(tokens_ref[...], wk_ref[...], NT)
        q_ref[...] = query.astype(low)
        k_ref[...] = key.astype(low)
        v_ref[...] = (dot(tokens_ref[...], wv_ref[...], NT) + vectors_ref[3:4, :]).astype(low)
        of_head = lax.broadcasted_iota(jnp.int32, (GW, PAIR), 0) // HDIM
        ones = (of_head == lax.broadcasted_iota(jnp.int32, (GW, PAIR), 1)).astype(low)
        query_size = jnp.max(dot((query * query).astype(low), ones, NN), axis=0, keepdims=True)
        key_size = jnp.max(dot((key * key).astype(low), ones, NN), axis=0, keepdims=True)
        size_ref[0] = jnp.max(query_size * key_size)

    second = lax.broadcasted_iota(jnp.int32, (1, PAIR), 1) >= HDIM
    masks = [jnp.where(second, 0.0, 1.0), jnp.where(second, 1.0, 0.0)]
    masks = [mask.astype(low) for mask in masks]
    value = v_ref[:, side] * live_ref[...]
    for j in range(2):
        value_ref[j] = value * masks[j] + live_ref[...] * masks[1 - j]
    coefs = [[coef_ref[c, 2 * pair + j] * LOG2E for c in range(2)] for j in range(2)]
    spread = [31.0 * (jnp.abs(c[0]) + jnp.abs(c[1])) for c in coefs]
    room = 57.0 - jnp.maximum(spread[0], spread[1])
    small = (room > 0) & (1.03 * size_ref[0] <= room * room)

    def rows_step(step, shifted):
        rows = tile_rows(step)
        query = q_ref[rows, side]
        bucket0 = bucket0_ref[rows, :]
        bucket1 = bucket1_ref[rows, :]
        found = []
        for j in range(2):
            score = dot(query * masks[j], k_ref[:, side], NT)
            score = score + coefs[j][0] * bucket0 + coefs[j][1] * bucket1
            if shifted:
                slot = lax.broadcasted_iota(jnp.int32, (1, slots), 1)
                score = jnp.where(slot < TEXT + patches_ref[0], score, -1e30)
                score = score - jnp.max(score, axis=1, keepdims=True)
            grown = jnp.exp2(score).astype(low)
            grown_ref[j, rows, :] = grown
            found.append(dot(grown, value_ref[j], NN))
        total = jnp.where(second, found[0], found[1])
        inv = 1.0 / pltpu.roll(total, HDIM, 1)
        exact = jnp.where(second, found[1], found[0]) * inv
        exact_ref[rows, :] = exact
        att_ref[rows, :] = exact.astype(low)
        inv_ref[rows, :] = inv

    @pl.when(small)
    def _():
        pl.loop(0, slots // TILE, unroll=4)(lambda step: rows_step(step, False))

    @pl.when(jnp.logical_not(small))
    def _():
        pl.loop(0, slots // TILE)(lambda step: rows_step(step, True))


def attention_forward(tokens, weights, vectors, boxes, boxes_t, patches, box_coef):
    slots = tokens.shape[0]
    blocks = D // GW
    smem = pl.BlockSpec(memory_space=pltpu.SMEM)
    lane_block = pl.BlockSpec((slots, GW), lambda h: (0, h // 2))
    pair_block = pl.BlockSpec((slots, PAIR), lambda h: (0, h))
    low = shape_of((slots, D), jnp.bfloat16)
    wide = shape_of((slots, D))

    def weight(at):
        return pl.BlockSpec((GW, D), lambda h: (at * blocks + h // 2, 0))

    return pl.pallas_call(
        attention_forward_kernel,
        grid=(HEADS // 2,),
        in_specs=[
            smem,
            smem,
            fixed((slots, D)),
            weight(0),
            weight(1),
            weight(2),
            pl.BlockSpec((vectors.shape[0], GW), lambda h: (0, h // 2)),
            fixed((2, slots)),
            fixed((slots, 2)),
        ],
        out_specs=[lane_block] * 3
        + [pl.BlockSpec((2, slots, slots), lambda h: (h, 0, 0))]
        + [pair_block] * 3,
        out_shape=[low] * 3 + [shape_of((HEADS, slots, slots), jnp.bfloat16), low, wide, wide],
        scratch_shapes=[pltpu.VMEM((slots, slots), jnp.float32)] * 2
        + [
            pltpu.VMEM((slots, PAIR), jnp.bfloat16),
            pltpu.VMEM((2, slots, PAIR), jnp.bfloat16),
            pltpu.SMEM((1,), jnp.float32),
        ],
        compiler_params=params(),
        cost_estimate=cost(10e9, 40e6),
        name="attention_forward",
    )(
        box_coef,
        patches,
        tokens,
        weights,
        weights,
        weights,
        vectors,
        boxes,
        boxes_t,
    )


def normalize(values):
    centered = values - jnp.mean(values, axis=-1, keepdims=True)
    inv_std = lax.rsqrt(jnp.mean(centered * centered, axis=-1, keepdims=True) + 1e-05)
    return (centered * inv_std, inv_std)


def normalize_back(grad_normed, normed, inv_std):
    first_mean = jnp.mean(grad_normed, axis=-1, keepdims=True)
    second_mean = jnp.mean(grad_normed * normed, axis=-1, keepdims=True)
    return inv_std * (grad_normed - first_mean - normed * second_mean)


def gelu_pair(values):
    below = 0.5 + 0.5 * lax.erf(values * (0.5**0.5))
    bell = jnp.exp(values * values * -0.5) * (0.5 / math.pi) ** 0.5
    return (values * below, below + values * bell)


def split_dot_left(a, exact, dims):
    high = a.astype(jnp.bfloat16)
    rest = a - high.astype(jnp.float32)
    middle = rest.astype(jnp.bfloat16)
    last = (rest - middle.astype(jnp.float32)).astype(jnp.bfloat16)
    return dot(high, exact, dims) + dot(middle, exact, dims) + dot(last, exact, dims)


def store_halves(ref, values):
    ref[0] = values[:, : D // 2].astype(jnp.bfloat16)
    ref[1] = values[:, D // 2 :].astype(jnp.bfloat16)


PARTS = FF // D
NORM_STEP = PARTS + 1
TAIL_STEP = PARTS + 2
PAIR_STEP = TAIL_STEP + PARTS + 1


def middle_kernel(
    patches_ref,
    att_ref,
    tokens_ref,
    wo_ref,
    wu_ref,
    wd_ref,
    wl_ref,
    wr_ref,
    vectors_ref,
    segment_row_ref,
    segment_col_ref,
    cot_pair_ref,
    cot_ref,
    slope_ref,
    late_ref,
    pair_ref,
    sums_ref,
    dbu_ref,
    inv1_ref,
    mixed_out,
    normed1_out,
    hidden_out,
    low_out,
    dres_out,
    act_ref,
    tail_ref,
    mixed_ref,
    normed1_ref,
    hidden_ref,
    low_ref,
    total_ref,
    normed2_ref,
    inv2_ref,
    pool_ref,
    pooled_ref,
    dpair_ref,
    sems,
):
    step = pl.program_id(0)
    slots = att_ref.shape[0]
    tiles = slots // TILE
    outs = (
        (normed1_ref, normed1_out),
        (hidden_ref, hidden_out),
        (mixed_ref, mixed_out),
        (low_ref, low_out),
        (total_ref, dres_out),
    )
    sends = [pltpu.make_async_copy(src, dst, sems.at[i]) for i, (src, dst) in enumerate(outs)]

    @pl.when(step == 0)
    def _():

        @pl.loop(0, tiles)
        def _(at):
            rows = tile_rows(at)
            branch = dot(att_ref[rows, :], wo_ref[...], NT) + vectors_ref[4:5, :]
            normed, inv = normalize(tokens_ref[rows, :].astype(jnp.float32) + branch)
            hidden = normed * vectors_ref[0:1, :] + vectors_ref[1:2, :]
            normed1_ref[rows, :] = normed
            inv1_ref[rows, :] = inv
            hidden_ref[rows, :] = hidden.astype(jnp.bfloat16)
            total_ref[rows, :] = hidden + vectors_ref[7:8, :]

        sends[0].start()
        sends[1].start()

    @pl.when((step > 0) & (step <= PARTS))
    def _():
        bias = vectors_ref[pl.ds(7 + step, 1), :]

        for at in range(tiles):
            rows = slice(at * TILE, (at + 1) * TILE)
            act, slope = gelu_pair(dot(hidden_ref[rows, :], wu_ref[...], NT) + bias)
            act = act.astype(jnp.bfloat16)
            act_ref[step - 1, rows, :] = act
            slope_ref[rows, :] = slope.astype(jnp.bfloat16)
            total_ref[rows, :] += dot(act, wd_ref[...], NN)

    @pl.when(step == NORM_STEP)
    def _():
        numbers = lax.broadcasted_iota(jnp.int32, (SEGS, 1), 0)
        slot_row = lax.broadcasted_iota(jnp.int32, (1, slots), 1)
        member = (segment_row_ref[...] == numbers) & (slot_row < TEXT)
        counted = jnp.sum(member.astype(jnp.float32), axis=1, keepdims=True)
        pool_ref[...] = jnp.zeros_like(pool_ref)

        @pl.loop(0, tiles)
        def _(at):
            rows = tile_rows(at)
            normed, inv = normalize(total_ref[rows, :])
            inv2_ref[rows, :] = inv
            output = normed * vectors_ref[5:6, :] + vectors_ref[6:7, :]
            normed2_ref[rows, :] = normed
            mixed_ref[rows, :] = output.astype(jnp.bfloat16)

            @pl.when(at * TILE < TEXT)
            def _():
                slot = at * TILE + lax.broadcasted_iota(jnp.int32, (1, TILE), 1)
                belongs = (segment_row_ref[:, rows] == numbers) & (slot < TEXT)
                pool_ref[...] += split_dot(belongs.astype(jnp.bfloat16), output, NN)

        sends[2].start()
        pooled = (pool_ref[...] / counted).astype(jnp.bfloat16)
        left_weight = wl_ref[...]
        right_weight = wr_ref[...]
        scale = D ** (-0.5)
        left = dot(pooled, left_weight, NT).astype(jnp.bfloat16)
        right = dot(pooled, right_weight, NT).astype(jnp.bfloat16)
        pair_ref[...] = dot(left, right, NT) * scale
        cot = cot_pair_ref[...]
        grad_left = (split_dot_left(cot, right, NN) * scale).astype(jnp.bfloat16)
        grad_right = (split_dot_left(cot, left, TN) * scale).astype(jnp.bfloat16)
        grad_pooled = dot(grad_left, left_weight, NN) + dot(grad_right, right_weight, NN)
        spread = grad_pooled / counted
        pooled_ref[...] = pooled
        dpair_ref[0] = grad_left
        dpair_ref[1] = grad_right
        columns = lax.broadcasted_iota(jnp.int32, (1, SEGS), 1)
        pool_ref[...] = spread
        sums_ref[...] = jnp.zeros_like(sums_ref)

        @pl.loop(0, tiles)
        def _(at):
            rows = tile_rows(at)
            slot = at * TILE + lax.broadcasted_iota(jnp.int32, (TILE, 1), 0)
            live = (slot < TEXT + patches_ref[0]).astype(jnp.float32)
            belongs = (segment_col_ref[rows, :] == columns) & (slot < TEXT)
            grad = cot_ref[rows, :].astype(jnp.float32) * live
            grad = grad + split_dot(belongs.astype(jnp.bfloat16), pool_ref[...], NN)
            normed = normed2_ref[rows, :]
            sums_ref[0:1, :] += jnp.sum(grad * normed, axis=0, keepdims=True)
            sums_ref[1:2, :] += jnp.sum(grad, axis=0, keepdims=True)
            dres = normalize_back(grad * vectors_ref[5:6, :], normed, inv2_ref[rows, :])
            low = dres.astype(jnp.bfloat16)
            sums_ref[2:3, :] += jnp.sum(low.astype(jnp.float32), axis=0, keepdims=True)
            total_ref[rows, :] = dres
            low_ref[rows, :] = low

        sends[3].start()

    @pl.when(step == TAIL_STEP)
    def _():
        dbu_ref[...] = jnp.zeros_like(dbu_ref)

        @pl.loop(0, slots // WIDE)
        def _(at):
            rows = wide_rows(at)
            dact = dot(low_ref[rows, :], wd_ref[...], NT)
            dpre = (dact * slope_ref[rows, :].astype(jnp.float32)).astype(jnp.bfloat16)
            dbu_ref[...] += jnp.sum(dpre.astype(jnp.float32), axis=0, keepdims=True)
            tail_ref[rows, :] = dpre
            total_ref[rows, :] += dot(dpre, wu_ref[...], NN)

        sends[4].start()
        store_halves(late_ref, dot(tail_ref[...], hidden_ref[...], TN))

    @pl.when((step > TAIL_STEP) & (step < PAIR_STEP))
    def _():
        store_halves(late_ref, dot(act_ref[step - TAIL_STEP - 1], low_ref[...], TN))

    @pl.when(step >= PAIR_STEP)
    def _():
        store_halves(late_ref, dot(dpair_ref[step - PAIR_STEP], pooled_ref[...], TN))

    @pl.when(step == PAIR_STEP + 1)
    def _():
        for send in sends:
            send.wait()


def middle(att, tokens, weights, vectors, segments, segments_t, cot_pair, cot_out, patches):
    slots = att.shape[0]
    full = once((slots, D))
    anywhere = pl.BlockSpec(memory_space=pl.ANY)
    low = jnp.bfloat16

    def part(step):
        return jnp.clip(step - 1, 0, PARTS - 1)

    def half_row(step):
        return jnp.clip(step - TAIL_STEP, 0, PARTS + 2)

    return pl.pallas_call(
        middle_kernel,
        grid=(PAIR_STEP + 2,),
        in_specs=[
            pl.BlockSpec(memory_space=pltpu.SMEM),
            full,
            full,
            square(3),
            pl.BlockSpec((D, D), lambda i: (4 + part(i), 0)),
            pl.BlockSpec((D, D), lambda i: (4 + PARTS + part(i), 0)),
            square(4 + 2 * PARTS),
            square(5 + 2 * PARTS),
            once(vectors.shape),
            once((1, slots)),
            once((slots, 1)),
            once((SEGS, SEGS)),
            full,
        ],
        out_specs=[
            pl.BlockSpec((slots, D), lambda i: (0, part(i))),
            pl.BlockSpec(HALF_BLOCK, lambda i: (0, half_row(i), 0)),
            fixed((SEGS, SEGS)),
            fixed((8, D)),
            fixed((1, D)),
            fixed((slots, 1)),
        ]
        + [anywhere] * 5,
        out_shape=[
            shape_of((slots, FF), low),
            shape_of((2, HALF_ROWS, D // 2), low),
            shape_of((SEGS, SEGS)),
            shape_of((8, D)),
            shape_of((1, D)),
            shape_of((slots, 1)),
            shape_of((slots, D), low),
            shape_of((slots, D)),
            shape_of((slots, D), low),
            shape_of((slots, D), low),
            shape_of((slots, D)),
        ],
        scratch_shapes=[
            pltpu.VMEM((PARTS, slots, D), low),
            pltpu.VMEM((slots, D), low),
            pltpu.VMEM((slots, D), low),
            pltpu.VMEM((slots, D), jnp.float32),
            pltpu.VMEM((slots, D), low),
            pltpu.VMEM((slots, D), low),
            pltpu.VMEM((slots, D), jnp.float32),
            pltpu.VMEM((slots, D), jnp.float32),
            pltpu.VMEM((slots, 1), jnp.float32),
            pltpu.VMEM((SEGS, D), jnp.float32),
            pltpu.VMEM((SEGS, D), low),
            pltpu.VMEM((2, SEGS, D), low),
            pltpu.SemaphoreType.DMA((5,)),
        ],
        compiler_params=params(),
        cost_estimate=cost(20e9, 40e6),
        name="middle",
    )(
        patches,
        att,
        tokens,
        *[weights] * 5,
        vectors,
        segments,
        segments_t,
        cot_pair,
        cot_out,
    )


def head_sums(values):
    rows = lax.broadcasted_iota(jnp.int32, (GW, GW), 0)
    cols = lax.broadcasted_iota(jnp.int32, (GW, GW), 1)
    takes = (rows // PAIR == cols // PAIR) & (rows // HDIM != cols // HDIM)
    takes = takes.astype(jnp.float32).astype(jnp.bfloat16)
    sums = jnp.concatenate(
        [split_dot_left(values[:, at : at + GW], takes, NN) for at in range(0, D, GW)], axis=1
    )
    high = sums.astype(jnp.bfloat16).astype(jnp.float32)
    middle = (sums - high).astype(jnp.bfloat16).astype(jnp.float32)
    place = lax.broadcasted_iota(jnp.int32, (1, D), 1) % HDIM
    terms = jnp.where(place == 0, high, jnp.where(place == 1, middle, sums - high - middle))
    return jnp.where(place < 3, terms, 0.0).astype(jnp.bfloat16)


def feed_backward_kernel(
    low_ref,
    hidden_ref,
    inv1_ref,
    vectors_ref,
    slope_ref,
    wd_ref,
    wu_ref,
    wo_ref,
    start_in,
    normed1_in,
    att_in,
    inv_sum_in,
    exact_in,
    early_ref,
    dbu_ref,
    sums_ref,
    dres_out,
    datt_out,
    terms_out,
    total_ref,
    normed1_ref,
    att_ref,
    inv_sum_ref,
    exact_ref,
    grad_ref,
    datt_ref,
    terms_ref,
    sems,
):
    step = pl.program_id(0)
    slots = low_ref.shape[0]
    last = pl.num_programs(0) - 1
    loads = [
        pltpu.make_async_copy(src, dst, sems.at[i])
        for i, (src, dst) in enumerate(
            (
                (start_in, total_ref),
                (normed1_in, normed1_ref),
                (att_in, att_ref),
                (inv_sum_in, inv_sum_ref),
                (exact_in, exact_ref),
            )
        )
    ]

    @pl.when(step == 0)
    def _():
        for load in loads:
            load.start()

    @pl.when(step < last)
    def _():
        dact = dot(low_ref[...], wd_ref[...], NT)
        dpre = (dact * slope_ref[...].astype(jnp.float32)).astype(jnp.bfloat16)
        dbu_ref[...] = jnp.sum(dpre.astype(jnp.float32), axis=0, keepdims=True)
        store_halves(early_ref, dot(dpre, hidden_ref[...], TN))
        pl.when(step == 0)(loads[0].wait)
        total_ref[...] += dot(dpre, wu_ref[...], NN)

    @pl.when(step == last)
    def _():
        sums_ref[...] = jnp.zeros_like(sums_ref)
        for load in loads[1:]:
            load.wait()

        def rows_step(at):
            rows = tile_rows(at)
            grad = total_ref[rows, :]
            normed = normed1_ref[rows, :]
            sums_ref[0:1, :] += jnp.sum(grad * normed, axis=0, keepdims=True)
            sums_ref[1:2, :] += jnp.sum(grad, axis=0, keepdims=True)
            dres = normalize_back(grad * vectors_ref[0:1, :], normed, inv1_ref[rows, :])
            low = dres.astype(jnp.bfloat16)
            sums_ref[4:5, :] += jnp.sum(low.astype(jnp.float32), axis=0, keepdims=True)
            total_ref[rows, :] = dres
            grad_ref[rows, :] = low
            datt = dot(low, wo_ref[...], NN).astype(jnp.bfloat16).astype(jnp.float32)
            datt = (datt * inv_sum_ref[rows, :]).astype(jnp.bfloat16)
            datt_ref[rows, :] = datt
            terms_ref[rows, :] = head_sums(datt.astype(jnp.float32) * exact_ref[rows, :])

        pl.loop(0, slots // TILE)(rows_step)
        sends = [
            pltpu.make_async_copy(src, dst, sems.at[5 + i])
            for i, (src, dst) in enumerate(
                ((total_ref, dres_out), (datt_ref, datt_out), (terms_ref, terms_out))
            )
        ]
        for send in sends:
            send.start()
        store_halves(early_ref, dot(grad_ref[...], att_ref[...], TN))
        for send in sends:
            send.wait()


def feed_backward(low, start, normed1, inv1, hidden, slope, att, inv_sum, exact, vectors, weights):
    slots = low.shape[0]
    last = PARTS - 1
    full = once((slots, D))
    anywhere = pl.BlockSpec(memory_space=pl.ANY)

    def at(i):
        return jnp.minimum(i, last - 1)

    return pl.pallas_call(
        feed_backward_kernel,
        grid=(PARTS,),
        in_specs=[
            full,
            full,
            once((slots, 1)),
            once(vectors.shape),
            pl.BlockSpec((slots, D), lambda i: (0, at(i))),
            pl.BlockSpec((D, D), lambda i: (4 + PARTS + at(i), 0)),
            pl.BlockSpec((D, D), lambda i: (4 + at(i), 0)),
            square(3),
        ]
        + [anywhere] * 5,
        out_specs=[
            pl.BlockSpec(HALF_BLOCK, lambda i: (0, jnp.where(i == last, 3, 4 + i), 0)),
            pl.BlockSpec((1, D), lambda i: (0, at(i))),
            fixed((8, D)),
        ]
        + [anywhere] * 3,
        out_shape=[
            shape_of((2, HALF_ROWS, D // 2), jnp.bfloat16),
            shape_of((1, FF - D)),
            shape_of((8, D)),
            shape_of((slots, D)),
            shape_of((slots, D), jnp.bfloat16),
            shape_of((slots, D), jnp.bfloat16),
        ],
        scratch_shapes=[
            pltpu.VMEM((slots, D), jnp.float32),
            pltpu.VMEM((slots, D), jnp.float32),
            pltpu.VMEM((slots, D), jnp.bfloat16),
            pltpu.VMEM((slots, D), jnp.float32),
            pltpu.VMEM((slots, D), jnp.float32),
            pltpu.VMEM((slots, D), jnp.bfloat16),
            pltpu.VMEM((slots, D), jnp.bfloat16),
            pltpu.VMEM((slots, D), jnp.bfloat16),
            pltpu.SemaphoreType.DMA((8,)),
        ],
        compiler_params=params(),
        cost_estimate=cost(17e9, 40e6),
        name="feed_backward",
    )(low, hidden, inv1, vectors, slope, weights, weights, weights, start, normed1, att, inv_sum, exact)


def attention_backward_kernel(
    patches_ref,
    grown_ref,
    datt_ref,
    terms_ref,
    v_ref,
    k_ref,
    q_ref,
    box_row_ref,
    box_col_ref,
    dqkv_ref,
    dcoef_ref,
    bucket0_ref,
    bucket1_ref,
    dscore_ref,
):
    pair = pl.program_id(0)
    slots = datt_ref.shape[0]
    low = jnp.bfloat16
    live_row = lax.broadcasted_iota(jnp.int32, (1, slots), 1) < TEXT + patches_ref[0]

    @pl.when(pair == 0)
    def _():
        write_buckets(box_row_ref, box_col_ref, (bucket0_ref, bucket1_ref), live_row)

    query_t = q_ref[...].astype(jnp.float32).T.astype(low)
    key_t = (k_ref[...].astype(jnp.float32) * HDIM ** (-0.5)).T
    key_t = jnp.where(live_row, key_t, 0.0).astype(low)
    datt_t = datt_ref[...].astype(jnp.float32).T.astype(low)
    lanes = lax.broadcasted_iota(jnp.int32, (1, PAIR), 1)
    second = lanes >= HDIM
    masks = [jnp.where(second, 0.0, 1.0), jnp.where(second, 1.0, 0.0)]
    masks = [mask.astype(low) for mask in masks]
    dcoef_ref[...] = jnp.zeros_like(dcoef_ref)
    leads = []
    values = []
    for j in range(2):
        at = HDIM * (1 - j)
        minus = jnp.where((lanes >= at) & (lanes < at + 3), -1.0, 0.0).astype(low)
        leads.append(datt_ref[...] * masks[j] + terms_ref[...] * masks[1 - j])
        values.append(v_ref[...] * masks[j] + minus)

    for j in range(2):
        head_rows = slice(j * HDIM, (j + 1) * HDIM)
        for step in range(slots // TILE):
            rows = slice(step * TILE, (step + 1) * TILE)
            diff = dot(leads[j][rows], values[j], NT)
            dscore = grown_ref[j, rows, :].astype(jnp.float32) * diff
            dscore_ref[j, rows, :] = dscore.astype(low)
            dcoef_ref[j, 0:1, :] += jnp.sum(dscore * bucket0_ref[rows, :], axis=0, keepdims=True)
            dcoef_ref[j, 1:2, :] += jnp.sum(dscore * bucket1_ref[rows, :], axis=0, keepdims=True)
        dqkv_ref[0, head_rows] = dot(key_t[head_rows], dscore_ref[j], NT).astype(low)
        dkey = dot(query_t[head_rows], dscore_ref[j], NN) * (1.0 / LOG2E)
        dqkv_ref[1, head_rows] = jnp.where(live_row, dkey, 0.0).astype(low)
        dvalue = dot(datt_t[head_rows], grown_ref[j], NN)
        dqkv_ref[2, head_rows] = jnp.where(live_row, dvalue, 0.0).astype(low)


def attention_backward(grown, datt, terms, q, k, v, boxes, boxes_t, patches):
    slots = datt.shape[0]
    pair_block = pl.BlockSpec((slots, PAIR), lambda h: (0, h))
    return pl.pallas_call(
        attention_backward_kernel,
        grid=(HEADS // 2,),
        in_specs=[
            pl.BlockSpec(memory_space=pltpu.SMEM),
            pl.BlockSpec((2, slots, slots), lambda h: (h, 0, 0)),
        ]
        + [pair_block] * 5
        + [fixed((2, slots)), fixed((slots, 2))],
        out_specs=[
            pl.BlockSpec((3, PAIR, slots), lambda h: (0, h, 0)),
            pl.BlockSpec((2, 2, slots), lambda h: (h, 0, 0)),
        ],
        out_shape=[
            shape_of((3, D, slots), jnp.bfloat16),
            shape_of((HEADS, 2, slots)),
        ],
        scratch_shapes=[pltpu.VMEM((slots, slots), jnp.float32)] * 2
        + [pltpu.VMEM((2, slots, slots), jnp.bfloat16)],
        compiler_params=params(),
        cost_estimate=cost(15e9, 40e6),
        name="attention_backward",
    )(patches, grown, datt, terms, v, k, q, boxes, boxes_t)


def qkv_weights_kernel(dqkv_ref, tokens_ref, _, early_ref, sums_ref):
    part = dqkv_ref[0]
    store_halves(early_ref, dot(part, tokens_ref[...], NN))
    sums_ref[0] = dot(jnp.ones((8, part.shape[1]), jnp.bfloat16), part, NT)


def qkv_weights(dqkv, tokens, early):
    slots = tokens.shape[0]
    return pl.pallas_call(
        qkv_weights_kernel,
        grid=(3,),
        in_specs=[
            pl.BlockSpec((1, D, slots), lambda i: (i, 0, 0)),
            fixed((slots, D)),
            pl.BlockSpec(memory_space=pl.ANY),
        ],
        out_specs=[
            pl.BlockSpec(HALF_BLOCK, lambda i: (0, i, 0)),
            pl.BlockSpec((1, 8, D), lambda i: (i, 0, 0)),
        ],
        out_shape=[shape_of(early.shape, jnp.bfloat16), shape_of((3, 8, D))],
        input_output_aliases={2: 0},
        compiler_params=params(),
        cost_estimate=cost(3.6e9, 10e6),
        name="qkv_weights",
    )(dqkv, tokens, early)


def token_gradient_kernel(dqkv_ref, weight_ref, dres_ref, grad_ref):
    total = dres_ref[...]
    for part in range(3):
        total = total + dot(dqkv_ref[part], weight_ref[part * D : (part + 1) * D, :], TN)
    grad_ref[...] = total.astype(jnp.bfloat16)


def token_gradient(dqkv, weights, dres):
    slots = dres.shape[0]
    tile = pl.BlockSpec((TILE, D), lambda i: (i, 0))
    return pl.pallas_call(
        token_gradient_kernel,
        grid=(slots // TILE,),
        in_specs=[
            pl.BlockSpec((3, D, TILE), lambda i: (0, 0, i)),
            pl.BlockSpec((3 * D, D), lambda i: (0, 0), pipeline_mode=pl.Buffered(1)),
            tile,
        ],
        out_specs=tile,
        out_shape=shape_of((slots, D), jnp.bfloat16),
        compiler_params=params(),
        cost_estimate=cost(3.6e9, 12e6),
        name="token_gradient",
    )(dqkv, weights, dres)


def page_step(
    tokens, boxes, boxes_t, segments, segments_t, patches, cot_out, cot_pair, weights, vectors, box_coef
):
    q, k, v, grown, att, inv_sum, exact = attention_forward(
        tokens, weights, vectors, boxes, boxes_t, patches, box_coef
    )
    slope, late, pair_scores, sums2, dbu_tail, inv1, mixed, normed1, hidden, low, start = middle(
        att, tokens, weights, vectors, segments, segments_t, cot_pair, cot_out, patches
    )
    early, dbu_head, sums1, dres, datt, terms = feed_backward(
        low, start, normed1, inv1, hidden, slope, att, inv_sum, exact, vectors, weights
    )
    dqkv, dcoef = attention_backward(grown, datt, terms, q, k, v, boxes, boxes_t, patches)
    early, bias_sums = qkv_weights(dqkv, tokens, early)
    early, late = lax.optimization_barrier((early, scatter_dp(late)))
    early = scatter_dp(early)
    token_grad = token_gradient(dqkv, weights, dres)
    vector_part = jnp.concatenate(
        [
            sums1[:2],
            bias_sums[0, :1],
            bias_sums[2, :1],
            sums1[4:5],
            sums2[:3],
            dbu_head.reshape(FF // D - 1, D),
            dbu_tail,
        ],
        axis=0,
    )
    coef_part = jnp.sum(dcoef, axis=2).T
    return (mixed, pair_scores, token_grad, early, late, vector_part, coef_part)


def exchange_sum(values):
    for axis in ("dp", "grid"):
        size = lax.axis_size(axis)
        reach = 1
        while reach < size:
            values = values + lax.ppermute(values, axis, [(i, i ^ reach) for i in range(size)])
            reach *= 2
    return values


def scatter_dp(halves):
    return lax.psum_scatter(
        halves.reshape(-1, D // 2), "dp", scatter_dimension=0, tiled=True
    )


def scatter_grid(rows):
    size = lax.axis_size("grid")
    place = lax.axis_index("grid")
    blocks = rows.reshape(size, -1, D // 2)

    def block(at):
        return lax.dynamic_index_in_dim(blocks, at % size, 0, keepdims=False)

    got = [
        lax.ppermute(block(place + s), "grid", [(i, (i + s) % size) for i in range(size)])
        for s in range(1, size)
    ]
    return sum((g.astype(jnp.float32) for g in got), block(place).astype(jnp.float32))


def swap_halves(first, second):
    size = lax.axis_size("dp")
    low = lax.axis_index("dp") < size // 2
    other = lax.ppermute(
        jnp.where(low, second, first).astype(jnp.bfloat16), "dp", [(i, (i + size // 2) % size) for i in range(size)]
    ).astype(jnp.float32)
    kept = jnp.where(low, first, second)
    return jnp.concatenate([jnp.where(low, kept, other), jnp.where(low, other, kept)], axis=1)


def momentum_step(grad, param, moment, average, rate):
    new_moment = 0.5 * moment + grad
    new_param = param - rate * (grad + 0.5 * new_moment)
    new_average = 0.5 * average + 0.5 * new_param
    return (new_moment, new_param, new_average)


def on_device(
    tokens,
    boxes,
    segments,
    patches,
    cot_out,
    cot_pair,
    weights,
    weight_momentum,
    weight_average,
    vectors,
    vector_momentum,
    vector_average,
    box_coef,
    coef_momentum,
    coef_average,
):
    axes = ("dp", "grid")
    page_count, slot_count = tokens.shape[:2]
    device_count = lax.axis_size(axes)
    gathered = lax.all_gather(weights.astype(jnp.bfloat16), axes, axis=0, tiled=True)
    boxes_t = boxes.transpose(0, 2, 1)
    segments = jnp.pad(segments, ((0, 0), (0, slot_count - segments.shape[1])), constant_values=SEGS)
    segments_t = segments.reshape(page_count, slot_count, 1)
    pages = [
        page_step(
            tokens[p],
            boxes[p],
            boxes_t[p],
            segments[p : p + 1],
            segments_t[p],
            patches[p : p + 1],
            cot_out[p],
            cot_pair[p],
            gathered,
            vectors,
            box_coef,
        )
        for p in range(page_count)
    ]
    mixed, pair_scores, token_grad = (jnp.stack([page[i] for page in pages]) for i in range(3))
    early, late = (sum(page[i] for page in pages) for i in (3, 4))
    small = sum(
        jnp.concatenate([page[5], jnp.pad(page[6].reshape(1, 2 * HEADS), ((0, 3), (0, D - 2 * HEADS)))], axis=0)
        for page in pages
    )
    late_rows = scatter_grid(late)
    early_rows = scatter_grid(early)
    small = exchange_sum(small)
    weight_grad = swap_halves(early_rows, late_rows)
    vector_rows = vectors.shape[0]
    vector_grad = small[:vector_rows]
    coef_grad = small[vector_rows, : 2 * HEADS].reshape(2, HEADS)
    rate_scale = (device_count * page_count * slot_count) ** (-0.5)
    new_weight_momentum, new_weights, new_weight_average = momentum_step(
        weight_grad, weights, weight_momentum, weight_average, 0.1 * rate_scale
    )
    new_vector_momentum, new_vectors, new_vector_average = momentum_step(
        vector_grad, vectors, vector_momentum, vector_average, 0.1 * rate_scale
    )
    new_coef_momentum, new_coef, new_coef_average = momentum_step(
        coef_grad, box_coef, coef_momentum, coef_average, 0.01 * rate_scale
    )
    return (
        mixed,
        pair_scores,
        token_grad,
        weight_grad,
        new_weights,
        new_weight_momentum,
        new_weight_average,
        new_weights.astype(jnp.bfloat16),
        vector_grad,
        new_vectors,
        new_vector_momentum,
        new_vector_average,
        coef_grad,
        new_coef,
        new_coef_momentum,
        new_coef_average,
    )


def solution(mesh):
    rows = P(("dp", "grid"))
    return jax.shard_map(
        on_device,
        mesh=mesh,
        in_specs=(rows,) * 9 + (P(),) * 6,
        out_specs=(rows,) * 8 + (P(),) * 8,
        check_vma=False,
    )
```

time: 425 us -> 410 us (0.965)
  Pallas kernels: 180 us -> 170 us
    pallas_call x6, Pallas kernels: 180 us -> 170 us  [the longest x1 46.7 us: attention_forward(): pl.pallas_call(attention_forward_kernel, grid=(HEADS // 2,), in_specs=[sm...]
    ppermute x6, waiting for transfers between devices: 20.4 us -> 10.8 us  [scatter_grid(): lax.ppermute(block(place + s), 'grid', [(i, (i + s) % size) for i in rang...]
    ppermute x5, waiting for transfers between devices: 5.67 us -> 10.5 us  [exchange_sum(): lax.ppermute(values, axis, [(i, i ^ reach) for i in range(size)])]
  transfers between devices with their start and end apart: 15 -> 15, of which waited for: 8 -> 8; matrix products, arithmetic and copies ran while one was open for 4% -> 4% of each run, Pallas kernels for 16% -> 20%
where the time goes in v3:
time: 410 us
  waiting for transfers between devices  192 us (47%)
  Pallas kernels  170 us (41%)
  between operations  14.7 us (4%)
  local copies, waits for them, and re-layouts  11.6 us (3%)
  starting transfers between devices  11.2 us (3%)
  other arithmetic  9.88 us (2%)
    all_gather x1, waiting for transfers between devices, on_device(): lax.all_gather(weights.astype(jnp.bfloat16), axes, axis=0, tiled=True)  114 us
    reduce_scatter x2, waiting for transfers between devices, scatter_dp(): lax.psum_scatter(halves.reshape(-1, D // 2), 'dp', scatter_dimension=0, t...  52.6 us
    pallas_call x1, Pallas kernels, attention_forward(): pl.pallas_call(attention_forward_kernel, grid=(HEADS // 2,), in_specs=[sm...  46.7 us
    pallas_call x1, Pallas kernels, middle(): pl.pallas_call(middle_kernel, grid=(PAIR_STEP + 2,), in_specs=[pl.BlockSp...  43.3 us
    pallas_call x1, Pallas kernels, attention_backward(): pl.pallas_call(attention_backward_kernel, grid=(HEADS // 2,), in_specs=[p...  35.6 us
    pallas_call x1, Pallas kernels, feed_backward(): pl.pallas_call(feed_backward_kernel, grid=(PARTS,), in_specs=[full, full,...  27.5 us
    ppermute x6, waiting for transfers between devices, scatter_grid(): lax.ppermute(block(place + s), 'grid', [(i, (i + s) % size) for i in rang...  10.8 us
    ppermute x5, waiting for transfers between devices, exchange_sum(): lax.ppermute(values, axis, [(i, i ^ reach) for i in range(size)])  10.5 us
  transfers between devices with their start and end apart: 15, of which 8 were waited for; matrix products, arithmetic and copies ran while one was open for 4% of the time, Pallas kernels for 20%

profile of v3, /device:TPU:0, one launch (start us, length us, event | category | flops | bytes accessed | tf_op | source)
XLA Modules:
  0.0 409.8 jit_solution(18138424771349201141)
XLA Ops:
  7.2 2.1 convert_element_type.44
  10.0 1.3 pad_bitcast_fusion
  11.3 1.0 copy.36.segment_col_ref
  12.3 1.7 copy.35
  14.0 113.8 %all-gather.2.cloned.1.call-done.wq_ref.wk_ref.wv_ref.wo_ref.wu_ref.wd_ref.wl_ref.wr_ref.weight_ref = bf16[10752,768]{1,0:T(8,128)(2,1)} async-done(((bf16[336,768]{1,0:T(8,128)(2,1)}), bf16[10752,768]{1,0:T(8,128)(2,1)}) %all-gather.2.cloned.1.call-update) | async-done | bytes 16515088 | tf_op jit(solution)/shard_map/all_gather | solution.py:927
  127.8 46.7 %attention_forward.1 = (bf16[1024,768]{1,0:T(8,128)(2,1)}, bf16[1024,768]{1,0:T(8,128)(2,1)}, bf16[1024,768]{1,0:T(8,128)(2,1)}, bf16[12,1024,1024]{2,1,0:T(8,12...) custom-call(f32[2,12]{1,0:T(2,128)} %coef_ref.1, s32[1]{0:T(128)S(6)} %copy.39.patches_ref, ...), custom_call_target="tpu_custom_call" | custom-call | flops 10000000000 | bytes 40000000 | tf_op jit(solution)/shard_map/attention_forward/pallas_call | solution.py:189
  174.5 43.3 %middle.1 = (bf16[1024,3072]{1,0:T(8,128)(2,1)}, bf16[2,5376,384]{2,1,0:T(8,128)(2,1)}, f32[64,64]{1,0:T(8,128)}, f32[8,768]{1,0:T(8,128)}, f32[1,768]{1,0:T(1,1...) custom-call(s32[1]{0:T(128)S(6)} %copy.39.patches_ref, ...), custom_call_target="tpu_custom_call" | custom-call | flops 20000000000 | bytes 40000000 | tf_op jit(solution)/shard_map/middle/pallas_call | solution.py:450
  217.8 27.5 %feed_backward.1 = (bf16[2,5376,384]{2,1,0:T(8,128)(2,1)}, f32[1,2304]{1,0:T(1,128)}, f32[8,768]{1,0:T(8,128)}, f32[1024,768]{1,0:T(8,128)}, bf16[1024,768]{1,0:T(8,128)(2,1)}, /*index=5*/bf16[1024,768]{1,0:T(8,128)(2,1)}) custom-call(bf16[1024,768]{1,0:T(8,128)(2,1)} %get-tuple-element.50.low_ref, bf16[1024,768]{1,0:T(8,128)(2,1)} %get-tuple-element.51.hidden_ref, ...), custom_call_target="tpu_custom_call" | custom-call | flops 16999999488 | bytes 40000000 | tf_op jit(solution)/shard_map/feed_backward/pallas_call | solution.py:641
  245.3 35.6 %attention_backward.1 = (bf16[3,768,1024]{2,1,0:T(8,128)(2,1)}, f32[12,2,1024]{2,1,0:T(2,128)}) custom-call(s32[1]{0:T(128)S(6)} %copy.39.patches_ref, bf16[12,1024,1024]{2,1,0:T(8,128)(2,1)} %get-tuple-element.49.grown_ref, bf16[1024,768]{1,0:T(8,128)(2,1)} %get-tuple-element.58.datt_ref, bf16[1024,768]{1,0:T(8,128)(2,1)} %get-tuple-element.59.terms_ref, ...), custom_call_target="tpu_custom_call" | custom-call | flops 15000000512 | bytes 40000000 | tf_op jit(solution)/shard_map/attention_backward/pallas_call | solution.py:747
  281.0 8.4 %qkv_weights.1 = (bf16[2,5376,384]{2,1,0:T(8,128)(2,1)}, f32[3,8,768]{2,1,0:T(8,128)}) custom-call(bf16[3,768,1024]{2,1,0:T(8,128)(2,1)} %get-tuple-element.63.dqkv_ref, bf16[1024,768]{1,0:T(8,128)(2,1)} %bitcast.44, bf16[2,5376,384]{2,1,0:T(8,128)(2,1)} %get-tuple-element.65._), custom_call_target="tpu_custom_call", output_to_operand_aliasing={{0}: (2, {})} | custom-call | flops 3600000000 | bytes 10000000 | tf_op jit(solution)/shard_map/qkv_weights/pallas_call | solution.py:780
  292.3 1.2 collective-permute-done.7
  293.5 0.9 dynamic-slice_bitcast_fusion.2
  294.4 1.0 collective-permute-start.3
  295.4 2.2 collective-permute-done.8
  297.6 1.1 collective-permute-start.9
  298.7 3.1 collective-permute-done.9
  301.9 4.1 collective-permute-done.10
  306.8 1.5 collective-permute-start.5
  308.9 52.6 %reduce-scatter.5.cloned.1.call-done = bf16[1344,384]{1,0:T(8,128)(2,1)} async-done(((bf16[10752,384]{1,0:T(8,128)(2,1)}), bf16[1344,384]{1,0:T(8,128)(2,1)}) %reduce-scatter.5.cloned.1.call-update) | async-done | bytes 1032208 | tf_op jit(solution)/shard_map/reduce_scatter | solution.py:870
  361.5 2.1 dynamic-slice_bitcast_fusion.5
  363.6 1.5 collective-permute-start
  365.1 2.3 collective-permute-start.2
  368.0 8.6 %token_gradient.1 = bf16[1024,768]{1,0:T(8,128)(2,1)} custom-call(bf16[3,768,1024]{2,1,0:T(8,128)(2,1)} %get-tuple-element.63.dqkv_ref, bf16[10752,768]{1,0:T(8,128)(2,1)} %all-gather.2.cloned.1.call-done.wq_ref.wk_ref.wv_ref.wo_ref.wu_ref.wd_ref.wl_ref.wr_ref.weight_ref, f32[1024,768]{1,0:T(8,128)} %get-tuple-element.64.dres_ref), custom_call_target="tpu_custom_call" | custom-call | flops 3600000000 | bytes 12000000 | tf_op jit(solution)/shard_map/token_gradient/pallas_call | solution.py:810
  376.6 1.0 add.141
  378.1 1.3 reshape_squeeze.3
  379.4 10.8 %collective-permute-done.1 = bf16[336,384]{1,0:T(8,128)(2,1)} collective-permute-done((bf16[336,384]{1,0:T(8,128)(2,1)}, bf16[336,384]{1,0:T(8,128)(2,1)}, u32[]{:S(2)}, u32[]{:S(2)}) %collective-permute-start.1) | collective-permute-done | bytes 258080 | tf_op jit(solution)/shard_map/ppermute | solution.py:884
  390.2 1.8 select_convert_fusion
  392.0 1.4 collective-permute-start.6
  393.4 1.3 add_multiply_fusion.2
  395.4 4.8 %collective-permute-done.6 = bf16[336,384]{1,0:T(8,128)(2,1)S(1)} collective-permute-done((bf16[336,384]{1,0:T(8,128)(2,1)S(1)}, bf16[336,384]{1,0:T(8,128)(2,1)S(1)}, u32[]{:S(2)}, u32[]{:S(2)}) %collective-permute-start.6) | collective-permute-done | bytes 258080 | tf_op jit(solution)/shard_map/ppermute | solution.py:893
  400.3 1.7 fusion.4
  402.0 1.2 add_multiply_fusion
  (67 shorter events, 6.7 us)
Async XLA Ops:
  7.2 120.6 %all-gather.2.cloned.1.call-start = ((), (), s32[]{:S(2)}) async-start(), calls=%async_computation.2 | async-start | bytes 17031168 | tf_op jit(solution)/shard_map/all_gather | solution.py:927
  9.3 280.0 %reduce-scatter.3.cloned.1.call-start = ((), (), s32[]{:S(2)}) async-start(), calls=%async_computation.3 | async-start | bytes 9289728 | tf_op jit(solution)/shard_map/reduce_scatter | solution.py:870
  217.8 143.7 %reduce-scatter.5.cloned.1.call-start = ((), (), s32[]{:S(2)}) async-start(), calls=%async_computation.4 | async-start | bytes 9289728 | tf_op jit(solution)/shard_map/reduce_scatter | solution.py:870
  289.3 1.6 copy-start.11
  289.3 1.7 copy-start.6
  289.3 1.9 copy-start.10
  289.3 2.7 copy-start.13
  289.4 4.2 %copy-start.4 = (bf16[1344,384]{1,0:T(8,128)(2,1)S(1)}, bf16[1344,384]{1,0:T(8,128)(2,1)}, u32[]{:S(2)}) copy-start(bf16[1344,384]{1,0:T(8,128)(2,1)} %reduce-scatter.3.cloned.1.call-done) | copy-start | bytes 3096580
  292.2 1.3 collective-permute-start.7
  293.5 4.2 %collective-permute-start.8 = (f32[16,768]{1,0:T(8,128)S(1)}, f32[16,768]{1,0:T(8,128)S(1)}, u32[]{:S(2)}, u32[]{:S(2)}) collective-permute-start(f32[16,768]{1,0:T(8,128)S(1)} %add.137), channel_id=1, source_target_pairs={{0,8},{4,12},{8,0},{12,4},{16,24},{20,28},{24,16},{28,20},{1,9},{5... | collective-permute-start | bytes 147464 | tf_op jit(solution)/shard_map/ppermute | solution.py:864
  294.4 73.0 %collective-permute-start.3 = (bf16[336,384]{1,0:T(8,128)(2,1)S(1)}, bf16[336,384]{1,0:T(8,128)(2,1)S(1)}, u32[]{:S(2)}, u32[]{:S(2)}) collective-permute-start(bf16[336,384]{1,0:T(8,128)(2,1)S(1)} %get-tuple-element.92), channel_id=1, source_target_pairs={{0,1},{1,2},{2,3},{3,0},{4,5},{5,6},{6,7},{7,4},{8,9},{9,10},{10,1... | collective-permute-start | bytes 774152 | tf_op jit(solution)/shard_map/ppermute | solution.py:884
  297.6 4.2 %collective-permute-start.9 = (f32[16,768]{1,0:T(8,128)S(1)}, f32[16,768]{1,0:T(8,128)S(1)}, u32[]{:S(2)}, u32[]{:S(2)}) collective-permute-start(f32[16,768]{1,0:T(8,128)S(1)} %add.138), channel_id=1, source_target_pairs={{0,16},{4,20},{8,24},{12,28},{16,0},{20,4},{24,8},{28,12},{1,17},{... | collective-permute-start | bytes 147464 | tf_op jit(solution)/shard_map/ppermute | solution.py:864
  301.8 4.2 %collective-permute-start.10 = (f32[16,768]{1,0:T(8,128)S(1)}, f32[16,768]{1,0:T(8,128)S(1)}, u32[]{:S(2)}, u32[]{:S(2)}) collective-permute-start(f32[16,768]{1,0:T(8,128)S(1)} %add.139), channel_id=1, source_target_pairs={{0,1},{1,0},{2,3},{3,2},{4,5},{5,4},{6,7},{7,6},{8,9},{9,8},{10,11... | collective-permute-start | bytes 147464 | tf_op jit(solution)/shard_map/ppermute | solution.py:864
  305.9 59.1 %collective-permute-start.11 = (f32[16,768]{1,0:T(8,128)S(1)}, f32[16,768]{1,0:T(8,128)S(1)}, u32[]{:S(2)}, u32[]{:S(2)}) collective-permute-start(f32[16,768]{1,0:T(8,128)S(1)} %add.140), channel_id=1, source_target_pairs={{0,2},{1,3},{2,0},{3,1},{4,6},{5,7},{6,4},{7,5},{8,10},{9,11},{10,... | collective-permute-start | bytes 147464 | tf_op jit(solution)/shard_map/ppermute | solution.py:864
  306.8 72.6 %collective-permute-start.5 = (bf16[336,384]{1,0:T(8,128)(2,1)}, bf16[336,384]{1,0:T(8,128)(2,1)}, u32[]{:S(2)}, u32[]{:S(2)}) collective-permute-start(bf16[336,384]{1,0:T(8,128)(2,1)} %get-tuple-element.93), channel_id=1, source_target_pairs={{0,3},{1,0},{2,1},{3,2},{4,7},{5,4},{6,5},{7,6},{8,11},{9,8},{10,9... | collective-permute-start | bytes 774152 | tf_op jit(solution)/shard_map/ppermute | solution.py:884
  308.4 71.0 %collective-permute-start.4 = (bf16[336,384]{1,0:T(8,128)(2,1)}, bf16[336,384]{1,0:T(8,128)(2,1)}, u32[]{:S(2)}, u32[]{:S(2)}) collective-permute-start(bf16[336,384]{1,0:T(8,128)(2,1)} %get-tuple-element.94), channel_id=1, source_target_pairs={{0,2},{1,3},{2,0},{3,1},{4,6},{5,7},{6,4},{7,5},{8,10},{9,11},{10,... | collective-permute-start | bytes 774152 | tf_op jit(solution)/shard_map/ppermute | solution.py:884
  363.6 15.8 %collective-permute-start = (bf16[336,384]{1,0:T(8,128)(2,1)}, bf16[336,384]{1,0:T(8,128)(2,1)}, u32[]{:S(2)}, u32[]{:S(2)}) collective-permute-start(bf16[336,384]{1,0:T(8,128)(2,1)} %get-tuple-element.95), channel_id=1, source_target_pairs={{0,1},{1,2},{2,3},{3,0},{4,5},{5,6},{6,7},{7,4},{8,9},{9,10},{10,1... | collective-permute-start | bytes 774152 | tf_op jit(solution)/shard_map/ppermute | solution.py:884
  365.1 2.9 copy-start.9
  365.1 14.4 %collective-permute-start.2 = (bf16[336,384]{1,0:T(8,128)(2,1)}, bf16[336,384]{1,0:T(8,128)(2,1)}, u32[]{:S(2)}, u32[]{:S(2)}) collective-permute-start(bf16[336,384]{1,0:T(8,128)(2,1)} %get-tuple-element.96), channel_id=1, source_target_pairs={{0,3},{1,0},{2,1},{3,2},{4,7},{5,4},{6,5},{7,6},{8,11},{9,8},{10,9... | collective-permute-start | bytes 774152 | tf_op jit(solution)/shard_map/ppermute | solution.py:884
  367.4 22.8 %collective-permute-start.1 = (bf16[336,384]{1,0:T(8,128)(2,1)}, bf16[336,384]{1,0:T(8,128)(2,1)}, u32[]{:S(2)}, u32[]{:S(2)}) collective-permute-start(bf16[336,384]{1,0:T(8,128)(2,1)} %get-tuple-element.97), channel_id=1, source_target_pairs={{0,2},{1,3},{2,0},{3,1},{4,6},{5,7},{6,4},{7,5},{8,10},{9,11},{10,... | collective-permute-start | bytes 774152 | tf_op jit(solution)/shard_map/ppermute | solution.py:884
  376.6 16.9 %copy-start.12 = (f32[2,12]{1,0:T(2,128)S(1)}, f32[2,12]{1,0:T(2,128)}, u32[]{:S(2)}) copy-start(f32[2,12]{1,0:T(2,128)} %coef_ref.1) | copy-start | bytes 292
  376.6 18.1 %copy-start.5 = (f32[12,768]{1,0:T(8,128)S(1)}, f32[12,768]{1,0:T(8,128)}, u32[]{:S(2)}) copy-start(f32[12,768]{1,0:T(8,128)} %vectors_ref.5) | copy-start | bytes 110596
  376.6 18.1 %copy-start.7 = (f32[12,768]{1,0:T(8,128)S(1)}, f32[12,768]{1,0:T(8,128)}, u32[]{:S(2)}) copy-start(f32[12,768]{1,0:T(8,128)} %param.26) | copy-start | bytes 110596
  376.6 23.7 %copy-start.1 = (f32[336,768]{1,0:T(8,128)S(1)}, f32[336,768]{1,0:T(8,128)}, u32[]{:S(2)}) copy-start(f32[336,768]{1,0:T(8,128)} %param.21) | copy-start | bytes 3096580
  376.6 23.7 %copy-start.2 = (f32[336,768]{1,0:T(8,128)S(1)}, f32[336,768]{1,0:T(8,128)}, u32[]{:S(2)}) copy-start(f32[336,768]{1,0:T(8,128)} %param.22) | copy-start | bytes 3096580
  377.6 17.1 %copy-start.8 = (f32[12,768]{1,0:T(8,128)S(1)}, f32[12,768]{1,0:T(8,128)}, u32[]{:S(2)}) copy-start(f32[12,768]{1,0:T(8,128)} %param.25) | copy-start | bytes 110596
  379.4 14.0 %copy-start.14 = (f32[2,12]{1,0:T(2,128)S(1)}, f32[2,12]{1,0:T(2,128)}, u32[]{:S(2)}) copy-start(f32[2,12]{1,0:T(2,128)} %reshape_squeeze.3) | copy-start | bytes 292
  392.0 8.2 %collective-permute-start.6 = (bf16[336,384]{1,0:T(8,128)(2,1)S(1)}, bf16[336,384]{1,0:T(8,128)(2,1)S(1)}, u32[]{:S(2)}, u32[]{:S(2)}) collective-permute-start(bf16[336,384]{1,0:T(8,128)(2,1)S(1)} %get-tuple-element.87), channel_id=1, source_target_pairs={{0,16},{4,20},{8,24},{12,28},{16,0},{20,4},{24,8},{28,12},{1,17},{... | collective-permute-start | bytes 774152 | tf_op jit(solution)/shard_map/ppermute | solution.py:893
  400.3 1.7 copy-start.3
  402.0 1.3 copy-start
Sparse Core Ops, SparseCore 0:
  11.4 116.3 all-gather.1
  217.9 68.7 reduce-scatter.2
  290.8 70.6 reduce-scatter.4

commit v4 on v3

--- a/solution.py
+++ b/solution.py
@@ -1,3 +1,4 @@
+import functools
 import math
 
 import jax
@@ -72,6 +73,8 @@
 
 
 def write_buckets(box_row_ref, box_col_ref, bucket_refs, live_row=None):
+    box_col_ref[...] = jnp.tile(box_row_ref[...].astype(jnp.float32), (4, 1)).T.astype(jnp.int32)
+
     def fill(step):
         rows = tile_rows(step)
         for c in range(2):
@@ -82,49 +85,110 @@
     pl.loop(0, box_row_ref.shape[1] // TILE)(fill)
 
 
+def place_weights(layout, piece_refs, weight_ref, out_ref, sems, meanwhile):
+    step = pl.program_id(0)
+    place = lax.axis_index("grid")
+    mine = lax.axis_index("dp")
+    depth = lax.axis_size("grid")
+    shard = weight_ref.shape[0] // (lax.axis_size("dp") * depth)
+    by_owner = {}
+    count = 0
+    for ref, (start, entries) in zip(piece_refs, layout):
+        rows = ref.shape[1]
+        if entries is None:
+            every = [(owner, "far") for owner in range(ref.shape[0])]
+        else:
+            every = [
+                ((mine ^ over) * depth + lax.rem(place + depth - back, depth), over)
+                for over, back in entries
+            ]
+        for at, (owner, over) in enumerate(every):
+            if over == "far" and owner * shard < 3 * D:
+                over = "near"
+            target = weight_ref.at[pl.ds(pl.multiple_of(owner * shard + start, 16), rows)]
+            by_owner.setdefault(over, []).append(pltpu.make_async_copy(ref.at[at], target, sems.at[count]))
+            count += 1
+    out = pltpu.make_async_copy(weight_ref, out_ref, sems.at[count])
+    needed = -(-3 * D // (shard * depth))
+
+    def each(first, action):
+        for over, copies in by_owner.items():
+            if over in ("near", "far"):
+                if first == (over == "near"):
+                    for copy in copies:
+                        action(copy)
+                continue
+            chosen = (mine ^ over) < needed
+
+            @pl.when(chosen if first else jnp.logical_not(chosen))
+            def _():
+                for copy in copies:
+                    action(copy)
+
+    @pl.when(step == 0)
+    def _():
+        each(True, lambda copy: copy.start())
+        meanwhile()
+        each(True, lambda copy: copy.wait())
+        each(False, lambda copy: copy.start())
+
+    @pl.when(step == 1)
+    def _():
+        each(False, lambda copy: copy.wait())
+        out.start()
+
+    @pl.when(step == pl.num_programs(0) - 1)
+    def _():
+        out.wait()
+
+
 def attention_forward_kernel(
+    layout,
+    pieces,
     coef_ref,
     patches_ref,
     tokens_ref,
-    wq_ref,
-    wk_ref,
-    wv_ref,
     vectors_ref,
     box_row_ref,
-    box_col_ref,
-    q_ref,
-    k_ref,
-    v_ref,
-    grown_ref,
-    att_ref,
-    inv_ref,
-    exact_ref,
-    bucket0_ref,
-    bucket1_ref,
-    live_ref,
-    value_ref,
-    size_ref,
+    *refs,
 ):
+    piece_refs, refs = refs[:pieces], refs[pieces:]
+    q_ref, k_ref, v_ref, grown_ref, att_ref, inv_ref, exact_ref = refs[:7]
+    box_col_ref, bucket0_ref, bucket1_ref, live_ref, value_ref, size_ref, weight_ref, sems = refs[-8:]
     pair = pl.program_id(0)
     slots = tokens_ref.shape[0]
     side = pl.ds(pl.multiple_of(pair % 2 * PAIR, PAIR), PAIR)
     low = jnp.bfloat16
 
-    @pl.when(pair == 0)
-    def _():
+    def prepare():
         write_buckets(box_row_ref, box_col_ref, (bucket0_ref, bucket1_ref))
         slot = lax.broadcasted_iota(jnp.int32, (slots, PAIR), 0)
         live_ref[...] = (slot < TEXT + patches_ref[0]).astype(jnp.float32).astype(low)
 
+    if layout is None:
+
+        @pl.when(pair == 0)
+        def _():
+            load = pltpu.make_async_copy(piece_refs[0].at[pl.ds(0, 3 * D)], weight_ref, sems.at[0])
+            load.start()
+            prepare()
+            load.wait()
+
+    else:
+        place_weights(layout, piece_refs, weight_ref, refs[7], sems, prepare)
+
     @pl.when(pair % 2 == 0)
     def _():
-        query = (dot(tokens_ref[...], wq_ref[...], NT) + vectors_ref[2:3, :]) * (
+        def weight(at):
+            return weight_ref[pl.ds(pl.multiple_of(at * D + pair // 2 * GW, GW), GW), :]
+
+        query = (dot(tokens_ref[...], weight(0), NT) + vectors_ref[2:3, :]) * (
             LOG2E * HDIM ** (-0.5)
         )
-        key = dot(tokens_ref[...], wk_ref[...], NT)
+        key = dot(tokens_ref[...], weight(1), NT)
         q_ref[...] = query.astype(low)
         k_ref[...] = key.astype(low)
-        v_ref[...] = (dot(tokens_ref[...], wv_ref[...], NT) + vectors_ref[3:4, :]).astype(low)
+        v_ref[...] = (dot(tokens_ref[...], weight(2), NT) + vectors_ref[3:4, :]).astype(low)
         of_head = lax.broadcasted_iota(jnp.int32, (GW, PAIR), 0) // HDIM
         ones = (of_head == lax.broadcasted_iota(jnp.int32, (GW, PAIR), 1)).astype(low)
         query_size = jnp.max(dot((query * query).astype(low), ones, NN), axis=0, keepdims=True)
@@ -174,56 +238,50 @@
         pl.loop(0, slots // TILE)(lambda step: rows_step(step, True))
 
 
-def attention_forward(tokens, weights, vectors, boxes, boxes_t, patches, box_coef):
+def attention_forward(tokens, pieces, layout, vectors, boxes, patches, box_coef):
     slots = tokens.shape[0]
-    blocks = D // GW
     smem = pl.BlockSpec(memory_space=pltpu.SMEM)
+    anywhere = pl.BlockSpec(memory_space=pl.ANY)
     lane_block = pl.BlockSpec((slots, GW), lambda h: (0, h // 2))
     pair_block = pl.BlockSpec((slots, PAIR), lambda h: (0, h))
     low = shape_of((slots, D), jnp.bfloat16)
     wide = shape_of((slots, D))
-
-    def weight(at):
-        return pl.BlockSpec((GW, D), lambda h: (at * blocks + h // 2, 0))
-
-    return pl.pallas_call(
-        attention_forward_kernel,
+    weights = shape_of((2 * HALF_ROWS, D), jnp.bfloat16)
+    copies = 0 if layout is None else sum(
+        piece.shape[0] if entries is None else len(entries) for piece, (_, entries) in zip(pieces, layout)
+    )
+    out = pl.pallas_call(
+        functools.partial(attention_forward_kernel, layout, len(pieces)),
         grid=(HEADS // 2,),
         in_specs=[
             smem,
             smem,
             fixed((slots, D)),
-            weight(0),
-            weight(1),
-            weight(2),
             pl.BlockSpec((vectors.shape[0], GW), lambda h: (0, h // 2)),
             fixed((2, slots)),
-            fixed((slots, 2)),
-        ],
+        ]
+        + [anywhere] * len(pieces),
         out_specs=[lane_block] * 3
         + [pl.BlockSpec((2, slots, slots), lambda h: (h, 0, 0))]
-        + [pair_block] * 3,
-        out_shape=[low] * 3 + [shape_of((HEADS, slots, slots), jnp.bfloat16), low, wide, wide],
-        scratch_shapes=[pltpu.VMEM((slots, slots), jnp.float32)] * 2
+        + [pair_block] * 3
+        + [anywhere] * bool(copies),
+        out_shape=[low] * 3
+        + [shape_of((HEADS, slots, slots), jnp.bfloat16), low, wide, wide]
+        + [weights] * bool(copies),
+        scratch_shapes=[pltpu.VMEM((slots, 8), jnp.int32)]
+        + [pltpu.VMEM((slots, slots), jnp.float32)] * 2
         + [
             pltpu.VMEM((slots, PAIR), jnp.bfloat16),
             pltpu.VMEM((2, slots, PAIR), jnp.bfloat16),
             pltpu.SMEM((1,), jnp.float32),
+            pltpu.VMEM(weights.shape if copies else (3 * D, D), jnp.bfloat16),
+            pltpu.SemaphoreType.DMA((copies + 1,)),
         ],
         compiler_params=params(),
         cost_estimate=cost(10e9, 40e6),
         name="attention_forward",
-    )(
-        box_coef,
-        patches,
-        tokens,
-        weights,
-        weights,
-        weights,
-        vectors,
-        boxes,
-        boxes_t,
-    )
+    )(box_coef, patches, tokens, vectors, boxes, *pieces)
+    return out[:7], out[7] if copies else pieces[0]
 
 
 def normalize(values):
@@ -274,7 +332,6 @@
     wr_ref,
     vectors_ref,
     segment_row_ref,
-    segment_col_ref,
     cot_pair_ref,
     cot_ref,
     slope_ref,
@@ -382,7 +439,6 @@
         pooled_ref[...] = pooled
         dpair_ref[0] = grad_left
         dpair_ref[1] = grad_right
-        columns = lax.broadcasted_iota(jnp.int32, (1, SEGS), 1)
         pool_ref[...] = spread
         sums_ref[...] = jnp.zeros_like(sums_ref)
 
@@ -391,9 +447,10 @@
             rows = tile_rows(at)
             slot = at * TILE + lax.broadcasted_iota(jnp.int32, (TILE, 1), 0)
             live = (slot < TEXT + patches_ref[0]).astype(jnp.float32)
-            belongs = (segment_col_ref[rows, :] == columns) & (slot < TEXT)
+            slot_of = at * TILE + lax.broadcasted_iota(jnp.int32, (1, TILE), 1)
+            belongs = (segment_row_ref[:, rows] == numbers) & (slot_of < TEXT)
             grad = cot_ref[rows, :].astype(jnp.float32) * live
-            grad = grad + split_dot(belongs.astype(jnp.bfloat16), pool_ref[...], NN)
+            grad = grad + split_dot(belongs.astype(jnp.bfloat16), pool_ref[...], TN)
             normed = normed2_ref[rows, :]
             sums_ref[0:1, :] += jnp.sum(grad * normed, axis=0, keepdims=True)
             sums_ref[1:2, :] += jnp.sum(grad, axis=0, keepdims=True)
@@ -435,7 +492,7 @@
             send.wait()
 
 
-def middle(att, tokens, weights, vectors, segments, segments_t, cot_pair, cot_out, patches):
+def middle(att, tokens, weights, vectors, segments, cot_pair, cot_out, patches):
     slots = att.shape[0]
     full = once((slots, D))
     anywhere = pl.BlockSpec(memory_space=pl.ANY)
@@ -461,7 +518,6 @@
             square(5 + 2 * PARTS),
             once(vectors.shape),
             once((1, slots)),
-            once((slots, 1)),
             once((SEGS, SEGS)),
             full,
         ],
@@ -512,7 +568,6 @@
         *[weights] * 5,
         vectors,
         segments,
-        segments_t,
         cot_pair,
         cot_out,
     )
@@ -692,9 +747,9 @@
     k_ref,
     q_ref,
     box_row_ref,
-    box_col_ref,
     dqkv_ref,
     dcoef_ref,
+    box_col_ref,
     bucket0_ref,
     bucket1_ref,
     dscore_ref,
@@ -741,7 +796,7 @@
         dqkv_ref[2, head_rows] = jnp.where(live_row, dvalue, 0.0).astype(low)
 
 
-def attention_backward(grown, datt, terms, q, k, v, boxes, boxes_t, patches):
+def attention_backward(grown, datt, terms, q, k, v, boxes, patches):
     slots = datt.shape[0]
     pair_block = pl.BlockSpec((slots, PAIR), lambda h: (0, h))
     return pl.pallas_call(
@@ -752,7 +807,7 @@
             pl.BlockSpec((2, slots, slots), lambda h: (h, 0, 0)),
         ]
         + [pair_block] * 5
-        + [fixed((2, slots)), fixed((slots, 2))],
+        + [fixed((2, slots))],
         out_specs=[
             pl.BlockSpec((3, PAIR, slots), lambda h: (0, h, 0)),
             pl.BlockSpec((2, 2, slots), lambda h: (h, 0, 0)),
@@ -761,12 +816,13 @@
             shape_of((3, D, slots), jnp.bfloat16),
             shape_of((HEADS, 2, slots)),
         ],
-        scratch_shapes=[pltpu.VMEM((slots, slots), jnp.float32)] * 2
+        scratch_shapes=[pltpu.VMEM((slots, 8), jnp.int32)]
+        + [pltpu.VMEM((slots, slots), jnp.float32)] * 2
         + [pltpu.VMEM((2, slots, slots), jnp.bfloat16)],
         compiler_params=params(),
         cost_estimate=cost(15e9, 40e6),
         name="attention_backward",
-    )(patches, grown, datt, terms, v, k, q, boxes, boxes_t)
+    )(patches, grown, datt, terms, v, k, q, boxes)
 
 
 def qkv_weights_kernel(dqkv_ref, tokens_ref, _, early_ref, sums_ref):
@@ -824,18 +880,18 @@
 
 
 def page_step(
-    tokens, boxes, boxes_t, segments, segments_t, patches, cot_out, cot_pair, weights, vectors, box_coef
+    tokens, boxes, segments, patches, cot_out, cot_pair, pieces, layout, vectors, box_coef
 ):
-    q, k, v, grown, att, inv_sum, exact = attention_forward(
-        tokens, weights, vectors, boxes, boxes_t, patches, box_coef
+    (q, k, v, grown, att, inv_sum, exact), weights = attention_forward(
+        tokens, pieces, layout, vectors, boxes, patches, box_coef
     )
     slope, late, pair_scores, sums2, dbu_tail, inv1, mixed, normed1, hidden, low, start = middle(
-        att, tokens, weights, vectors, segments, segments_t, cot_pair, cot_out, patches
+        att, tokens, weights, vectors, segments, cot_pair, cot_out, patches
     )
     early, dbu_head, sums1, dres, datt, terms = feed_backward(
         low, start, normed1, inv1, hidden, slope, att, inv_sum, exact, vectors, weights
     )
-    dqkv, dcoef = attention_backward(grown, datt, terms, q, k, v, boxes, boxes_t, patches)
+    dqkv, dcoef = attention_backward(grown, datt, terms, q, k, v, boxes, patches)
     early, bias_sums = qkv_weights(dqkv, tokens, early)
     early, late = lax.optimization_barrier((early, scatter_dp(late)))
     early = scatter_dp(early)
@@ -895,6 +951,44 @@
     ).astype(jnp.float32)
     kept = jnp.where(low, first, second)
     return jnp.concatenate([jnp.where(low, kept, other), jnp.where(low, other, kept)], axis=1)
+
+
+def gather_weights(shard, ready):
+    dp_size, grid_size = lax.axis_size("dp"), lax.axis_size("grid")
+    rows = shard.shape[0]
+    if (dp_size, grid_size) != (8, 4) or rows != 336:
+        return [lax.all_gather(shard, ("dp", "grid"), axis=0, tiled=True)], None
+    barrier = lax.optimization_barrier
+
+    def over(values, reach):
+        return lax.ppermute(values, "dp", [(i, i ^ reach) for i in range(dp_size)])
+
+    def up(values, reach):
+        return lax.ppermute(values, "grid", [(i, (i + reach) % grid_size) for i in range(grid_size)])
+
+    cuts = (0, *CUTS)
+    one, two = (shard[a:b] for a, b in zip(cuts, cuts[1:]))
+    rest = lax.all_gather(shard[cuts[-1] :], ("dp", "grid"), axis=0)
+    hops = (1, 2, 3)
+    one_grid = jnp.stack([one] + [up(one, s) for s in hops])
+    one_grid, two, *_ = barrier((one_grid, two, *ready))
+    one_x, one_y = over(one_grid, 2), over(one_grid, 4)
+    two_grid = jnp.stack([two] + [up(two, s) for s in hops])
+    one_x, one_y, two_grid = barrier((one_x, one_y, two_grid))
+    two_x, two_y = over(two_grid, 2), over(two_grid, 4)
+    two_x, two_y = barrier((two_x, two_y))
+    xy = over(jnp.concatenate([one_y[:2], two_y[:2]], axis=1), 2)
+    yx = over(jnp.concatenate([one_x[2:], two_x[2:]], axis=1), 4)
+    own = [one_grid, one_x, one_y, two_grid, two_x, two_y, xy, yx]
+    every = tuple(range(grid_size))
+    layout = [(cuts[part], [(r, s) for s in every]) for part in (0, 1) for r in (0, 2, 4)]
+    layout += [(0, [(6, s) for s in (0, 1)]), (0, [(6, s) for s in (2, 3)])]
+    layout += [(start, [(r ^ 1, s) for r, s in entries]) for start, entries in layout]
+    pieces = own + [over(piece, 1) for piece in own]
+    return pieces + [rest], layout + [(cuts[-1], None)]
+
+
+CUTS = (96, 208)
 
 
 def momentum_step(grad, param, moment, average, rate):
@@ -924,21 +1018,18 @@
     axes = ("dp", "grid")
     page_count, slot_count = tokens.shape[:2]
     device_count = lax.axis_size(axes)
-    gathered = lax.all_gather(weights.astype(jnp.bfloat16), axes, axis=0, tiled=True)
-    boxes_t = boxes.transpose(0, 2, 1)
     segments = jnp.pad(segments, ((0, 0), (0, slot_count - segments.shape[1])), constant_values=SEGS)
-    segments_t = segments.reshape(page_count, slot_count, 1)
+    pieces, layout = gather_weights(weights.astype(jnp.bfloat16), (segments,))
     pages = [
         page_step(
             tokens[p],
             boxes[p],
-            boxes_t[p],
             segments[p : p + 1],
-            segments_t[p],
             patches[p : p + 1],
             cot_out[p],
             cot_pair[p],
-            gathered,
+            pieces,
+            layout,
             vectors,
             box_coef,
         )

time: 410 us -> 386 us (0.941)
  waiting for transfers between devices: 192 us -> 153 us
  starting transfers between devices: 11.2 us -> 43.5 us
  Pallas kernels: 170 us -> 159 us
    all_gather x1, waiting for transfers between devices: 114 us -> 0.01 us  [gather_weights(): rest = lax.all_gather(shard[cuts[-1]:], ('dp', 'grid'), axis=0)]
    ppermute x0 -> x20, waiting for transfers between devices: none -> 60 us  [the longest x14 34.4 us: over(): return lax.ppermute(values, 'dp', [(i, i ^ reach) for i in range(dp_size)])]
    ppermute x0 -> x20, starting transfers between devices: none -> 28.1 us  [the longest x6 20.8 us: up(): lax.ppermute(values, 'grid', [(i, (i + reach) % grid_size) for i in range...]
    reduce_scatter x2, waiting for transfers between devices: 52.6 us -> 64 us  [scatter_dp(): lax.psum_scatter(halves.reshape(-1, D // 2), 'dp', scatter_dimension=0, t...]
    pallas_call x1, Pallas kernels: 46.7 us -> 35.5 us  [attention_forward(): pl.pallas_call(functools.partial(attention_forward_kernel, layout, len(pi...]
    ppermute x5, starting transfers between devices: 2.15 us -> 6.35 us  [exchange_sum(): lax.ppermute(values, axis, [(i, i ^ reach) for i in range(size)])]
  transfers between devices with their start and end apart: 15 -> 35, of which waited for: 8 -> 16; matrix products, arithmetic and copies ran while one was open for 4% -> 2% of each run, Pallas kernels for 20% -> 21%
where the time goes in v4:
time: 386 us; the launch traced here: 385 us
  Pallas kernels  159 us (41%)
  waiting for transfers between devices  153 us (40%)
  starting transfers between devices  43.5 us (11%)
  between operations  14.9 us (4%)
  local copies, waits for them, and re-layouts  8.3 us (2%)
  other arithmetic  7.22 us (2%)
    reduce_scatter x2, waiting for transfers between devices, scatter_dp(): lax.psum_scatter(halves.reshape(-1, D // 2), 'dp', scatter_dimension=0, t...  64 us
    pallas_call x1, Pallas kernels, middle(): pl.pallas_call(middle_kernel, grid=(PAIR_STEP + 2,), in_specs=[pl.BlockSp...  43 us
    pallas_call x1, Pallas kernels, attention_forward(): pl.pallas_call(functools.partial(attention_forward_kernel, layout, len(pi...  35.5 us
    pallas_call x1, Pallas kernels, attention_backward(): pl.pallas_call(attention_backward_kernel, grid=(HEADS // 2,), in_specs=[p...  35.4 us
    ppermute x14, waiting for transfers between devices, over(): return lax.ppermute(values, 'dp', [(i, i ^ reach) for i in range(dp_size)])  34.4 us
    pallas_call x1, Pallas kernels, feed_backward(): pl.pallas_call(feed_backward_kernel, grid=(PARTS,), in_specs=[full, full,...  27.6 us
    ppermute x6, waiting for transfers between devices, up(): lax.ppermute(values, 'grid', [(i, (i + reach) % grid_size) for i in range...  25.6 us
    ppermute x6, starting transfers between devices, up(): lax.ppermute(values, 'grid', [(i, (i + reach) % grid_size) for i in range...  20.8 us
  transfers between devices with their start and end apart: 35, of which 16 were waited for; matrix products, arithmetic and copies ran while one was open for 2% of the time, Pallas kernels for 21%

profile of v4, /device:TPU:0, one launch (start us, length us, event | category | flops | bytes accessed | tf_op | source)
XLA Modules:
  0.0 385.2 jit_solution(6171539887884828144)
XLA Ops:
  9.3 4.1 %collective-permute-start.1 = (bf16[96,768]{1,0:T(8,128)(2,1)S(1)}, bf16[96,768]{1,0:T(8,128)(2,1)S(1)}, u32[]{:S(2)}, u32[]{:S(2)}) collective-permute-start(bf16[96,768]{1,0:T(8,128)(2,1)S(1)} %get-tuple-element.115), channel_id=1, source_target_pairs={{0,2},{1,3},{2,0},{3,1},{4,6},{5,7},{6,4},{7,5},{8,10},{9,11},{10,... | collective-permute-start | bytes 442376 | tf_op jit(solution)/shard_map/ppermute | solution.py:967
  13.4 1.6 collective-permute-start
  15.0 2.2 collective-permute-start.2
  17.9 6.6 %collective-permute-done.1 = bf16[96,768]{1,0:T(8,128)(2,1)S(1)} collective-permute-done((bf16[96,768]{1,0:T(8,128)(2,1)S(1)}, bf16[96,768]{1,0:T(8,128)(2,1)S(1)}, u32[]{:S(2)}, u32[]{:S(2)}) %collective-permute-start.1) | collective-permute-done | bytes 147488 | tf_op jit(solution)/shard_map/ppermute | solution.py:967
  25.3 1.6 collective-permute-start.4
  28.4 2.0 collective-permute-start.7
  30.4 8.8 %collective-permute-start.6 = (bf16[112,768]{1,0:T(8,128)(2,1)S(1)}, bf16[112,768]{1,0:T(8,128)(2,1)S(1)}, u32[]{:S(2)}, u32[]{:S(2)}) collective-permute-start(bf16[112,768]{1,0:T(8,128)(2,1)S(1)} %slice.57), channel_id=1, source_target_pairs={{0,2},{1,3},{2,0},{3,1},{4,6},{5,7},{6,4},{7,5},{8,10},{9,11},{10,... | collective-permute-start | bytes 516104 | tf_op jit(solution)/shard_map/ppermute | solution.py:967
  39.3 2.0 collective-permute-start.5
  41.3 18.3 %collective-permute-done.6 = bf16[112,768]{1,0:T(8,128)(2,1)S(1)} collective-permute-done((bf16[112,768]{1,0:T(8,128)(2,1)S(1)}, bf16[112,768]{1,0:T(8,128)(2,1)S(1)}, u32[]{:S(2)}, u32[]{:S(2)}) %collective-permute-start.6) | collective-permute-done | bytes 172064 | tf_op jit(solution)/shard_map/ppermute | solution.py:967
  60.7 22.6 %collective-permute-done.9.refs_5_ = bf16[4,112,768]{2,1,0:T(8,128)(2,1)S(1)} collective-permute-done((bf16[4,112,768]{2,1,0:T(8,128)(2,1)S(1)}, bf16[4,112,768]{2,1,0:T(8,128)(2,1)S(1)}, u32[]{:S(2)}, u32[]{:S(2)}) %collective-permute-start.9) | collective-permute-done | bytes 688160 | tf_op jit(solution)/shard_map/ppermute | solution.py:964
  83.3 4.1 %collective-permute-done.8.refs_4_ = bf16[4,112,768]{2,1,0:T(8,128)(2,1)S(1)} collective-permute-done((bf16[4,112,768]{2,1,0:T(8,128)(2,1)S(1)}, bf16[4,112,768]{2,1,0:T(8,128)(2,1)S(1)}, u32[]{:S(2)}, u32[]{:S(2)}) %collective-permute-start.8) | collective-permute-done | bytes 688160 | tf_op jit(solution)/shard_map/ppermute | solution.py:964
  87.7 2.5 collective-permute-start.11
  91.0 7.1 %collective-permute-done.10.refs_6_ = bf16[2,208,768]{2,1,0:T(8,128)(2,1)S(1)} collective-permute-done((bf16[2,208,768]{2,1,0:T(8,128)(2,1)S(1)}, bf16[2,208,768]{2,1,0:T(8,128)(2,1)S(1)}, u32[]{:S(2)}, u32[]{:S(2)}) %collective-permute-start.10) | collective-permute-done | bytes 639008 | tf_op jit(solution)/shard_map/ppermute | solution.py:964
  101.2 35.5 %attention_forward.1 = (bf16[1024,768]{1,0:T(8,128)(2,1)}, bf16[1024,768]{1,0:T(8,128)(2,1)}, bf16[1024,768]{1,0:T(8,128)(2,1)}, bf16[12,1024,1024]{2,1,0:T(8,12...) custom-call(f32[2,12]{1,0:T(2,128)} %coef_ref.1, ...), custom_call_target="tpu_custom_call" | custom-call | flops 10000000000 | bytes 40000000 | tf_op jit(solution)/shard_map/attention_forward/pallas_call | solution.py:253
  136.8 43.0 %middle.1 = (bf16[1024,3072]{1,0:T(8,128)(2,1)}, bf16[2,5376,384]{2,1,0:T(8,128)(2,1)}, f32[64,64]{1,0:T(8,128)}, f32[8,768]{1,0:T(8,128)}, f32[1,768]{1,0:T(1,1...) custom-call(s32[1]{0:T(128)S(6)} %copy.34.patches_ref, ...), custom_call_target="tpu_custom_call" | custom-call | flops 20000000000 | bytes 40000000 | tf_op jit(solution)/shard_map/middle/pallas_call | solution.py:507
  179.8 27.6 %feed_backward.1 = (bf16[2,5376,384]{2,1,0:T(8,128)(2,1)}, f32[1,2304]{1,0:T(1,128)}, f32[8,768]{1,0:T(8,128)}, f32[1024,768]{1,0:T(8,128)}, bf16[1024,768]{1,0:T(8,128)(2,1)}, /*index=5*/bf16[1024,768]{1,0:T(8,128)(2,1)}) custom-call(bf16[1024,768]{1,0:T(8,128)(2,1)} %get-tuple-element.66.low_ref, bf16[1024,768]{1,0:T(8,128)(2,1)} %get-tuple-element.67.hidden_ref, ...), custom_call_target="tpu_custom_call" | custom-call | flops 16999999488 | bytes 40000000 | tf_op jit(solution)/shard_map/feed_backward/pallas_call | solution.py:696
  207.4 35.4 %attention_backward.1 = (bf16[3,768,1024]{2,1,0:T(8,128)(2,1)}, f32[12,2,1024]{2,1,0:T(2,128)}) custom-call(s32[1]{0:T(128)S(6)} %copy.34.patches_ref, bf16[12,1024,1024]{2,1,0:T(8,128)(2,1)} %get-tuple-element.65.grown_ref, bf16[1024,768]{1,0:T(8,128)(2,1)} %get-tuple-element.74.datt_ref, bf16[1024,768]{1,0:T(8,128)(2,1)} %get-tuple-element.75.terms_ref, ...), custom_call_target="tpu_custom_call" | custom-call | flops 15000000512 | bytes 40000000 | tf_op jit(solution)/shard_map/attention_backward/pallas_call | solution.py:802
  242.8 8.6 %qkv_weights.1 = (bf16[2,5376,384]{2,1,0:T(8,128)(2,1)}, f32[3,8,768]{2,1,0:T(8,128)}) custom-call(bf16[3,768,1024]{2,1,0:T(8,128)(2,1)} %get-tuple-element.79.dqkv_ref, bf16[1024,768]{1,0:T(8,128)(2,1)} %bitcast.50, bf16[2,5376,384]{2,1,0:T(8,128)(2,1)} %get-tuple-element.81._), custom_call_target="tpu_custom_call", output_to_operand_aliasing={{0}: (2, {})} | custom-call | flops 3600000000 | bytes 10000000 | tf_op jit(solution)/shard_map/qkv_weights/pallas_call | solution.py:836
  251.5 11.3 %reduce-scatter.3.cloned.1.call-done = bf16[1344,384]{1,0:T(8,128)(2,1)} async-done(((bf16[10752,384]{1,0:T(8,128)(2,1)}), bf16[1344,384]{1,0:T(8,128)(2,1)}) %reduce-scatter.3.cloned.1.call-update) | async-done | bytes 1032208 | tf_op jit(solution)/shard_map/reduce_scatter | solution.py:926
  266.8 2.8 collective-permute-start.28
  269.9 2.1 collective-permute-done.28
  271.9 2.4 collective-permute-start.29
  274.3 2.1 collective-permute-done.29
  276.7 4.3 %collective-permute-done.30 = f32[16,768]{1,0:T(8,128)S(1)} collective-permute-done((f32[16,768]{1,0:T(8,128)S(1)}, f32[16,768]{1,0:T(8,128)S(1)}, u32[]{:S(2)}, u32[]{:S(2)}) %collective-permute-start.30) | collective-permute-done | bytes 49184 | tf_op jit(solution)/shard_map/ppermute | solution.py:920
  284.7 52.8 %reduce-scatter.5.cloned.1.call-done = bf16[1344,384]{1,0:T(8,128)(2,1)} async-done(((bf16[10752,384]{1,0:T(8,128)(2,1)}), bf16[1344,384]{1,0:T(8,128)(2,1)}) %reduce-scatter.5.cloned.1.call-update) | async-done | bytes 1032208 | tf_op jit(solution)/shard_map/reduce_scatter | solution.py:926
  337.5 2.1 dynamic-slice_bitcast_fusion.5
  341.0 2.4 collective-permute-start.22
  344.0 8.6 %token_gradient.1 = bf16[1024,768]{1,0:T(8,128)(2,1)} custom-call(bf16[3,768,1024]{2,1,0:T(8,128)(2,1)} %get-tuple-element.79.dqkv_ref, bf16[10752,768]{1,0:T(8,128)(2,1)} %get-tuple-element.62.wo_ref.wu_ref.wd_ref.wl_ref.wr_ref.weight_ref, f32[1024,768]{1,0:T(8,128)} %get-tuple-element.80.dres_ref), custom_call_target="tpu_custom_call" | custom-call | flops 3600000000 | bytes 12000000 | tf_op jit(solution)/shard_map/token_gradient/pallas_call | solution.py:866
  352.7 1.7 collective-permute-done.22
  354.4 11.6 %collective-permute-done.21 = bf16[336,384]{1,0:T(8,128)(2,1)S(1)} collective-permute-done((bf16[336,384]{1,0:T(8,128)(2,1)S(1)}, bf16[336,384]{1,0:T(8,128)(2,1)S(1)}, u32[]{:S(2)}, u32[]{:S(2)}) %collective-permute-start.21) | collective-permute-done | bytes 258080 | tf_op jit(solution)/shard_map/ppermute | solution.py:940
  370.0 5.5 %collective-permute-done.26 = bf16[336,384]{1,0:T(8,128)(2,1)S(1)} collective-permute-done((bf16[336,384]{1,0:T(8,128)(2,1)S(1)}, bf16[336,384]{1,0:T(8,128)(2,1)S(1)}, u32[]{:S(2)}, u32[]{:S(2)}) %collective-permute-start.26) | collective-permute-done | bytes 258080 | tf_op jit(solution)/shard_map/ppermute | solution.py:949
  375.7 1.7 fusion.4
  (150 shorter events, 25.3 us)
Async XLA Ops:
  7.2 94.0 %all-gather.3.cloned.1.call-start = ((), (), s32[]{:S(2)}) async-start(), calls=%async_computation.4 | async-start | bytes 6488064 | tf_op jit(solution)/shard_map/all_gather | solution.py:971
  9.2 253.5 %reduce-scatter.3.cloned.1.call-start = ((), (), s32[]{:S(2)}) async-start(), calls=%async_computation.2 | async-start | bytes 9289728 | tf_op jit(solution)/shard_map/reduce_scatter | solution.py:926
  9.3 15.1 %collective-permute-start.1 = (bf16[96,768]{1,0:T(8,128)(2,1)S(1)}, bf16[96,768]{1,0:T(8,128)(2,1)S(1)}, u32[]{:S(2)}, u32[]{:S(2)}) collective-permute-start(bf16[96,768]{1,0:T(8,128)(2,1)S(1)} %get-tuple-element.115), channel_id=1, source_target_pairs={{0,2},{1,3},{2,0},{3,1},{4,6},{5,7},{6,4},{7,5},{8,10},{9,11},{10,... | collective-permute-start | bytes 442376 | tf_op jit(solution)/shard_map/ppermute | solution.py:967
  13.4 11.0 %collective-permute-start = (bf16[96,768]{1,0:T(8,128)(2,1)S(1)}, bf16[96,768]{1,0:T(8,128)(2,1)S(1)}, u32[]{:S(2)}, u32[]{:S(2)}) collective-permute-start(bf16[96,768]{1,0:T(8,128)(2,1)S(1)} %get-tuple-element.115), channel_id=1, source_target_pairs={{0,1},{1,2},{2,3},{3,0},{4,5},{5,6},{6,7},{7,4},{8,9},{9,10},{10,1... | collective-permute-start | bytes 442376 | tf_op jit(solution)/shard_map/ppermute | solution.py:967
  15.0 10.2 %collective-permute-start.2 = (bf16[96,768]{1,0:T(8,128)(2,1)S(1)}, bf16[96,768]{1,0:T(8,128)(2,1)S(1)}, u32[]{:S(2)}, u32[]{:S(2)}) collective-permute-start(bf16[96,768]{1,0:T(8,128)(2,1)S(1)} %get-tuple-element.115), channel_id=1, source_target_pairs={{0,3},{1,0},{2,1},{3,2},{4,7},{5,4},{6,5},{7,6},{8,11},{9,8},{10,9... | collective-permute-start | bytes 442376 | tf_op jit(solution)/shard_map/ppermute | solution.py:967
  25.3 34.5 %collective-permute-start.4 = (bf16[4,96,768]{2,1,0:T(8,128)(2,1)S(1)}, bf16[4,96,768]{2,1,0:T(8,128)(2,1)S(1)}, u32[]{:S(2)}, u32[]{:S(2)}) collective-permute-start(bf16[4,96,768]{2,1,0:T(8,128)(2,1)S(1)} %pad_maximum_fusion.4.refs_0_), channel_id=1, source_target_pairs={{0,16},{4,20},{8,24},{12,28},{16,0},{20,4},{24,8},{28,12},{1,17},{... | collective-permute-start | bytes 1769480 | tf_op jit(solution)/shard_map/ppermute | solution.py:964
  26.9 32.9 %collective-permute-start.3 = (bf16[4,96,768]{2,1,0:T(8,128)(2,1)S(1)}, bf16[4,96,768]{2,1,0:T(8,128)(2,1)S(1)}, u32[]{:S(2)}, u32[]{:S(2)}) collective-permute-start(bf16[4,96,768]{2,1,0:T(8,128)(2,1)S(1)} %pad_maximum_fusion.4.refs_0_), channel_id=1, source_target_pairs={{0,8},{4,12},{8,0},{12,4},{16,24},{20,28},{24,16},{28,20},{1,9},{5... | collective-permute-start | bytes 1769480 | tf_op jit(solution)/shard_map/ppermute | solution.py:964
  28.4 12.9 %collective-permute-start.7 = (bf16[112,768]{1,0:T(8,128)(2,1)S(1)}, bf16[112,768]{1,0:T(8,128)(2,1)S(1)}, u32[]{:S(2)}, u32[]{:S(2)}) collective-permute-start(bf16[112,768]{1,0:T(8,128)(2,1)S(1)} %slice.57), channel_id=1, source_target_pairs={{0,3},{1,0},{2,1},{3,2},{4,7},{5,4},{6,5},{7,6},{8,11},{9,8},{10,9... | collective-permute-start | bytes 516104 | tf_op jit(solution)/shard_map/ppermute | solution.py:967
  30.4 29.2 %collective-permute-start.6 = (bf16[112,768]{1,0:T(8,128)(2,1)S(1)}, bf16[112,768]{1,0:T(8,128)(2,1)S(1)}, u32[]{:S(2)}, u32[]{:S(2)}) collective-permute-start(bf16[112,768]{1,0:T(8,128)(2,1)S(1)} %slice.57), channel_id=1, source_target_pairs={{0,2},{1,3},{2,0},{3,1},{4,6},{5,7},{6,4},{7,5},{8,10},{9,11},{10,... | collective-permute-start | bytes 516104 | tf_op jit(solution)/shard_map/ppermute | solution.py:967
  39.3 20.4 %collective-permute-start.5 = (bf16[112,768]{1,0:T(8,128)(2,1)S(1)}, bf16[112,768]{1,0:T(8,128)(2,1)S(1)}, u32[]{:S(2)}, u32[]{:S(2)}) collective-permute-start(bf16[112,768]{1,0:T(8,128)(2,1)S(1)} %slice.57), channel_id=1, source_target_pairs={{0,1},{1,2},{2,3},{3,0},{4,5},{5,6},{6,7},{7,4},{8,9},{9,10},{10,1... | collective-permute-start | bytes 516104 | tf_op jit(solution)/shard_map/ppermute | solution.py:967
  59.8 23.6 %collective-permute-start.9 = (bf16[4,112,768]{2,1,0:T(8,128)(2,1)S(1)}, bf16[4,112,768]{2,1,0:T(8,128)(2,1)S(1)}, u32[]{:S(2)}, u32[]{:S(2)}) collective-permute-start(bf16[4,112,768]{2,1,0:T(8,128)(2,1)S(1)} %pad_maximum_fusion.1.refs_3_), channel_id=1, source_target_pairs={{0,16},{4,20},{8,24},{12,28},{16,0},{20,4},{24,8},{28,12},{1,17},{... | collective-permute-start | bytes 2064392 | tf_op jit(solution)/shard_map/ppermute | solution.py:964
  59.9 27.6 %collective-permute-start.8 = (bf16[4,112,768]{2,1,0:T(8,128)(2,1)S(1)}, bf16[4,112,768]{2,1,0:T(8,128)(2,1)S(1)}, u32[]{:S(2)}, u32[]{:S(2)}) collective-permute-start(bf16[4,112,768]{2,1,0:T(8,128)(2,1)S(1)} %pad_maximum_fusion.1.refs_3_), channel_id=1, source_target_pairs={{0,8},{4,12},{8,0},{12,4},{16,24},{20,28},{24,16},{28,20},{1,9},{5... | collective-permute-start | bytes 2064392 | tf_op jit(solution)/shard_map/ppermute | solution.py:964
  59.9 30.3 %collective-permute-start.12 = (bf16[4,96,768]{2,1,0:T(8,128)(2,1)S(1)}, bf16[4,96,768]{2,1,0:T(8,128)(2,1)S(1)}, u32[]{:S(2)}, u32[]{:S(2)}) collective-permute-start(bf16[4,96,768]{2,1,0:T(8,128)(2,1)S(1)} %pad_maximum_fusion.4.refs_0_), channel_id=1, source_target_pairs={{0,4},{4,0},{8,12},{12,8},{16,20},{20,16},{24,28},{28,24},{1,5},{5... | collective-permute-start | bytes 1769480 | tf_op jit(solution)/shard_map/ppermute | solution.py:964
  60.0 30.2 %collective-permute-start.13 = (bf16[4,96,768]{2,1,0:T(8,128)(2,1)S(1)}, bf16[4,96,768]{2,1,0:T(8,128)(2,1)S(1)}, u32[]{:S(2)}, u32[]{:S(2)}) collective-permute-start(bf16[4,96,768]{2,1,0:T(8,128)(2,1)S(1)} %collective-permute-done.3.refs_1_), channel_id=1, source_target_pairs={{0,4},{4,0},{8,12},{12,8},{16,20},{20,16},{24,28},{28,24},{1,5},{5... | collective-permute-start | bytes 1769480 | tf_op jit(solution)/shard_map/ppermute | solution.py:964
  60.6 30.2 %collective-permute-start.14 = (bf16[4,96,768]{2,1,0:T(8,128)(2,1)S(1)}, bf16[4,96,768]{2,1,0:T(8,128)(2,1)S(1)}, u32[]{:S(2)}, u32[]{:S(2)}) collective-permute-start(bf16[4,96,768]{2,1,0:T(8,128)(2,1)S(1)} %collective-permute-done.4.refs_2_), channel_id=1, source_target_pairs={{0,4},{4,0},{8,12},{12,8},{16,20},{20,16},{24,28},{28,24},{1,5},{5... | collective-permute-start | bytes 1769480 | tf_op jit(solution)/shard_map/ppermute | solution.py:964
  87.6 10.5 %collective-permute-start.10 = (bf16[2,208,768]{2,1,0:T(8,128)(2,1)S(1)}, bf16[2,208,768]{2,1,0:T(8,128)(2,1)S(1)}, u32[]{:S(2)}, u32[]{:S(2)}) collective-permute-start(bf16[2,208,768]{2,1,0:T(8,128)(2,1)S(1)} %pad_maximum_fusion.2), channel_id=1, source_target_pairs={{0,8},{4,12},{8,0},{12,4},{16,24},{20,28},{24,16},{28,20},{1,9},{5... | collective-permute-start | bytes 1916936 | tf_op jit(solution)/shard_map/ppermute | solution.py:964
  87.7 10.9 %collective-permute-start.11 = (bf16[2,208,768]{2,1,0:T(8,128)(2,1)S(1)}, bf16[2,208,768]{2,1,0:T(8,128)(2,1)S(1)}, u32[]{:S(2)}, u32[]{:S(2)}) collective-permute-start(bf16[2,208,768]{2,1,0:T(8,128)(2,1)S(1)} %pad_maximum_fusion.3), channel_id=1, source_target_pairs={{0,16},{4,20},{8,24},{12,28},{16,0},{20,4},{24,8},{28,12},{1,17},{... | collective-permute-start | bytes 1916936 | tf_op jit(solution)/shard_map/ppermute | solution.py:964
  90.2 9.0 %collective-permute-start.15 = (bf16[4,112,768]{2,1,0:T(8,128)(2,1)S(1)}, bf16[4,112,768]{2,1,0:T(8,128)(2,1)S(1)}, u32[]{:S(2)}, u32[]{:S(2)}) collective-permute-start(bf16[4,112,768]{2,1,0:T(8,128)(2,1)S(1)} %pad_maximum_fusion.1.refs_3_), channel_id=1, source_target_pairs={{0,4},{4,0},{8,12},{12,8},{16,20},{20,16},{24,28},{28,24},{1,5},{5... | collective-permute-start | bytes 2064392 | tf_op jit(solution)/shard_map/ppermute | solution.py:964
  90.3 9.0 %collective-permute-start.16 = (bf16[4,112,768]{2,1,0:T(8,128)(2,1)S(1)}, bf16[4,112,768]{2,1,0:T(8,128)(2,1)S(1)}, u32[]{:S(2)}, u32[]{:S(2)}) collective-permute-start(bf16[4,112,768]{2,1,0:T(8,128)(2,1)S(1)} %collective-permute-done.8.refs_4_), channel_id=1, source_target_pairs={{0,4},{4,0},{8,12},{12,8},{16,20},{20,16},{24,28},{28,24},{1,5},{5... | collective-permute-start | bytes 2064392 | tf_op jit(solution)/shard_map/ppermute | solution.py:964
  90.9 8.4 %collective-permute-start.17 = (bf16[4,112,768]{2,1,0:T(8,128)(2,1)S(1)}, bf16[4,112,768]{2,1,0:T(8,128)(2,1)S(1)}, u32[]{:S(2)}, u32[]{:S(2)}) collective-permute-start(bf16[4,112,768]{2,1,0:T(8,128)(2,1)S(1)} %collective-permute-done.9.refs_5_), channel_id=1, source_target_pairs={{0,4},{4,0},{8,12},{12,8},{16,20},{20,16},{24,28},{28,24},{1,5},{5... | collective-permute-start | bytes 2064392 | tf_op jit(solution)/shard_map/ppermute | solution.py:964
  179.8 157.7 %reduce-scatter.5.cloned.1.call-start = ((), (), s32[]{:S(2)}) async-start(), calls=%async_computation.3 | async-start | bytes 9289728 | tf_op jit(solution)/shard_map/reduce_scatter | solution.py:926
  266.8 5.1 %collective-permute-start.28 = (f32[16,768]{1,0:T(8,128)S(1)}, f32[16,768]{1,0:T(8,128)S(1)}, u32[]{:S(2)}, u32[]{:S(2)}) collective-permute-start(f32[16,768]{1,0:T(8,128)S(1)} %add.137), channel_id=1, source_target_pairs={{0,8},{4,12},{8,0},{12,4},{16,24},{20,28},{24,16},{28,20},{1,9},{5... | collective-permute-start | bytes 147464 | tf_op jit(solution)/shard_map/ppermute | solution.py:920
  269.7 73.6 %collective-permute-start.23 = (bf16[336,384]{1,0:T(8,128)(2,1)S(1)}, bf16[336,384]{1,0:T(8,128)(2,1)S(1)}, u32[]{:S(2)}, u32[]{:S(2)}) collective-permute-start(bf16[336,384]{1,0:T(8,128)(2,1)S(1)} %get-tuple-element.108), channel_id=1, source_target_pairs={{0,1},{1,2},{2,3},{3,0},{4,5},{5,6},{6,7},{7,4},{8,9},{9,10},{10,1... | collective-permute-start | bytes 774152 | tf_op jit(solution)/shard_map/ppermute | solution.py:940
  271.9 4.5 %collective-permute-start.29 = (f32[16,768]{1,0:T(8,128)S(1)}, f32[16,768]{1,0:T(8,128)S(1)}, u32[]{:S(2)}, u32[]{:S(2)}) collective-permute-start(f32[16,768]{1,0:T(8,128)S(1)} %add.138), channel_id=1, source_target_pairs={{0,16},{4,20},{8,24},{12,28},{16,0},{20,4},{24,8},{28,12},{1,17},{... | collective-permute-start | bytes 147464 | tf_op jit(solution)/shard_map/ppermute | solution.py:920
  276.4 4.5 %collective-permute-start.30 = (f32[16,768]{1,0:T(8,128)S(1)}, f32[16,768]{1,0:T(8,128)S(1)}, u32[]{:S(2)}, u32[]{:S(2)}) collective-permute-start(f32[16,768]{1,0:T(8,128)S(1)} %add.139), channel_id=1, source_target_pairs={{0,1},{1,0},{2,3},{3,2},{4,5},{5,4},{6,7},{7,6},{8,9},{9,8},{10,11... | collective-permute-start | bytes 147464 | tf_op jit(solution)/shard_map/ppermute | solution.py:920
  280.9 60.1 %collective-permute-start.31 = (f32[16,768]{1,0:T(8,128)S(1)}, f32[16,768]{1,0:T(8,128)S(1)}, u32[]{:S(2)}, u32[]{:S(2)}) collective-permute-start(f32[16,768]{1,0:T(8,128)S(1)} %add.140), channel_id=1, source_target_pairs={{0,2},{1,3},{2,0},{3,1},{4,6},{5,7},{6,4},{7,5},{8,10},{9,11},{10,... | collective-permute-start | bytes 147464 | tf_op jit(solution)/shard_map/ppermute | solution.py:920
  281.8 70.9 %collective-permute-start.25 = (bf16[336,384]{1,0:T(8,128)(2,1)S(1)}, bf16[336,384]{1,0:T(8,128)(2,1)S(1)}, u32[]{:S(2)}, u32[]{:S(2)}) collective-permute-start(bf16[336,384]{1,0:T(8,128)(2,1)S(1)} %get-tuple-element.109), channel_id=1, source_target_pairs={{0,3},{1,0},{2,1},{3,2},{4,7},{5,4},{6,5},{7,6},{8,11},{9,8},{10,9... | collective-permute-start | bytes 774152 | tf_op jit(solution)/shard_map/ppermute | solution.py:940
  283.2 69.5 %collective-permute-start.24 = (bf16[336,384]{1,0:T(8,128)(2,1)S(1)}, bf16[336,384]{1,0:T(8,128)(2,1)S(1)}, u32[]{:S(2)}, u32[]{:S(2)}) collective-permute-start(bf16[336,384]{1,0:T(8,128)(2,1)S(1)} %get-tuple-element.110), channel_id=1, source_target_pairs={{0,2},{1,3},{2,0},{3,1},{4,6},{5,7},{6,4},{7,5},{8,10},{9,11},{10,... | collective-permute-start | bytes 774152 | tf_op jit(solution)/shard_map/ppermute | solution.py:940
  339.5 13.2 %collective-permute-start.20 = (bf16[336,384]{1,0:T(8,128)(2,1)}, bf16[336,384]{1,0:T(8,128)(2,1)S(1)}, u32[]{:S(2)}, u32[]{:S(2)}) collective-permute-start(bf16[336,384]{1,0:T(8,128)(2,1)} %get-tuple-element.111), channel_id=1, source_target_pairs={{0,1},{1,2},{2,3},{3,0},{4,5},{5,6},{6,7},{7,4},{8,9},{9,10},{10,1... | collective-permute-start | bytes 774152 | tf_op jit(solution)/shard_map/ppermute | solution.py:940
  341.0 13.4 %collective-permute-start.22 = (bf16[336,384]{1,0:T(8,128)(2,1)}, bf16[336,384]{1,0:T(8,128)(2,1)S(1)}, u32[]{:S(2)}, u32[]{:S(2)}) collective-permute-start(bf16[336,384]{1,0:T(8,128)(2,1)} %get-tuple-element.112), channel_id=1, source_target_pairs={{0,3},{1,0},{2,1},{3,2},{4,7},{5,4},{6,5},{7,6},{8,11},{9,8},{10,9... | collective-permute-start | bytes 774152 | tf_op jit(solution)/shard_map/ppermute | solution.py:940
  343.4 22.7 %collective-permute-start.21 = (bf16[336,384]{1,0:T(8,128)(2,1)S(1)}, bf16[336,384]{1,0:T(8,128)(2,1)S(1)}, u32[]{:S(2)}, u32[]{:S(2)}) collective-permute-start(bf16[336,384]{1,0:T(8,128)(2,1)S(1)} %get-tuple-element.113), channel_id=1, source_target_pairs={{0,2},{1,3},{2,0},{3,1},{4,6},{5,7},{6,4},{7,5},{8,10},{9,11},{10,... | collective-permute-start | bytes 774152 | tf_op jit(solution)/shard_map/ppermute | solution.py:940
  367.3 8.2 %collective-permute-start.26 = (bf16[336,384]{1,0:T(8,128)(2,1)S(1)}, bf16[336,384]{1,0:T(8,128)(2,1)S(1)}, u32[]{:S(2)}, u32[]{:S(2)}) collective-permute-start(bf16[336,384]{1,0:T(8,128)(2,1)S(1)} %get-tuple-element.103), channel_id=1, source_target_pairs={{0,16},{4,20},{8,24},{12,28},{16,0},{20,4},{24,8},{28,12},{1,17},{... | collective-permute-start | bytes 774152 | tf_op jit(solution)/shard_map/ppermute | solution.py:949
  (35 other events, 360.2 us)
Sparse Core Ops, SparseCore 0:
  11.5 87.9 all-gather.2
  179.9 82.7 reduce-scatter.2
  266.8 70.6 reduce-scatter.4
